TPU v7x, 32 devices: a whole 2x2x4 slice. The times are simulated.
32 devices in a mesh: dp: 4 (over y, x), fsdp: 8 (over z, core).
Axes of the slice: x: 2, y: 2, z: 4, core: 2. Of those that a mesh axis runs over, the one named last changes fastest.
Arguments:
- images: bfloat16 [64, 2304, 320], P(('dp', 'fsdp')), may hold values from -6 to 6
- cotangent: bfloat16 [64, 2304, 320], P(('dp', 'fsdp')), may hold values from -6 to 6
- kv_sides: int32 [64], P(('dp', 'fsdp')), may hold values from 14 to 24, as said below
- params: float32 [1658880], P(('dp', 'fsdp')), may hold values from -2 to 2
- first_moment: float32 [1658880], P(('dp', 'fsdp')), may hold values from -1 to 1
- second_moment: float32 [1658880], P(('dp', 'fsdp')), may hold values from 0 to 1, as said below
Outputs:
- output: bfloat16 [64, 2304, 320], P(('dp', 'fsdp'))
- grad_images: float32 [64, 2304, 320], P(('dp', 'fsdp'))
- grad_norm: float32 [], replicated
- new_first: float32 [1658880], P(('dp', 'fsdp'))
- new_second: float32 [1658880], P(('dp', 'fsdp'))
- new_params: float32 [1658880], P(('dp', 'fsdp'))
Inputs may be any that keep to these rules, and one draw needn't show every extreme that they name: `kv_sides`: each entry is 14, 20 or 24: token grids of 28, 40 or 48 per side at real sizes, the segment-3 grids of 448, 640 or 768 pixel images; some image has 24. `second_moment`: positive.
All inputs are finite; a program needn't handle non-finite values.
Results may differ from a plain program's by a relative error of at most 0.0089.
Values may be sent and summed in bfloat16 or wider, within the bound.
A program may use at most 256 MiB of HBM per device.

v0:
```python
from functools import partial
import math

import jax
import jax.numpy as jnp
from jax import lax
from jax.sharding import PartitionSpec as P

HEADS = 5
HEAD_DIM = 64
GRID = 48
KV = 24
STEP = 10


CLIP_NORM = 1.0
BETA_FIRST = 0.9
BETA_SECOND = 0.999
RATE = 0.04
DECAY = 0.05
EPSILON = 1e-08


def layout_shapes(model_width, hidden_width):
    return [
        (model_width,),
        (model_width,),
        (model_width, model_width),
        (model_width,),
        (4 * model_width, model_width),
        (model_width,),
        (model_width,),
        (model_width,),
        (model_width, 2 * model_width),
        (model_width,),
        (model_width, model_width),
        (model_width,),
        (model_width,),
        (model_width,),
        (model_width, hidden_width),
        (hidden_width,),
        (9, hidden_width),
        (hidden_width,),
        (hidden_width, model_width),
        (model_width,),
    ]


def unpack_params(flat, model_width, hidden_width):
    pieces = []
    offset = 0
    for shape in layout_shapes(model_width, hidden_width):
        count = math.prod(shape)
        pieces.append(flat[offset : offset + count].reshape(shape))
        offset += count
    return pieces


def build_masks(kv_sides):
    positions = jnp.arange(GRID * GRID, dtype=jnp.int32)
    limit = 2 * kv_sides[:, None]
    row_mask = ((positions[None] // GRID < limit) & (positions[None] % GRID < limit)).astype(
        jnp.float32
    )
    cells = jnp.arange(KV * KV, dtype=jnp.int32)
    key_mask = (cells[None] // KV < kv_sides[:, None]) & (cells[None] % KV < kv_sides[:, None])
    return (row_mask[:, :, None], key_mask)


def norm_forward(values, gain, shift):
    centred = values - jnp.mean(values, axis=-1, keepdims=True)
    variance = jnp.mean(centred * centred, axis=-1, keepdims=True)
    rstd = lax.rsqrt(variance + 1e-06)
    normed = centred * rstd
    return (normed * gain + shift, normed, rstd)


def norm_backward(grad_out, normed, rstd, gain):
    scaled = grad_out * gain
    grad_gain = jnp.sum(grad_out * normed, axis=(0, 1))
    grad_shift = jnp.sum(grad_out, axis=(0, 1))
    mean_plain = jnp.mean(scaled, axis=-1, keepdims=True)
    mean_mixed = jnp.mean(scaled * normed, axis=-1, keepdims=True)
    return (rstd * (scaled - mean_plain - normed * mean_mixed), grad_gain, grad_shift)


def project(left, right):
    return jnp.dot(left, right, preferred_element_type=jnp.float32)


def project_back(grad, weight):
    return jnp.einsum("...e,de->...d", grad, weight, preferred_element_type=jnp.float32)


def outer_sum(left, right):
    return jnp.einsum("...d,...e->de", left, right, preferred_element_type=jnp.float32)


def column_sum(grad):
    return jnp.sum(grad.astype(jnp.float32), axis=(0, 1))


def depthwise(filled, taps, bias):
    count_images = filled.shape[0]
    hidden_width = filled.shape[2]
    grid = filled.astype(jnp.float32).reshape(count_images, GRID, GRID, hidden_width)
    padded = jnp.pad(grid, ((0, 0), (1, 1), (1, 1), (0, 0)))
    result = jnp.zeros_like(grid) + bias
    for index in range(9):
        row_step = index // 3
        col_step = index % 3
        result = (
            result + taps[index] * padded[:, row_step : row_step + GRID, col_step : col_step + GRID]
        )
    return result.reshape(count_images, GRID * GRID, hidden_width)


def depthwise_back(grad_conv, filled, taps):
    count_images = filled.shape[0]
    hidden_width = filled.shape[2]
    grid = filled.astype(jnp.float32).reshape(count_images, GRID, GRID, hidden_width)
    padded = jnp.pad(grid, ((0, 0), (1, 1), (1, 1), (0, 0)))
    grad_grid = grad_conv.reshape(count_images, GRID, GRID, hidden_width)
    grad_padded = jnp.pad(grad_grid, ((0, 0), (1, 1), (1, 1), (0, 0)))
    tap_grads = []
    grad_filled = jnp.zeros_like(grid)
    for index in range(9):
        row_step = index // 3
        col_step = index % 3
        window = padded[:, row_step : row_step + GRID, col_step : col_step + GRID]
        tap_grads.append(jnp.sum(window * grad_grid, axis=(0, 1, 2)))
        grad_filled = (
            grad_filled
            + taps[index]
            * grad_padded[:, 2 - row_step : 2 - row_step + GRID, 2 - col_step : 2 - col_step + GRID]
        )
    return (jnp.stack(tap_grads), grad_filled.reshape(count_images, GRID * GRID, hidden_width))


def head_scores(queries, keys, key_mask):
    query_heads = queries.reshape(queries.shape[0], HEADS, HEAD_DIM)
    key_heads = keys.reshape(keys.shape[0], HEADS, HEAD_DIM)
    scores = jnp.einsum(
        "shd,khd->hsk", query_heads, key_heads, preferred_element_type=jnp.float32
    ) * HEAD_DIM ** (-0.5)
    return (jnp.where(key_mask[None, None, :], scores, -1e30), query_heads, key_heads)


def attend_forward(packed):
    queries, keys, values, key_mask = packed
    scores, query_heads, key_heads = head_scores(queries, keys, key_mask)
    top = jnp.max(scores, axis=-1, keepdims=True)
    log_total = top + jnp.log(jnp.sum(jnp.exp(scores - top), axis=-1, keepdims=True))
    attend = jnp.exp(scores - log_total).astype(jnp.bfloat16)
    value_heads = values.reshape(values.shape[0], HEADS, HEAD_DIM)
    mixed = jnp.einsum("hsk,khd->shd", attend, value_heads, preferred_element_type=jnp.float32)
    return (mixed.reshape(queries.shape[0], -1).astype(jnp.bfloat16), log_total)


def attend_backward(packed):
    queries, keys, values, key_mask, log_total, grad_mixed = packed
    scores, query_heads, key_heads = head_scores(queries, keys, key_mask)
    attend = jnp.exp(scores - log_total)
    value_heads = values.reshape(values.shape[0], HEADS, HEAD_DIM)
    grad_heads = grad_mixed.reshape(grad_mixed.shape[0], HEADS, HEAD_DIM)
    grad_values = jnp.einsum(
        "hsk,shd->khd", attend.astype(jnp.bfloat16), grad_heads, preferred_element_type=jnp.float32
    )
    grad_attend = jnp.einsum(
        "shd,khd->hsk", grad_heads, value_heads, preferred_element_type=jnp.float32
    )
    grad_scores = attend * (grad_attend - jnp.sum(attend * grad_attend, axis=-1, keepdims=True))
    grad_scores = grad_scores.astype(jnp.bfloat16)
    scale = HEAD_DIM ** (-0.5)
    grad_queries = (
        jnp.einsum("hsk,khd->shd", grad_scores, key_heads, preferred_element_type=jnp.float32)
        * scale
    )
    grad_keys = (
        jnp.einsum("hsk,shd->khd", grad_scores, query_heads, preferred_element_type=jnp.float32)
        * scale
    )
    return (
        grad_queries.reshape(queries.shape[0], -1).astype(jnp.bfloat16),
        grad_keys.reshape(keys.shape[0], -1).astype(jnp.bfloat16),
        grad_values.reshape(values.shape[0], -1).astype(jnp.bfloat16),
    )


def local(images, cotangent, kv_sides, params, first_moment, second_moment):
    count_images = images.shape[0]
    model_width = images.shape[2]
    hidden_width = 4 * model_width
    tokens_image = GRID * GRID
    row_mask, key_mask = build_masks(kv_sides)
    low_params = params.astype(jnp.bfloat16)
    pieces = unpack_params(
        lax.all_gather(low_params, ("dp", "fsdp"), axis=0, tiled=True), model_width, hidden_width
    )
    (
        pre_gain,
        pre_shift,
        query_weight,
        query_bias,
        reduce_weight,
        reduce_bias,
        reduce_gain,
        reduce_shift,
        pair_weight,
        value_bias,
        output_weight,
        output_bias,
        mlp_gain,
        mlp_shift,
        expand_weight,
        expand_bias,
        spatial_weight,
        spatial_bias,
        shrink_weight,
        shrink_bias,
    ) = pieces

    def to_float(vector):
        return vector.astype(jnp.float32)

    inputs = images.astype(jnp.float32) * row_mask
    pre_out, pre_normed, pre_rstd = norm_forward(inputs, to_float(pre_gain), to_float(pre_shift))
    pre_low = pre_out.astype(jnp.bfloat16)
    queries = (project(pre_low, query_weight) + to_float(query_bias)).astype(jnp.bfloat16)
    patches = pre_low.reshape(count_images, KV, 2, KV, 2, model_width).transpose(0, 1, 3, 2, 4, 5)
    patches = patches.reshape(count_images, KV * KV, 4 * model_width)
    reduced = project(patches, reduce_weight) + to_float(reduce_bias)
    memory_out, memory_normed, memory_rstd = norm_forward(
        reduced, to_float(reduce_gain), to_float(reduce_shift)
    )
    memory = memory_out.astype(jnp.bfloat16)
    paired = project(memory, pair_weight)
    keys = paired[..., :model_width].astype(jnp.bfloat16)
    values = (paired[..., model_width:] + to_float(value_bias)).astype(jnp.bfloat16)
    mixed, log_total = lax.map(attend_forward, (queries, keys, values, key_mask))
    middle = inputs + project(mixed, output_weight) + to_float(output_bias)
    post_out, post_normed, post_rstd = norm_forward(middle, to_float(mlp_gain), to_float(mlp_shift))
    post = post_out.astype(jnp.bfloat16)
    expanded = project(post, expand_weight) + to_float(expand_bias)
    filled = (expanded * row_mask).astype(jnp.bfloat16)
    conv = depthwise(filled, to_float(spatial_weight), to_float(spatial_bias))
    gelu_out, gelu_pull = jax.vjp(partial(jax.nn.gelu, approximate=True), conv)
    activated = gelu_out.astype(jnp.bfloat16)
    shrunk = project(activated, shrink_weight) + to_float(shrink_bias)
    output = ((middle + shrunk) * row_mask).astype(jnp.bfloat16)
    pieces_back = unpack_params(
        lax.all_gather(low_params, ("dp", "fsdp"), axis=0, tiled=True), model_width, hidden_width
    )
    (
        back_pre_gain,
        unused_a,
        back_query_weight,
        unused_b,
        back_reduce_weight,
        unused_c,
        back_reduce_gain,
        unused_d,
        back_pair_weight,
        unused_e,
        back_output_weight,
        unused_f,
        back_mlp_gain,
        unused_g,
        back_expand_weight,
        unused_h,
        back_spatial_weight,
        unused_i,
        back_shrink_weight,
        unused_j,
    ) = pieces_back
    grad_float = cotangent.astype(jnp.float32) * row_mask
    grad_out = grad_float.astype(jnp.bfloat16)
    g_shrink_bias = column_sum(grad_out)
    g_shrink_weight = outer_sum(activated, grad_out)
    (grad_conv,) = gelu_pull(project_back(grad_out, back_shrink_weight))
    g_spatial_bias = jnp.sum(grad_conv, axis=(0, 1))
    g_spatial_weight, grad_filled = depthwise_back(grad_conv, filled, to_float(back_spatial_weight))
    grad_expanded = (grad_filled * row_mask).astype(jnp.bfloat16)
    g_expand_bias = column_sum(grad_expanded)
    g_expand_weight = outer_sum(post, grad_expanded)
    grad_post = project_back(grad_expanded, back_expand_weight)
    grad_middle_norm, g_mlp_gain, g_mlp_shift = norm_backward(
        grad_post, post_normed, post_rstd, to_float(back_mlp_gain)
    )
    grad_middle = grad_float + grad_middle_norm
    grad_branch = grad_middle.astype(jnp.bfloat16)
    g_output_bias = column_sum(grad_branch)
    g_output_weight = outer_sum(mixed, grad_branch)
    grad_mixed = project_back(grad_branch, back_output_weight).astype(jnp.bfloat16)
    grad_queries, grad_keys, grad_values = lax.map(
        attend_backward, (queries, keys, values, key_mask, log_total, grad_mixed)
    )
    g_query_bias = column_sum(grad_queries)
    g_query_weight = outer_sum(pre_low, grad_queries)
    grad_pre = project_back(grad_queries, back_query_weight)
    grad_pair = jnp.concatenate([grad_keys, grad_values], axis=-1)
    g_value_bias = column_sum(grad_values)
    g_pair_weight = outer_sum(memory, grad_pair)
    grad_memory = project_back(grad_pair, back_pair_weight)
    grad_reduced_float, g_reduce_gain, g_reduce_shift = norm_backward(
        grad_memory, memory_normed, memory_rstd, to_float(back_reduce_gain)
    )
    grad_reduced = grad_reduced_float.astype(jnp.bfloat16)
    g_reduce_bias = column_sum(grad_reduced)
    g_reduce_weight = outer_sum(patches, grad_reduced)
    grad_patches = project_back(grad_reduced, back_reduce_weight)
    grad_patches = grad_patches.reshape(count_images, KV, KV, 2, 2, model_width).transpose(
        0, 1, 3, 2, 4, 5
    )
    grad_pre = grad_pre + grad_patches.reshape(count_images, tokens_image, model_width)
    grad_inputs, g_pre_gain, g_pre_shift = norm_backward(
        grad_pre, pre_normed, pre_rstd, to_float(back_pre_gain)
    )
    grad_images = (grad_middle + grad_inputs) * row_mask
    n_outer = lax.axis_size("dp")
    n_inner = lax.axis_size("fsdp")
    total_entries = params.shape[0] * n_outer * n_inner
    grad_list = [
        g_pre_gain,
        g_pre_shift,
        g_query_weight,
        g_query_bias,
        g_reduce_weight,
        g_reduce_bias,
        g_reduce_gain,
        g_reduce_shift,
        g_pair_weight,
        g_value_bias,
        g_output_weight,
        g_output_bias,
        g_mlp_gain,
        g_mlp_shift,
        g_expand_weight,
        g_expand_bias,
        g_spatial_weight,
        g_spatial_bias,
        g_shrink_weight,
        g_shrink_bias,
    ]
    flat_grads = jnp.concatenate([piece.reshape(-1) for piece in grad_list])
    flat_grads = jnp.concatenate(
        [flat_grads, jnp.zeros((total_entries - flat_grads.shape[0],), jnp.float32)]
    )
    shard = lax.psum_scatter(flat_grads, ("dp", "fsdp"), scatter_dimension=0, tiled=True)
    squares = lax.psum(jnp.sum(shard * shard), ("dp", "fsdp"))
    grad_norm = jnp.sqrt(squares)
    clipped = shard * jnp.minimum(1.0, CLIP_NORM / (grad_norm + 1e-06))
    new_first = BETA_FIRST * first_moment + (1.0 - BETA_FIRST) * clipped
    new_second = BETA_SECOND * second_moment + (1.0 - BETA_SECOND) * clipped * clipped
    first_hat = new_first / (1.0 - BETA_FIRST**STEP)
    second_hat = new_second / (1.0 - BETA_SECOND**STEP)
    new_params = params - RATE * (first_hat / (jnp.sqrt(second_hat) + EPSILON) + DECAY * params)
    return (output, grad_images, grad_norm, new_first, new_second, new_params)


def solution(mesh):
    in_specs = (
        P(("dp", "fsdp"), None, None),
        P(("dp", "fsdp"), None, None),
        P(("dp", "fsdp")),
        P(("dp", "fsdp")),
        P(("dp", "fsdp")),
        P(("dp", "fsdp")),
    )
    out_specs = (
        P(("dp", "fsdp"), None, None),
        P(("dp", "fsdp"), None, None),
        P(),
        P(("dp", "fsdp")),
        P(("dp", "fsdp")),
        P(("dp", "fsdp")),
    )
    return jax.shard_map(local, mesh=mesh, in_specs=in_specs, out_specs=out_specs, check_vma=False)
```

profile of v0, /device:TPU:0, one launch (start us, length us, event | category | flops | bytes accessed | tf_op | source)
XLA Modules:
  0.0 1169.7 jit_solution(17053465655892715439)
XLA Ops:
  15.0 70.1 %all-gather.3.cloned.1.call-done = bf16[32,1,51840]{2,1,0:T(2,128)(2,1)} async-done(((bf16[1,1,51840]{2,1,0:T(2,128)(2,1)}), bf16[32,1,51840]{2,1,0:T(2,128)(2,1)}) %all-gather.3.cloned.1.call-update) | async-done | bytes 3317776 | tf_op jit(solution)/shard_map/all_gather | solution.py:198
  85.1 21.7 %reduce.4 = bf16[32,51840]{1,0:T(8,128)(2,1)} reduce(bf16[32,1,51840]{2,1,0:T(2,128)(2,1)} %all-gather.3.cloned.1.call-done, bf16[]{:T(256)} %constant.164), dimensions={1}, to_apply=%all-gather.reduce_sub_computation | reduce | bytes 6635522 | tf_op jit(solution)/shard_map/all_gather | solution.py:198
  182.2 80.3 %while.26 = (s32[]{:T(128)}, bf16[2,2304,320]{1,2,0:T(8,128)(2,1)}, f32[2,5,2304,1]{2,1,3,0:T(8,128)}, bf16[2,576,320]{1,2,0:T(8,128)(2,1)}, pred[2,576]{1,0:T(4...) while((s32[]{:T(128)}, bf16[2,2304,320]{1,2,0:T(8,128)(2,1)}, ...), condition=%wide.region_7.8_spmd, body=%wide.region_4.7_spmd.sunk | while | flops 1772409600 | bytes 114677728 | solution.py:240
  196.9 11.6 exponential_reduce_fusion.2
  209.2 11.8 %fusion.155 = bf16[5,64,2304]{2,1,0:T(8,128)(2,1)S(1)} fusion(bf16[576,5,64]{0,2,1:T(8,128)(2,1)S(1)} %bitcast.200, f32[5,2304,576]{1,2,0:T(8,128)} %get-tuple-element.399, f32[5,2304]{1,0:T(8,128)S(1)} %get-tuple-element.401, pred[576]{0:T(1024)(128)(4,1)S(1)} %dynamic-slice_reduce_fusion.4), kind=kOutput, calls=%fused_computation.6.clone.1 | convolution fusion | flops 876625920 | bytes 28431936 | tf_op jit(solution)/shard_map/while/body/eval_jaxpr/hsk,khd->shd/dot_general | solution.py:156
  249.0 11.8 %fusion.155 = bf16[5,64,2304]{2,1,0:T(8,128)(2,1)S(1)} fusion(bf16[576,5,64]{0,2,1:T(8,128)(2,1)S(1)} %bitcast.200, f32[5,2304,576]{1,2,0:T(8,128)} %get-tuple-element.399, f32[5,2304]{1,0:T(8,128)S(1)} %get-tuple-element.401, pred[576]{0:T(1024)(128)(4,1)S(1)} %dynamic-slice_reduce_fusion.4), kind=kOutput, calls=%fused_computation.6.clone.1 | convolution fusion | flops 876625920 | bytes 28431936 | tf_op jit(solution)/shard_map/while/body/eval_jaxpr/hsk,khd->shd/dot_general | solution.py:156
  268.5 11.6 fusion.51
  280.2 78.9 %fusion.46 = (bf16[2,48,48,1280]{3,2,1,0:T(8,128)(2,1)}, f32[2,48,48,1280]{3,2,1,0:T(8,128)}) fusion(f32[1280]{0:T(1024)S(1)} %copy-done.50, f32[1280]{0:T(1024)S(1)} %copy-done.51, f32[1280]{0:T(1024)S(1)} %copy-done.52, f32[1280]{0:T(1024)S(1)} %copy-done.53, f32[2,48,48,1280]{3,2,1,0:T(8,128)} %bitcast.185, f32[1280]{0:T(1024)S(1)} %copy-done.54, ...), kind=kLoop, calls=%fused_computation.86 | loop fusion | flops 159252480 | bytes 59033600 | tf_op jit(solution)/shard_map/convert_element_type | solution.py:248
  359.1 21.1 %fusion.48 = (bf16[2,2304,1280]{2,1,0:T(8,128)(2,1)}, f32[2,2304,1280]{2,1,0:T(8,128)}) fusion(f32[2,48,48,1280]{3,2,1,0:T(8,128)} %get-tuple-element.241), kind=kLoop, calls=%fused_computation.91 | loop fusion | flops 53084160 | bytes 58982400 | tf_op jit(solution)/shard_map/convert_element_type | solution.py:248
  380.2 35.4 %fusion.92 = (f32[1280]{0:T(1024)}, f32[1280]{0:T(1024)}, f32[2,2304,1280]{2,1,0:T(8,128)}) fusion(f32[2,2304,1280]{2,1,0:T(8,128)} %fusion.51, f32[2,2304,1280]{2,1,0:T(8,128)} %get-tuple-element.251, f32[2,48,48,1280]{3,2,1,0:T(8,128)} %get-tuple-element.241, bf16[1280,320]{1,0:T(8,128)(2,1)} %reshape.488, bf16[2,2304,320]{1,2,0:T(8,128)(2,1)S(1)} %copy-done.19, ...), kind=kOutput, calls=%fused_computation.235 | convolution fusion | flops 3885463040 | bytes 98168832 | tf_op jit(solution)/shard_map/...e,de->...d/dot_general | solution.py:92
  415.6 67.2 %multiply_reduce_fusion.1 = (f32[1280]{0:T(1024)}, f32[1280]{0:T(1024)}, f32[1280]{0:T(1024)}, f32[1280]{0:T(1024)}, f32[1280]{0:T(1024)}, /*index=5*/f32[1280]{0:T(1024)}, f32[1280]{0:T(1024)}, f32[1280]{0:T(1024)}) fusion(f32[2,48,48,1280]{3,2,1,0:T(8,128)} %bitcast.183, f32[2,48,48,1280]{3,2,1,0:T(8,128)} %bitcast.186), kind=kLoop, calls=%fused_computation.94 | loop fusion | flops 94361600 | bytes 47226880 | tf_op jit(solution)/shard_map/reduce_sum | solution.py:131
  482.8 80.0 %convert_reduce_fusion = (f32[1280]{0:T(1024)}, bf16[2,48,48,1280]{3,2,1,0:T(8,128)(2,1)}, f32[2,48,48,1280]{3,2,1,0:T(8,128)}) fusion(f32[2,48,48]{2,1,0:T(8,128)S(1)} %copy-done.41, f32[1280]{0:T(1024)S(1)} %copy-done.50, f32[1280]{0:T(1024)S(1)} %copy-done.51, f32[1280]{0:T(1024)S(1)} %copy-done.52, f32[1280]{0:T(1024)S(1)} %copy-done.53, ...), kind=kLoop, calls=%fused_computation.103 | loop fusion | flops 123861760 | bytes 59052032 | tf_op jit(solution)/shard_map/reduce_sum | solution.py:100
  586.4 186.5 %while.27 = (s32[]{:T(128)}, bf16[2,2304,320]{1,2,0:T(8,128)(2,1)}, bf16[2,576,320]{1,2,0:T(8,128)(2,1)}, bf16[2,576,320]{1,2,0:T(8,128)(2,1)}, bf16[2,576,320]{...) while((s32[]{:T(128)}, bf16[2,2304,320]{1,2,0:T(8,128)(2,1)}, ...), condition=%wide.region_14.15_spmd, body=%wide.region_12.14_spmd.sunk | while | flops 4348281856 | bytes 257431728 | solution.py:295
  604.2 12.4 %fusion.168 = bf16[5,64,576]{2,1,0:T(8,128)(2,1)} fusion(bf16[2304,5,64]{0,2,1:T(8,128)(2,1)S(1)} %bitcast.177, f32[5,2304,576]{1,2,0:T(8,128)} %fusion.166, f32[5,2304]{1,0:T(8,128)S(1)} %dynamic-slice_bitcast_fusion.2, pred[576]{0:T(1024)(128)(4,1)S(1)} %dynamic-slice_reduce_fusion.5), kind=kOutput, calls=%fused_computation.26.clone.1 | convolution fusion | flops 876072960 | bytes 28431936 | tf_op jit(solution)/shard_map/while/body/eval_jaxpr/hsk,shd->khd/dot_general | solution.py:166
  616.6 21.9 %multiply_reduce_fusion.24 = (f32[5,2304]{1,0:T(8,128)S(1)}, f32[5,2304,576]{1,2,0:T(8,128)}) fusion(f32[5,2304,576]{1,2,0:T(8,128)} %fusion.166, f32[5,2304]{1,0:T(8,128)S(1)} %dynamic-slice_bitcast_fusion.2, pred[576]{0:T(1024)(128)(4,1)S(1)} %dynamic-slice_reduce_fusion.5, bf16[2304,5,64]{0,2,1:T(8,128)(2,1)S(1)} %bitcast.178, ...), kind=kOutput, calls=%fused_computation.17.clone.1 | convolution fusion | flops 882512640 | bytes 55020096 | tf_op jit(solution)/shard_map/while/body/eval_jaxpr/shd,khd->hsk/dot_general | solution.py:169
  638.5 22.5 %multiply_convert_fusion.8 = bf16[5,2304,576]{1,2,0:T(8,128)(2,1)} fusion(f32[5,2304,576]{1,2,0:T(8,128)} %get-tuple-element.413, f32[5,2304,576]{1,2,0:T(8,128)} %fusion.166, f32[5,2304]{1,0:T(8,128)S(1)} %get-tuple-element.414, f32[5,2304]{1,0:T(8,128)S(1)} %dynamic-slice_bitcast_fusion.2, pred[576]{0:T(1024)(128)(4,1)S(1)} %dynamic-slice_reduce_fusion.5), kind=kLoop, calls=%fused_computation.16.clone.1 | loop fusion | flops 39813120 | bytes 66447936 | tf_op jit(solution)/shard_map/while/body/eval_jaxpr/convert_element_type | solution.py:173
  697.2 12.4 %fusion.168 = bf16[5,64,576]{2,1,0:T(8,128)(2,1)} fusion(bf16[2304,5,64]{0,2,1:T(8,128)(2,1)S(1)} %bitcast.177, f32[5,2304,576]{1,2,0:T(8,128)} %fusion.166, f32[5,2304]{1,0:T(8,128)S(1)} %dynamic-slice_bitcast_fusion.2, pred[576]{0:T(1024)(128)(4,1)S(1)} %dynamic-slice_reduce_fusion.5), kind=kOutput, calls=%fused_computation.26.clone.1 | convolution fusion | flops 876072960 | bytes 28431936 | tf_op jit(solution)/shard_map/while/body/eval_jaxpr/hsk,shd->khd/dot_general | solution.py:166
  709.6 21.9 %multiply_reduce_fusion.24 = (f32[5,2304]{1,0:T(8,128)S(1)}, f32[5,2304,576]{1,2,0:T(8,128)}) fusion(f32[5,2304,576]{1,2,0:T(8,128)} %fusion.166, f32[5,2304]{1,0:T(8,128)S(1)} %dynamic-slice_bitcast_fusion.2, pred[576]{0:T(1024)(128)(4,1)S(1)} %dynamic-slice_reduce_fusion.5, bf16[2304,5,64]{0,2,1:T(8,128)(2,1)S(1)} %bitcast.178, ...), kind=kOutput, calls=%fused_computation.17.clone.1 | convolution fusion | flops 882512640 | bytes 55020096 | tf_op jit(solution)/shard_map/while/body/eval_jaxpr/shd,khd->hsk/dot_general | solution.py:169
  731.5 22.5 %multiply_convert_fusion.8 = bf16[5,2304,576]{1,2,0:T(8,128)(2,1)} fusion(f32[5,2304,576]{1,2,0:T(8,128)} %get-tuple-element.413, f32[5,2304,576]{1,2,0:T(8,128)} %fusion.166, f32[5,2304]{1,0:T(8,128)S(1)} %get-tuple-element.414, f32[5,2304]{1,0:T(8,128)S(1)} %dynamic-slice_bitcast_fusion.2, pred[576]{0:T(1024)(128)(4,1)S(1)} %dynamic-slice_reduce_fusion.5), kind=kLoop, calls=%fused_computation.16.clone.1 | loop fusion | flops 39813120 | bytes 66447936 | tf_op jit(solution)/shard_map/while/body/eval_jaxpr/convert_element_type | solution.py:173
  850.2 12.1 %copy.73 = f32[2,2304,320]{1,2,0:T(8,128)} copy(f32[2,2304,320]{2,0,1:T(2,128)} %bitcast.195) | data formatting | bytes 11796480 | tf_op jit(solution)/shard_map/reshape | solution.py:315
  873.6 72.5 %concatenate.7 = f32[1658880]{0:T(1024)} concatenate(f32[320]{0:T(512)} %get-tuple-element.183, f32[320]{0:T(512)} %get-tuple-element.188, f32[102400]{0:T(1024)} %reshape.492, f32[320]{0:T(512)S(1)} %copy-done.85, f32[409600]{0:T(1024)} %reshape.493, f32[320]{0:T(512)S(1)} %get-tuple-element.238, f32[320]{0:T(512)} %get-tuple-element.189, f32[320]{0:T(512)} %get-tuple-element.192, ...), dimensions={0} | concatenate | bytes 13271040 | tf_op jit(solution)/shard_map/concatenate | solution.py:346
  953.6 150.9 %all-reduce.5.cloned.1.call-done = f32[1658880]{0:T(1024)} async-done(((f32[1658880]{0:T(1024)}), f32[1658880]{0:T(1024)}) %all-reduce.5.cloned.1.call-update) | async-done | bytes 6635536
  1106.2 12.3 %multiply_convert_fusion.3 = bf16[2,2304,320]{1,2,0:T(8,128)(2,1)} fusion(f32[2,2304,320]{1,2,0:T(8,128)} %copy-done.4, bf16[2,2304,1280]{2,1,0:T(8,128)(2,1)} %bitcast.197, f32[320]{0:T(512)S(1)} %copy-done.86, f32[2,2304]{1,0:T(2,128)S(1)} %copy-done.25, bf16[1280,320]{1,0:T(8,128)(2,1)} %reshape.488), kind=kOutput, calls=%fused_computation.119 | convolution fusion | flops 3780771840 | bytes 21482752 | tf_op jit(solution)/shard_map/dot_general | solution.py:88
  1118.5 40.3 %psum.7 = f32[]{:T(128)} all-reduce(f32[]{:T(128)} %multiply_reduce_fusion.22), channel_id=1, replica_groups=mesh['dp'=4,'fsdp'=8] {'dp','fsdp'}, use_global_device_ids=true, to_apply=%region_43.44 | all-reduce | flops 1 | bytes 8 | tf_op jit(solution)/shard_map/psum | solution.py:350
  (351 shorter events, 328.2 us)
Async XLA Ops:
  7.2 77.9 %all-gather.3.cloned.1.call-start = ((), (), s32[]{:S(2)}) async-start(), calls=%async_computation | async-start | bytes 6842880 | tf_op jit(solution)/shard_map/all_gather | solution.py:198
  9.1 1095.4 %all-reduce.5.cloned.1.call-start = ((), (), s32[]{:S(2)}) async-start(), calls=%async_computation.1 | async-start | bytes 13271040
  11.5 130.3 %copy-start.23 = (f32[2,2304]{1,0:T(2,128)}, f32[2,2304]{1,0:T(2,128)S(1)}, u32[]{:S(2)}) copy-start(f32[2,2304]{1,0:T(2,128)S(1)} %and_convert_fusion.1) | copy-start | bytes 55300
  13.9 127.8 %copy-start.36 = (f32[2,2304]{1,0:T(2,128)}, f32[2,2304]{1,0:T(2,128)S(1)}, u32[]{:S(2)}) copy-start(f32[2,2304]{1,0:T(2,128)S(1)} %broadcast_multiply_fusion.5) | copy-start | bytes 55300
  15.0 126.8 %copy-start.45 = (f32[2,2304]{1,0:T(2,128)}, f32[2,2304]{1,0:T(2,128)S(1)}, u32[]{:S(2)}) copy-start(f32[2,2304]{1,0:T(2,128)S(1)} %add_rsqrt_fusion.1) | copy-start | bytes 55300
  116.9 24.8 %copy-start.74 = (f32[320]{0:T(512)}, f32[320]{0:T(512)S(1)}, u32[]{:S(2)}) copy-start(f32[320]{0:T(512)S(1)} %get-tuple-element.265) | copy-start | bytes 3844
  116.9 51.2 %copy-start.72 = (f32[320]{0:T(512)}, f32[320]{0:T(512)S(1)}, u32[]{:S(2)}) copy-start(f32[320]{0:T(512)S(1)} %get-tuple-element.263) | copy-start | bytes 3844
  116.9 51.2 %copy-start.77 = (f32[320]{0:T(512)}, f32[320]{0:T(512)S(1)}, u32[]{:S(2)}) copy-start(f32[320]{0:T(512)S(1)} %get-tuple-element.262) | copy-start | bytes 3844
  182.2 80.3 %copy-start.2 = (bf16[2,2304,320]{1,2,0:T(8,128)(2,1)S(1)}, bf16[2,2304,320]{1,2,0:T(8,128)(2,1)}, u32[]{:S(2)}) copy-start(bf16[2,2304,320]{1,2,0:T(8,128)(2,1)} %param.10) | copy-start | bytes 8847364
  182.2 80.3 %copy-start.24 = (f32[2,2304]{1,0:T(2,128)S(1)}, f32[2,2304]{1,0:T(2,128)}, u32[]{:S(2)}) copy-start(f32[2,2304]{1,0:T(2,128)} %copy-done.23) | copy-start | bytes 55300
  182.2 80.3 %copy-start.27 = (bf16[320,320]{1,0:T(8,128)(2,1)S(1)}, bf16[320,320]{1,0:T(8,128)(2,1)}, u32[]{:S(2)}) copy-start(bf16[320,320]{1,0:T(8,128)(2,1)} %reshape.485) | copy-start | bytes 614404
  182.2 80.3 %copy-start.76 = (f32[320]{0:T(512)S(1)}, f32[320]{0:T(512)}, u32[]{:S(2)}) copy-start(f32[320]{0:T(512)} %get-tuple-element.258) | copy-start | bytes 3844
  266.7 307.7 %copy-start.43 = (f32[2,2304]{1,0:T(2,128)}, f32[2,2304]{1,0:T(2,128)S(1)}, u32[]{:S(2)}) copy-start(f32[2,2304]{1,0:T(2,128)S(1)} %broadcast_multiply_fusion.4) | copy-start | bytes 55300
  267.4 307.1 %copy-start.47 = (f32[2,2304]{1,0:T(2,128)}, f32[2,2304]{1,0:T(2,128)S(1)}, u32[]{:S(2)}) copy-start(f32[2,2304]{1,0:T(2,128)S(1)} %add_rsqrt_fusion) | copy-start | bytes 55300
  359.1 21.1 %copy-start.19 = (bf16[2,2304,320]{1,2,0:T(8,128)(2,1)S(1)}, bf16[2,2304,320]{1,2,0:T(8,128)(2,1)}, u32[]{:S(2)}) copy-start(bf16[2,2304,320]{1,2,0:T(8,128)(2,1)} %param.11) | copy-start | bytes 8847364
  415.6 67.2 %copy-start.41 = (f32[2,48,48]{2,1,0:T(8,128)S(1)}, f32[2,48,48]{2,1,0:T(8,128)}, u32[]{:S(2)}) copy-start(f32[2,48,48]{2,1,0:T(8,128)} %and_convert_fusion) | copy-start | bytes 55300
  482.8 80.0 %copy-start.31 = (bf16[320,1280,1]{1,0,2:T(8,128)(2,1)S(1)}, bf16[320,1280,1]{1,0,2:T(8,128)(2,1)}, u32[]{:S(2)}) copy-start(bf16[320,1280,1]{1,0,2:T(8,128)(2,1)} %reshape.506) | copy-start | bytes 2457604
  482.8 91.7 %slice-start = ((s8[5898240]{0:T(1024)(128)(4,1)}), s8[1703936]{0:T(1024)(128)(4,1)S(1)}, s32[]{:S(2)}) async-start(s8[5898240]{0:T(1024)(128)(4,1)} %bitcast.188), calls=%async_computation.2 | async-start | bytes 3407872
  792.8 14.6 %copy-start.62 = (f32[1280]{0:T(1024)S(1)}, f32[1280]{0:T(1024)}, u32[]{:S(2)}) copy-start(f32[1280]{0:T(1024)} %get-tuple-element.177) | copy-start | bytes 15364
  792.8 14.7 %copy-start.61 = (f32[1280]{0:T(1024)S(1)}, f32[1280]{0:T(1024)}, u32[]{:S(2)}) copy-start(f32[1280]{0:T(1024)} %get-tuple-element.178) | copy-start | bytes 15364
  946.1 160.1 %copy-start.86 = (f32[320]{0:T(512)S(1)}, f32[320]{0:T(512)}, u32[]{:S(2)}) copy-start(f32[320]{0:T(512)} %get-tuple-element.255) | copy-start | bytes 3844
  1106.2 53.3 %copy-start.29 = (f32[51840]{0:T(1024)S(1)}, f32[51840]{0:T(1024)}, u32[]{:S(2)}) copy-start(f32[51840]{0:T(1024)} %param.13) | copy-start | bytes 622084
  1106.2 53.3 %copy-start.39 = (f32[51840]{0:T(1024)S(1)}, f32[51840]{0:T(1024)}, u32[]{:S(2)}) copy-start(f32[51840]{0:T(1024)} %param.15) | copy-start | bytes 622084
  1106.2 53.3 %copy-start.40 = (f32[51840]{0:T(1024)S(1)}, f32[51840]{0:T(1024)}, u32[]{:S(2)}) copy-start(f32[51840]{0:T(1024)} %param.14) | copy-start | bytes 622084
  (83 other events, 662.6 us)
Sparse Core Ops, SparseCore 0:
  11.5 73.5 all-gather.2
  946.2 158.3 all-reduce.4
where the time goes:
time: 1180 us; the launch traced here: 1170 us
  other arithmetic  382 us (32%)
  matrix products  303 us (26%)
  waiting for transfers between devices  221 us (19%)
  local copies, waits for them, and re-layouts  205 us (17%)
  blocking collectives  40.3 us (3%)
  between operations  17.3 us (1%)
    unnamed x3, waiting for transfers between devices  151 us
    convert_element_type x2, other arithmetic, local(): activated = gelu_out.astype(jnp.bfloat16)  100 us
    reduce_sum x5, other arithmetic, column_sum(): return jnp.sum(grad.astype(jnp.float32), axis=(0, 1))  86.6 us
    concatenate x1, local copies, waits for them, and re-layouts, local(): jnp.concatenate([flat_grads, jnp.zeros((total_entries - flat_grads.shape[...  72.5 us
    all_gather x1, waiting for transfers between devices, local(): lax.all_gather(low_params, ('dp', 'fsdp'), axis=0, tiled=True)  70.1 us
    dot_general x6, matrix products, project_back(): jnp.einsum('...e,de->...d', grad, weight, preferred_element_type=jnp.floa...  68.2 us
    reduce_sum x1, other arithmetic, depthwise_back(): tap_grads.append(jnp.sum(window * grad_grid, axis=(0, 1, 2)))  67.2 us
    convert_element_type x2, other arithmetic, attend_backward(): grad_scores = grad_scores.astype(jnp.bfloat16)  45 us
  transfers between devices with their start and end apart: 2, of which 2 were waited for; matrix products, arithmetic and copies ran while one was open for 1% of the time, Pallas kernels for 0%

commit v1 on v0

v1 whole, which is shorter than its diff:
```python
from functools import partial
import math

import jax
import jax.numpy as jnp
import numpy as np
from jax import lax
from jax.experimental import pallas as pl
from jax.experimental.pallas import tpu as pltpu
from jax.sharding import PartitionSpec as P

HEADS = 5
HEAD_DIM = 64
GRID = 48
KV = 24
STEP = 10

CLIP_NORM = 1.0
BETA_FIRST = 0.9
BETA_SECOND = 0.999
RATE = 0.04
DECAY = 0.05
EPSILON = 1e-08

F32 = jnp.float32
BF = jnp.bfloat16
NN = (((1,), (0,)), ((), ()))
NT = (((1,), (1,)), ((), ()))
TOKENS = GRID * GRID
KEYS = KV * KV
PITCH = GRID + 8
EXT = 16
LOG2E = math.log2(math.e)
QUERY_SCALE = HEAD_DIM**-0.5 * LOG2E
GELU_A = math.sqrt(2.0 / math.pi)
GELU_B = GELU_A * 0.044715
VMEM_BYTES = 63 * 1024 * 1024


def mm(left, right, dims=NN):
    return lax.dot_general(left, right, dims, preferred_element_type=F32)


def patch_order():
    matrix = np.zeros((8 * GRID, 8 * GRID), np.float32)
    for p in range(4):
        for a in range(4):
            for b in range(KV):
                matrix[p * 96 + a * KV + b, (2 * a + p // 2) * GRID + 2 * b + p % 2] = 1.0
    return matrix


def fold_rows(x):
    return jnp.sum(x.reshape(x.shape[0] // 8, 8, x.shape[1]), axis=0)


def norm_columns(x):
    scale = 1.0 / x.shape[0]
    centred = x - jnp.sum(x, axis=0, keepdims=True) * scale
    rstd = lax.rsqrt(jnp.sum(centred * centred, axis=0, keepdims=True) * scale + 1e-06)
    return centred * rstd, rstd


def norm_columns_back(normed, rstd, scaled):
    scale = 1.0 / scaled.shape[0]
    plain = jnp.sum(scaled, axis=0, keepdims=True) * scale
    mixed = jnp.sum(scaled * normed, axis=0, keepdims=True) * scale
    return rstd * (scaled - plain - normed * mixed)


def norm_rows(x):
    centred = x - jnp.mean(x, axis=-1, keepdims=True)
    rstd = lax.rsqrt(jnp.mean(centred * centred, axis=-1, keepdims=True) + 1e-06)
    return centred * rstd, rstd


def norm_rows_back(normed, rstd, scaled):
    plain = jnp.mean(scaled, axis=-1, keepdims=True)
    mixed = jnp.mean(scaled * normed, axis=-1, keepdims=True)
    return rstd * (scaled - plain - normed * mixed)


def first_row(row, rows=EXT):
    index = lax.broadcasted_iota(jnp.int32, (rows, row.shape[-1]), 0)
    return jnp.where(index == 0, row, 0.0)


def three_parts(x):
    high = x.astype(BF).astype(F32)
    middle = (x - high).astype(BF).astype(F32)
    return high, middle, (x - high - middle).astype(BF).astype(F32)


def whole(x):
    zeros = (0,) * len(x.shape)
    return pl.BlockSpec(x.shape, lambda *_: zeros)


def per_image(x, **kwargs):
    zeros = (0,) * (len(x.shape) - 1)
    return pl.BlockSpec((1,) + tuple(x.shape[1:]), lambda i, *_: (i,) + zeros, **kwargs)


def key_columns(ref, side, h_range, ones_from, ones_to, with_mask):
    lane = lax.broadcasted_iota(jnp.int32, (KV, 64), 1)
    cell = lax.broadcasted_iota(jnp.int32, (KV, 64), 0)
    ones = jnp.where((lane >= ones_from) & (lane <= ones_to), 1.0, 0.0)
    for a in range(KV):
        block = ones
        if with_mask:
            bias = jnp.where((cell < side) & (a < side), 0.0, -1e30)
            block = jnp.where(lane == 0, bias, ones)
        block = block.astype(BF)
        for h in h_range:
            ref[h, a * KV : (a + 1) * KV, 64:128] = block


def attention_forward_kernel(
    sides, images, mask, perm, vec, rows, wqt, wr, wk, wvt, wot,
    pre, patches, reduced, memory, mixed, lse, middle, post,
    key_ref, value_ref,
):
    i = pl.program_id(0)
    width = images.shape[1]

    def first_norm(t, _):
        for u in range(3):
            at = pl.ds(pl.multiple_of(t * 384 + u * 128, 128), 128)
            x = images[0, :, at].astype(F32) * mask[0, 0:1, at]
            normed, _unused = norm_columns(x)
            pre[0, 0:width, at] = (normed * vec[0] + vec[1]).astype(BF)
            pre[0, width : width + EXT, at] = first_row(jnp.ones((1, 128), F32)).astype(BF)
        at = pl.ds(pl.multiple_of(t * 384, 128), 384)
        picked = mm(perm[...], pre[0, 0:width, at], NT).astype(BF)
        for p in range(4):
            patches[0, p, pl.ds(pl.multiple_of(t * 96, 32), 96), :] = picked[p * 96 : (p + 1) * 96]
        return 0

    lax.fori_loop(0, TOKENS // 384, first_norm, 0)

    total = rows[0:1, :]
    for p in range(4):
        total = total + mm(patches[0, p], wr[p])
    reduced[0] = total
    normed, _unused = norm_rows(total)
    memory[0, :, 0:width] = (normed * rows[1:2, :] + rows[2:3, :]).astype(BF)
    lane = lax.broadcasted_iota(jnp.int32, (KEYS, 64), 1)
    memory[0, :, width : width + 64] = jnp.where(lane == 0, 1.0, 0.0).astype(BF)
    keys = mm(memory[0, :, 0:width], wk[...]).astype(BF)
    key_columns(key_ref, sides[i], range(HEADS), 1, 0, True)
    values = mm(wvt[...], memory[0], NT).astype(BF)
    ones = first_row(jnp.ones((1, KEYS), F32)).astype(BF)
    for h in range(HEADS):
        at = slice(h * HEAD_DIM, (h + 1) * HEAD_DIM)
        key_ref[h, :, 0:HEAD_DIM] = keys[:, at]
        value_ref[h, 0:HEAD_DIM, :] = values[at]
        value_ref[h, HEAD_DIM : HEAD_DIM + EXT, :] = ones
    mixed[0, width : width + EXT, :] = first_row(jnp.ones((1, TOKENS), F32)).astype(BF)
    queries = (mm(wqt[...], pre[0]) * QUERY_SCALE).astype(BF)
    tail = first_row(jnp.ones((1, TOKENS), F32), 64).astype(BF)
    for h in range(HEADS):
        at = slice(h * HEAD_DIM, (h + 1) * HEAD_DIM)
        scores = mm(key_ref[h], jnp.concatenate([queries[at], tail], axis=0))
        top = jnp.max(scores, axis=0, keepdims=True)
        weights = jnp.exp2(scores - top).astype(BF)
        out = mm(value_ref[h], weights)
        total = out[HEAD_DIM : HEAD_DIM + 1]
        mixed[0, at, :] = (out[0:HEAD_DIM] * (1.0 / total)).astype(BF)
        lse[0, h : h + 1, :] = top + jnp.log2(total)

    def second_norm(t, _):
        at = pl.ds(pl.multiple_of(t * 384, 128), 384)
        branch = mm(wot[...], mixed[0, :, at])
        for u in range(3):
            at = pl.ds(pl.multiple_of(t * 384 + u * 128, 128), 128)
            here = mask[0, 0:1, at]
            x = images[0, :, at].astype(F32) * here + branch[:, u * 128 : (u + 1) * 128]
            middle[0, :, at] = x
            normed, _unused = norm_columns(x)
            post[0, 0:width, at] = ((normed * vec[2] + vec[3]) * here).astype(BF)
            post[0, width : width + EXT, at] = first_row(here).astype(BF)
        return 0

    lax.fori_loop(0, TOKENS // 384, second_norm, 0)


def attention_forward(sides, images, mask, perm, vec, rows, wqt, wr, wk, wvt, wot):
    n, width, tokens = images.shape
    shape = jax.ShapeDtypeStruct
    outs = [
        shape((n, width + EXT, tokens), BF),
        shape((n, 4, KEYS, width), BF),
        shape((n, KEYS, width), F32),
        shape((n, KEYS, width + 64), BF),
        shape((n, width + EXT, tokens), BF),
        shape((n, 8, tokens), F32),
        shape((n, width, tokens), F32),
        shape((n, width + EXT, tokens), BF),
    ]
    weights = (perm, vec, rows, wqt, wr, wk, wvt, wot)
    return pl.pallas_call(
        attention_forward_kernel,
        grid_spec=pltpu.PrefetchScalarGridSpec(
            num_scalar_prefetch=1,
            grid=(n,),
            in_specs=[per_image(images), per_image(mask)] + [whole(x) for x in weights],
            out_specs=[per_image(x) for x in outs],
            scratch_shapes=[
                pltpu.VMEM((HEADS, KEYS, 128), BF),
                pltpu.VMEM((HEADS, HEAD_DIM + EXT, KEYS), BF),
            ],
        ),
        out_shape=outs,
        compiler_params=pltpu.CompilerParams(vmem_limit_bytes=VMEM_BYTES),
        name="attention_forward",
    )(sides, images, mask, *weights)


def feed_forward_kernel(
    post, cot, mask, middle, we, wst, taps, vec,
    output, grad_post, gwe, gwst, gtaps, gbias,
    padded, grad_padded, grad_act, act, grad_exp, post_rows, out_grad, out_grad_rows, total,
):
    i = pl.program_id(0)
    j = pl.program_id(1)
    width, block = wst.shape
    halves = block // 128
    rows = 8
    chunks = GRID // rows
    span = rows * GRID
    cols = 16

    @pl.when((i == 0) & (j == 0))
    def _():
        for ref in (padded, grad_padded, gwe, gwst, gtaps, gbias, post_rows):
            ref[...] = jnp.zeros_like(ref)

    @pl.when(j == 0)
    def _():
        for t in range(TOKENS // 384):
            at = slice(t * 384, (t + 1) * 384)
            grad = cot[0, :, at].astype(F32) * mask[0, 0:1, at]
            gbias[...] += grad[:, 0:128] + grad[:, 128:256] + grad[:, 256:384]
            grad = grad.astype(BF)
            out_grad[:, at] = grad
            out_grad_rows[at, :] = grad.T
            post_rows[at, 0 : width + EXT] = post[0, :, at].T

    def expand(t, _):
        at = pl.ds(pl.multiple_of(t * span, span), span)
        filled = mm(post_rows[at, :], we[...]).astype(BF).astype(F32)
        for h in range(halves):
            for r in range(rows):
                start = pl.multiple_of((t * rows + r + 1) * PITCH + 8, 8)
                padded[h, pl.ds(start, GRID), :] = filled[
                    r * GRID : (r + 1) * GRID, h * 128 : (h + 1) * 128
                ]
        grad_act[at, :] = mm(out_grad_rows[at, :], wst[...])
        return 0

    lax.fori_loop(0, chunks, expand, 0)

    def convolve(t, _):
        for h in range(halves):
            hs = slice(h * 128, (h + 1) * 128)
            w = [jnp.broadcast_to(taps[k : k + 1, hs], (cols, 128)) for k in range(10)]
            sums = jnp.zeros((8, 128), F32)
            for ct in range(GRID // cols):
                open_rows = {}
                for q in range(-1, rows + 1):
                    base = (t * rows + q + 1) * PITCH + 8 + ct * cols
                    x = [padded[h, pl.ds(base + s, cols), :] for s in (-1, 0, 1)]
                    for a in (2, 1, 0):
                        r = q + 1 - a
                        if 0 <= r < rows:
                            part = w[3 * a] * x[0] + w[3 * a + 1] * x[1] + w[3 * a + 2] * x[2]
                            open_rows[r] = part + open_rows.get(r, w[9])
                    r = q - 1
                    if r < 0:
                        continue
                    conv = open_rows.pop(r)
                    square = conv * conv
                    half = 0.5 * jnp.tanh(conv * (GELU_B * square + GELU_A)) + 0.5
                    gelu = conv * half
                    slope = half + gelu * (1.0 - half) * ((6.0 * GELU_B) * square + 2.0 * GELU_A)
                    at = pl.ds(pl.multiple_of((t * rows + r) * GRID + ct * cols, cols), cols)
                    act[at, hs] = gelu.astype(BF)
                    grad = grad_act[at, hs] * slope
                    start = pl.multiple_of((t * rows + r + 1) * PITCH + 8 + ct * cols, 8)
                    grad_padded[h, pl.ds(start, cols), :] = grad
                    sums = sums + grad[0:8] + grad[8:16]
            js = pl.ds(pl.multiple_of(j * block + h * 128, 128), 128)
            gtaps[72:80, js] += sums
        return 0

    lax.fori_loop(0, chunks, convolve, 0)

    def convolve_back(t, _):
        for h in range(halves):
            hs = slice(h * 128, (h + 1) * 128)
            w = [jnp.broadcast_to(taps[k : k + 1, hs], (cols, 128)) for k in range(9)]
            sums = [jnp.zeros((8, 128), F32) for _ in range(9)]
            for ct in range(GRID // cols):
                open_rows = {}
                x = {}
                for q in range(-1, rows + 1):
                    base = (t * rows + q + 1) * PITCH + 8 + ct * cols
                    grads = [grad_padded[h, pl.ds(base + 1 - b, cols), :] for b in range(3)]
                    if q + 1 < rows:
                        start = pl.multiple_of((t * rows + q + 2) * PITCH + 8 + ct * cols, 8)
                        x[q + 1] = padded[h, pl.ds(start, cols), :]
                    for a in range(3):
                        r = q + a - 1
                        if not 0 <= r < rows:
                            continue
                        part = w[3 * a] * grads[0] + w[3 * a + 1] * grads[1] + w[3 * a + 2] * grads[2]
                        open_rows[r] = part + open_rows[r] if r in open_rows else part
                        for b in range(3):
                            product = x[r] * grads[b]
                            sums[3 * a + b] = sums[3 * a + b] + product[0:8] + product[8:16]
                    r = q - 1
                    if r >= 0:
                        at = pl.ds(pl.multiple_of((t * rows + r) * GRID + ct * cols, cols), cols)
                        grad_exp[at, hs] = open_rows.pop(r).astype(BF)
                        x.pop(r)
            js = pl.ds(pl.multiple_of(j * block + h * 128, 128), 128)
            for k in range(9):
                gtaps[8 * k : 8 * k + 8, js] += sums[k]
        return 0

    lax.fori_loop(0, chunks, convolve_back, 0)

    js = pl.ds(pl.multiple_of(j * block, block), block)
    gwst[:, js] += mm(out_grad[...], act[...])
    gwe[:, js] += mm(post[0], grad_exp[...])
    shrunk = mm(wst[...], act[...], NT)
    back = mm(we[0:width, :], grad_exp[...], NT)

    @pl.when(j == 0)
    def _():
        total[...] = shrunk
        grad_post[0] = back

    @pl.when(j != 0)
    def _():
        total[...] += shrunk
        grad_post[0] += back

    @pl.when(j == pl.num_programs(1) - 1)
    def _():
        for t in range(TOKENS // 128):
            at = slice(t * 128, (t + 1) * 128)
            output[0, :, at] = ((middle[0, :, at] + total[:, at] + vec[4]) * mask[0, 0:1, at]).astype(BF)


def feed_forward(post, cot, mask, middle, we, wst, taps, vec, block=256):
    n, width, tokens = cot.shape
    hidden = wst.shape[1]
    shape = jax.ShapeDtypeStruct
    outs = [
        shape((n, width, tokens), BF),
        shape((n, width, tokens), F32),
        shape((width + EXT, hidden), F32),
        shape((width, hidden), F32),
        shape((80, hidden), F32),
        shape((width, 128), F32),
    ]
    one = {"pipeline_mode": pl.Buffered(1)}
    columns = lambda x: pl.BlockSpec((x.shape[0], block), lambda i, j: (0, j))
    return pl.pallas_call(
        feed_forward_kernel,
        grid=(n, hidden // block),
        in_specs=[per_image(post), per_image(cot), per_image(mask), per_image(middle, **one)]
        + [columns(we), columns(wst), columns(taps), whole(vec)],
        out_specs=[per_image(x) for x in outs[:2]] + [whole(x) for x in outs[2:]],
        out_shape=outs,
        scratch_shapes=[
            pltpu.VMEM((block // 128, (GRID + 2) * PITCH + 8, 128), F32),
            pltpu.VMEM((block // 128, (GRID + 2) * PITCH + 8, 128), F32),
            pltpu.VMEM((tokens, block), F32),
            pltpu.VMEM((tokens, block), BF),
            pltpu.VMEM((tokens, block), BF),
            pltpu.VMEM((tokens, width + 64), BF),
            pltpu.VMEM((width, tokens), BF),
            pltpu.VMEM((tokens, width), BF),
            pltpu.VMEM((width, tokens), F32),
        ],
        compiler_params=pltpu.CompilerParams(vmem_limit_bytes=VMEM_BYTES),
        name="feed_forward",
    )(post, cot, mask, middle, we, wst, taps, vec)


def attention_backward_kernel(
    sides, images, cot, mask, pre, patches, reduced, memory, mixed, lse, middle, grad_post,
    perm, vec, rows, wq, wqt, wr, wk, wv, wvt, wo,
    grad_images, gwo, gwq, gpair, gwr, gcols, grows,
    branch, grad_mixed, queries, grad_queries, key_ref, value_ref, keys_t, grad_keys, grad_values, grad_patches,
):
    i = pl.program_id(0)
    width = images.shape[1]

    @pl.when(i == 0)
    def _():
        for ref in (gwo, gwq, gpair, gwr, gcols, grows):
            ref[...] = jnp.zeros_like(ref)

    def mlp_norm_back(t, _):
        gain = shift = jnp.zeros((width, 128), F32)
        for u in range(3):
            at = pl.ds(pl.multiple_of(t * 384 + u * 128, 128), 128)
            here = mask[0, 0:1, at]
            normed, rstd = norm_columns(middle[0, :, at])
            grad = grad_post[0, :, at] * here
            gain = gain + grad * normed
            shift = shift + grad
            grad = cot[0, :, at].astype(F32) * here + norm_columns_back(normed, rstd, grad * vec[2])
            grad_images[0, :, at] = grad
            branch[:, at] = grad.astype(BF)
        gcols[2] += gain
        gcols[3] += shift
        return 0

    lax.fori_loop(0, TOKENS // 384, mlp_norm_back, 0)
    gwo[...] += mm(mixed[0], branch[...], NT)
    grad_mixed[...] = mm(wo[...], branch[...]).astype(BF)
    queries[...] = (mm(wqt[...], pre[0]) * QUERY_SCALE).astype(BF)
    keys = mm(memory[0, :, 0:width], wk[...]).astype(BF)
    keys_t[...] = keys.T
    values = mm(wvt[...], memory[0], NT).astype(BF).T
    key_columns(key_ref, sides[i], range(HEADS), 1, 3, True)
    key_columns(value_ref, sides[i], range(HEADS), 1, 3, False)
    for h in range(HEADS):
        at = slice(h * HEAD_DIM, (h + 1) * HEAD_DIM)
        key_ref[h, :, 0:HEAD_DIM] = keys[:, at]
        value_ref[h, :, 0:HEAD_DIM] = values[:, at]

    span = TOKENS // 2
    index = lax.broadcasted_iota(jnp.int32, (64, span), 0)
    for t in range(TOKENS // span):
        at = slice(t * span, (t + 1) * span)
        for h in range(HEADS):
            hs = slice(h * HEAD_DIM, (h + 1) * HEAD_DIM)
            one, two, three = three_parts(-lse[0, h : h + 1, at])
            tail = jnp.where(index == 2, two, jnp.where(index == 3, three, 0.0))
            tail = jnp.where(index == 0, 1.0, jnp.where(index == 1, one, tail)).astype(BF)
            query = queries[hs, at]
            attend = jnp.exp2(mm(key_ref[h], jnp.concatenate([query, tail], axis=0)))
            low = attend.astype(BF)
            grad = grad_mixed[hs, at]
            inner = grad.astype(F32) * mixed[0, hs, at].astype(F32)
            one, two, three = three_parts(-jnp.sum(inner, axis=0, keepdims=True))
            tail = jnp.where(index == 2, two, jnp.where(index == 3, three, 0.0))
            tail = jnp.where(index == 1, one, tail).astype(BF)
            grad_attend = mm(value_ref[h], jnp.concatenate([grad, tail], axis=0))
            grad_scores = (attend * grad_attend).astype(BF)
            grad_value = mm(grad, low, NT)
            grad_key = mm(query, grad_scores, NT) * (1.0 / LOG2E)
            if t == 0:
                grad_values[hs, :] = grad_value
                grad_keys[hs, :] = grad_key
            else:
                grad_values[hs, :] += grad_value
                grad_keys[hs, :] += grad_key
            grad_queries[hs, at] = (mm(keys_t[hs, :], grad_scores) * HEAD_DIM**-0.5).astype(BF)

    low_keys = grad_keys[...].astype(BF)
    low_values = grad_values[...].astype(BF)
    gpair[0:width, :] += mm(low_keys, memory[0])
    gpair[width : 2 * width, :] += mm(low_values, memory[0])
    grad_memory = mm(low_keys.T, wk[...], NT) + mm(low_values.T, wv[...], NT)
    normed, rstd = norm_rows(reduced[0])
    grows[8:16, :] += fold_rows(grad_memory * normed)
    grows[16:24, :] += fold_rows(grad_memory)
    grad_reduced = norm_rows_back(normed, rstd, grad_memory * rows[1:2, :]).astype(BF)
    grows[0:8, :] += fold_rows(grad_reduced.astype(F32))
    grad_reduced_t = grad_reduced.T
    for p in range(4):
        gwr[p] += mm(grad_reduced_t, patches[0, p])
        grad_patches[p] = mm(grad_reduced, wr[p], NT).astype(BF)
    gwq[...] += mm(pre[0], grad_queries[...], NT)

    def pre_norm_back(t, _):
        at = pl.ds(pl.multiple_of(t * 384, 128), 384)
        grad_pre = mm(wq[...], grad_queries[:, at])
        start = pl.ds(pl.multiple_of(t * 96, 32), 96)
        picked = jnp.concatenate([grad_patches[p, start, :] for p in range(4)], axis=0)
        grad_pre = grad_pre + mm(picked.T, perm[...])
        gain = shift = jnp.zeros((width, 128), F32)
        for u in range(3):
            at = pl.ds(pl.multiple_of(t * 384 + u * 128, 128), 128)
            here = mask[0, 0:1, at]
            normed, rstd = norm_columns(images[0, :, at].astype(F32) * here)
            grad = grad_pre[:, u * 128 : (u + 1) * 128]
            gain = gain + grad * normed
            shift = shift + grad
            back = norm_columns_back(normed, rstd, grad * vec[0])
            grad_images[0, :, at] = (grad_images[0, :, at] + back) * here
        gcols[0] += gain
        gcols[1] += shift
        return 0

    lax.fori_loop(0, TOKENS // 384, pre_norm_back, 0)


def attention_backward(
    sides, images, cot, mask, pre, patches, reduced, memory, mixed, lse, middle, grad_post,
    perm, vec, rows, wq, wqt, wr, wk, wv, wvt, wo,
):
    n, width, tokens = images.shape
    shape = jax.ShapeDtypeStruct
    outs = [
        shape((n, width, tokens), F32),
        shape((width + EXT, width), F32),
        shape((width + EXT, width), F32),
        shape((2 * width, width + 64), F32),
        shape((4, width, width), F32),
        shape((4, width, 128), F32),
        shape((24, width), F32),
    ]
    one = {"pipeline_mode": pl.Buffered(1)}
    inputs = (images, cot, mask, pre, patches, reduced, memory, mixed, lse)
    weights = (perm, vec, rows, wq, wqt, wr, wk, wv, wvt, wo)
    return pl.pallas_call(
        attention_backward_kernel,
        grid_spec=pltpu.PrefetchScalarGridSpec(
            num_scalar_prefetch=1,
            grid=(n,),
            in_specs=[per_image(x) for x in inputs]
            + [per_image(middle, **one), per_image(grad_post, **one)]
            + [whole(x) for x in weights],
            out_specs=[per_image(outs[0], **one)] + [whole(x) for x in outs[1:]],
            scratch_shapes=[
                pltpu.VMEM((width, tokens), BF),
                pltpu.VMEM((width, tokens), BF),
                pltpu.VMEM((width, tokens), BF),
                pltpu.VMEM((width, tokens), BF),
                pltpu.VMEM((HEADS, KEYS, 128), BF),
                pltpu.VMEM((HEADS, KEYS, 128), BF),
                pltpu.VMEM((width, KEYS), BF),
                pltpu.VMEM((width, KEYS), F32),
                pltpu.VMEM((width, KEYS), F32),
                pltpu.VMEM((4, KEYS, width), BF),
            ],
        ),
        out_shape=outs,
        compiler_params=pltpu.CompilerParams(vmem_limit_bytes=VMEM_BYTES),
        name="attention_backward",
    )(sides, *inputs, middle, grad_post, *weights)


def layout_shapes(model_width, hidden_width):
    return [
        (model_width,),
        (model_width,),
        (model_width, model_width),
        (model_width,),
        (4 * model_width, model_width),
        (model_width,),
        (model_width,),
        (model_width,),
        (model_width, 2 * model_width),
        (model_width,),
        (model_width, model_width),
        (model_width,),
        (model_width,),
        (model_width,),
        (model_width, hidden_width),
        (hidden_width,),
        (9, hidden_width),
        (hidden_width,),
        (hidden_width, model_width),
        (model_width,),
    ]


def unpack_params(flat, model_width, hidden_width):
    pieces = []
    offset = 0
    for shape in layout_shapes(model_width, hidden_width):
        count = math.prod(shape)
        pieces.append(flat[offset : offset + count].reshape(shape))
        offset += count
    return pieces


def arrange_weights(flat, width, hidden):
    (
        pre_gain,
        pre_shift,
        query_weight,
        query_bias,
        reduce_weight,
        reduce_bias,
        reduce_gain,
        reduce_shift,
        pair_weight,
        value_bias,
        output_weight,
        output_bias,
        mlp_gain,
        mlp_shift,
        expand_weight,
        expand_bias,
        spatial_weight,
        spatial_bias,
        shrink_weight,
        shrink_bias,
    ) = unpack_params(flat, width, hidden)

    def with_bias(weight, bias, extra):
        return jnp.concatenate([weight.T, bias[:, None], jnp.zeros((width, extra - 1), BF)], axis=1)

    columns = jnp.stack([pre_gain, pre_shift, mlp_gain, mlp_shift, shrink_bias]).astype(F32)
    return dict(
        vec=jnp.broadcast_to(columns[:, :, None], (5, width, 128)),
        rows=jnp.stack([reduce_bias, reduce_gain, reduce_shift]).astype(F32),
        wq=query_weight,
        wqt=with_bias(query_weight, query_bias, EXT),
        wr=reduce_weight.reshape(4, width, width),
        wk=pair_weight[:, :width],
        wv=pair_weight[:, width:],
        wvt=with_bias(pair_weight[:, width:], value_bias, 64),
        wo=output_weight,
        wot=with_bias(output_weight, output_bias, EXT),
        we=jnp.concatenate([expand_weight, expand_bias[None], jnp.zeros((63, hidden), BF)]),
        wst=shrink_weight.T,
        taps=jnp.concatenate([spatial_weight, spatial_bias[None]]).astype(F32),
    )


def device_step(images, cotangent, kv_sides, w):
    positions = jnp.arange(TOKENS, dtype=jnp.int32)
    limit = 2 * kv_sides[:, None]
    mask = ((positions[None] // GRID < limit) & (positions[None] % GRID < limit)).astype(F32)
    mask = jnp.broadcast_to(mask[:, None, :], (mask.shape[0], 8, TOKENS))
    perm = jnp.asarray(patch_order(), BF)
    pre, patches, reduced, memory, mixed, lse, middle, post = attention_forward(
        kv_sides, images, mask, perm, w["vec"], w["rows"], w["wqt"], w["wr"], w["wk"], w["wvt"], w["wot"]
    )
    output, grad_post, gwe, gwst, gtaps, gbias = feed_forward(
        post, cotangent, mask, middle, w["we"], w["wst"], w["taps"], w["vec"]
    )
    grad_images, gwo, gwq, gpair, gwr, gcols, grows = attention_backward(
        kv_sides, images, cotangent, mask, pre, patches, reduced, memory, mixed, lse, middle, grad_post,
        perm, w["vec"], w["rows"], w["wq"], w["wqt"], w["wr"], w["wk"], w["wv"], w["wvt"], w["wo"],
    )
    return output, grad_images, (gwe, gwst, gtaps, gbias, gwo, gwq, gpair, gwr, gcols, grows)


def gradient_pieces(grads, width, hidden):
    gwe, gwst, gtaps, gbias, gwo, gwq, gpair, gwr, gcols, grows = grads
    columns = gcols.sum(axis=2)
    sums = grows.reshape(3, 8, width).sum(axis=1)
    taps = gtaps.reshape(10, 8, hidden).sum(axis=1)
    pair = gpair.T
    return [
        columns[0],
        columns[1],
        gwq[:width],
        gwq[width],
        gwr.transpose(0, 2, 1),
        sums[0],
        sums[1],
        sums[2],
        pair[:width],
        pair[width, width:],
        gwo[:width],
        gwo[width],
        columns[2],
        columns[3],
        gwe[:width],
        gwe[width],
        taps[:9],
        taps[9],
        gwst.T,
        gbias.sum(axis=1),
    ]


def local(images, cotangent, kv_sides, params, first_moment, second_moment):
    width = images.shape[2]
    hidden = 4 * width
    total_entries = params.shape[0] * lax.axis_size("dp") * lax.axis_size("fsdp")
    flat = lax.all_gather(params.astype(BF), ("dp", "fsdp"), axis=0, tiled=True)
    output, grad_images, grads = device_step(
        images.transpose(0, 2, 1), cotangent.transpose(0, 2, 1), kv_sides, arrange_weights(flat, width, hidden)
    )
    flat_grads = jnp.concatenate([piece.reshape(-1) for piece in gradient_pieces(grads, width, hidden)])
    flat_grads = jnp.concatenate([flat_grads, jnp.zeros((total_entries - flat_grads.shape[0],), F32)])
    shard = lax.psum_scatter(flat_grads, ("dp", "fsdp"), scatter_dimension=0, tiled=True)
    grad_norm = jnp.sqrt(lax.psum(jnp.sum(shard * shard), ("dp", "fsdp")))
    clipped = shard * jnp.minimum(1.0, CLIP_NORM / (grad_norm + 1e-06))
    new_first = BETA_FIRST * first_moment + (1.0 - BETA_FIRST) * clipped
    new_second = BETA_SECOND * second_moment + (1.0 - BETA_SECOND) * clipped * clipped
    first_hat = new_first / (1.0 - BETA_FIRST**STEP)
    second_hat = new_second / (1.0 - BETA_SECOND**STEP)
    new_params = params - RATE * (first_hat / (jnp.sqrt(second_hat) + EPSILON) + DECAY * params)
    return (
        output.transpose(0, 2, 1),
        grad_images.transpose(0, 2, 1),
        grad_norm,
        new_first,
        new_second,
        new_params,
    )


def solution(mesh):
    data = P(("dp", "fsdp"), None, None)
    flat = P(("dp", "fsdp"))
    return jax.shard_map(
        local,
        mesh=mesh,
        in_specs=(data, data, flat, flat, flat, flat),
        out_specs=(data, data, P(), flat, flat, flat),
        check_vma=False,
    )
```

time: 1180 us -> 685 us (0.58)
  other arithmetic: 382 us -> 35.7 us
  matrix products: 303 us -> 0 us
  Pallas kernels: 0 us -> 236 us
  local copies, waits for them, and re-layouts: 205 us -> 114 us
    dot_general x32 -> x0, matrix products: 303 us -> none  [the longest x6 68.2 us: project_back(): jnp.einsum('...e,de->...d', grad, weight, preferred_element_type=jnp.floa...]
    pallas_call x0 -> x3, Pallas kernels: none -> 236 us  [the longest x1 115 us: feed_forward(): pl.pallas_call(feed_forward_kernel, grid=(n, hidden // block), in_specs=[...]
    reduce_sum x13 -> x5, other arithmetic: 183 us -> 4.14 us  [the longest x1 1.66 us: local(): grad_norm = jnp.sqrt(lax.psum(jnp.sum(shard * shard), ('dp', 'fsdp')))]
    convert_element_type x13 -> x4, other arithmetic: 165 us -> 2.87 us  [the longest x1 0.95 us: local(): flat = lax.all_gather(params.astype(BF), ('dp', 'fsdp'), axis=0, tiled=True)]
    reshape x9 -> x7, local copies, waits for them, and re-layouts: 30.5 us -> 10 us  [local(): piece.reshape(-1)]
    dynamic_slice x16 -> x0, local copies, waits for them, and re-layouts: 17.3 us -> none  [local(): lax.map(attend_forward, (queries, keys, values, key_mask))]
    while x40 -> x0, local copies, waits for them, and re-layouts: 15.5 us -> none
    concatenate x1, local copies, waits for them, and re-layouts: 72.5 us -> 59.5 us  [local(): jnp.concatenate([flat_grads, jnp.zeros((total_entries - flat_grads.shape[...]
  transfers between devices with their start and end apart: 2 -> 2, of which waited for: 2 -> 2; matrix products, arithmetic and copies ran while one was open for 1% -> 0% of each run, Pallas kernels for 0% -> 0%
where the time goes in v1:
time: 685 us; the launch traced here: 675 us
  Pallas kernels  236 us (34%)
  waiting for transfers between devices  232 us (34%)
  local copies, waits for them, and re-layouts  114 us (17%)
  blocking collectives  40.3 us (6%)
  other arithmetic  35.7 us (5%)
  between operations  16.7 us (2%)
    unnamed x3, waiting for transfers between devices  159 us
    pallas_call x1, Pallas kernels, feed_forward(): pl.pallas_call(feed_forward_kernel, grid=(n, hidden // block), in_specs=[...  115 us
    pallas_call x1, Pallas kernels, attention_backward(): pl.pallas_call(attention_backward_kernel, grid_spec=pltpu.PrefetchScalarG...  80.1 us
    all_gather x1, waiting for transfers between devices, local(): flat = lax.all_gather(params.astype(BF), ('dp', 'fsdp'), axis=0, tiled=True)  73.5 us
    concatenate x1, local copies, waits for them, and re-layouts, local(): jnp.concatenate([flat_grads, jnp.zeros((total_entries - flat_grads.shape[...  59.5 us
    pallas_call x1, Pallas kernels, attention_forward(): pl.pallas_call(attention_forward_kernel, grid_spec=pltpu.PrefetchScalarGr...  40.7 us
    psum x1, blocking collectives, local(): grad_norm = jnp.sqrt(lax.psum(jnp.sum(shard * shard), ('dp', 'fsdp')))  40.3 us
    all_gather x1, other arithmetic, local(): flat = lax.all_gather(params.astype(BF), ('dp', 'fsdp'), axis=0, tiled=True)  21.5 us
  transfers between devices with their start and end apart: 2, of which 2 were waited for; matrix products, arithmetic and copies ran while one was open for 0% of the time, Pallas kernels for 0%

profile of v1, /device:TPU:0, one launch (start us, length us, event | category | flops | bytes accessed | tf_op | source)
XLA Modules:
  0.0 675.1 jit_solution(11603085692731938961)
XLA Ops:
  11.6 73.5 %all-gather.3.cloned.1.call-done = bf16[32,1,51840]{2,1,0:T(2,128)(2,1)} async-done(((bf16[1,1,51840]{2,1,0:T(2,128)(2,1)}), bf16[32,1,51840]{2,1,0:T(2,128)(2,1)}) %all-gather.3.cloned.1.call-update) | async-done | bytes 3317776 | tf_op jit(solution)/shard_map/all_gather | solution.py:684
  85.1 21.5 %reduce = bf16[32,51840]{1,0:T(8,128)(2,1)} reduce(bf16[32,1,51840]{2,1,0:T(2,128)(2,1)} %all-gather.3.cloned.1.call-done, bf16[]{:T(256)} %constant.62), dimensions={1}, to_apply=%all-gather.reduce_sub_computation | reduce | bytes 6635522 | tf_op jit(solution)/shard_map/all_gather | solution.py:684
  106.6 6.2 reshape.225
  115.2 1.9 fusion.10
  122.4 1.3 slice.164
  125.3 1.4 broadcast_in_dim.49
  131.4 1.8 reshape_reshape.3.wr
  135.2 1.3 copy.36
  136.6 1.8 maximum_maximum_fusion.2.wqt
  143.5 40.7 %attention_forward.1 = (bf16[2,336,2304]{2,1,0:T(8,128)(2,1)}, bf16[2,4,576,320]{3,2,1,0:T(8,128)(2,1)}, f32[2,576,320]{2,1,0:T(8,128)}, bf16[2,576,384]{2,1,0:T...) custom-call(s32[2]{0:T(128)} %sides.3, ...), custom_call_target="tpu_custom_call" | custom-call | tf_op jit(solution)/shard_map/attention_forward/pallas_call | solution.py:201
  184.2 115.2 %feed_forward.1 = (bf16[2,320,2304]{2,1,0:T(8,128)(2,1)}, f32[2,320,2304]{2,1,0:T(8,128)}, f32[336,1280]{1,0:T(8,128)}, f32[320,1280]{1,0:T(8,128)}, f32[80,1280]{1,0:T(8,128)}, /*index=5*/f32[320,128]{1,0:T(8,128)}) custom-call(bf16[2,336,2304]{2,1,0:T(8,128)(2,1)} %get-tuple-element.27.post, bf16[2,320,2304]{2,1,0:T(8,128)(2,1)} %bitcast.19, ...), custom_call_target="tpu_custom_call" | custom-call | tf_op jit(solution)/shard_map/feed_forward/pallas_call | solution.py:370
  299.4 80.1 %attention_backward.1 = (f32[2,320,2304]{2,1,0:T(8,128)}, f32[336,320]{1,0:T(8,128)}, f32[336,320]{1,0:T(8,128)}, f32[640,384]{1,0:T(8,128)}, f32[4,320,320]{2,1...) custom-call(s32[2]{0:T(128)} %sides.3, bf16[2,320,2304]{2,1,0:T(8,128)(2,1)} %bitcast.18, ...), custom_call_target="tpu_custom_call" | custom-call | tf_op jit(solution)/shard_map/attention_backward/pallas_call | solution.py:523
  383.3 1.3 slice.188
  384.6 1.9 copy.38
  386.5 2.2 reshape.216
  389.9 1.5 copy.39
  394.9 1.8 copy.40
  396.7 2.2 reshape.223
  398.9 2.6 reshape.220
  403.8 59.5 %concatenate.27 = f32[1658880]{0:T(1024)} concatenate(f32[320]{0:T(512)S(1)} %get-tuple-element.51, f32[320]{0:T(512)S(1)} %get-tuple-element.50, f32[102400]{0:T(1024)} %reshape.215, f32[320]{0:T(512)S(1)} %slice_reduce_fusion.11, f32[409600]{0:T(1024)S(1)} %copy-done, f32[320]{0:T(512)S(1)} %get-tuple-element.54, f32[320]{0:T(512)S(1)} %get-tuple-element.53, ...), dimensions={0} | concatenate | bytes 13271040 | tf_op jit(solution)/shard_map/concatenate | solution.py:689
  463.3 158.7 %all-reduce.3.cloned.1.call-done = f32[1658880]{0:T(1024)} async-done(((f32[1658880]{0:T(1024)}), f32[1658880]{0:T(1024)}) %all-reduce.3.cloned.1.call-update) | async-done | bytes 6635536
  622.0 1.7 multiply_reduce_fusion
  623.7 40.3 %psum.7 = f32[]{:T(128)} all-reduce(f32[]{:T(128)} %multiply_reduce_fusion), channel_id=1, replica_groups=mesh['dp'=4,'fsdp'=8] {'dp','fsdp'}, use_global_device_ids=true, to_apply=%region_6.7 | all-reduce | flops 1 | bytes 8 | tf_op jit(solution)/shard_map/psum | solution.py:691
  664.7 2.0 multiply_subtract_fusion
  (117 shorter events, 35.9 us)
Async XLA Ops:
  7.2 78.0 %all-gather.3.cloned.1.call-start = ((), (), s32[]{:S(2)}) async-start(), calls=%async_computation | async-start | bytes 6842880 | tf_op jit(solution)/shard_map/all_gather | solution.py:684
  9.0 613.0 %all-reduce.3.cloned.1.call-start = ((), (), s32[]{:S(2)}) async-start(), calls=%async_computation.1 | async-start | bytes 13271040
  117.1 14.2 %copy-start.3 = (bf16[409600]{0:T(1024)(128)(2,1)S(1)}, bf16[409600]{0:T(1024)(128)(2,1)}, u32[]{:S(2)}) copy-start(bf16[409600]{0:T(1024)(128)(2,1)} %get-tuple-element.62) | copy-start | bytes 2457604
  123.7 9.6 %copy-start.4 = (bf16[409600]{0:T(1024)(128)(2,1)S(1)}, bf16[409600]{0:T(1024)(128)(2,1)}, u32[]{:S(2)}) copy-start(bf16[409600]{0:T(1024)(128)(2,1)} %get-tuple-element.61) | copy-start | bytes 2457604
  126.7 7.6 %copy-start.2 = (bf16[409600]{0:T(1024)(128)(2,1)S(1)}, bf16[409600]{0:T(1024)(128)(2,1)}, u32[]{:S(2)}) copy-start(bf16[409600]{0:T(1024)(128)(2,1)} %get-tuple-element.60) | copy-start | bytes 2457604
  133.2 5.1 copy-start.12
  134.2 4.2 copy-start.9
  134.2 4.2 copy-start.17
  134.3 6.7 copy-start.23
  134.3 6.7 copy-start.24
  134.3 6.7 copy-start.25
  134.3 7.3 %copy-start.18 = (bf16[1,320]{1,0:T(2,128)(2,1)S(1)}, bf16[1,320]{1,0:T(2,128)(2,1)}, u32[]{:S(2)}) copy-start(bf16[1,320]{1,0:T(2,128)(2,1)} %stack.30) | copy-start | bytes 1924
  134.3 7.3 %copy-start.19 = (bf16[1,320]{1,0:T(2,128)(2,1)S(1)}, bf16[1,320]{1,0:T(2,128)(2,1)}, u32[]{:S(2)}) copy-start(bf16[1,320]{1,0:T(2,128)(2,1)} %stack.31) | copy-start | bytes 1924
  134.3 7.3 %copy-start.20 = (bf16[1,320]{1,0:T(2,128)(2,1)S(1)}, bf16[1,320]{1,0:T(2,128)(2,1)}, u32[]{:S(2)}) copy-start(bf16[1,320]{1,0:T(2,128)(2,1)} %stack.32) | copy-start | bytes 1924
  134.3 7.3 %copy-start.21 = (bf16[1,320]{1,0:T(2,128)(2,1)S(1)}, bf16[1,320]{1,0:T(2,128)(2,1)}, u32[]{:S(2)}) copy-start(bf16[1,320]{1,0:T(2,128)(2,1)} %stack.33) | copy-start | bytes 1924
  134.4 7.3 %copy-start.22 = (bf16[1,320]{1,0:T(2,128)(2,1)S(1)}, bf16[1,320]{1,0:T(2,128)(2,1)}, u32[]{:S(2)}) copy-start(bf16[1,320]{1,0:T(2,128)(2,1)} %stack.34) | copy-start | bytes 1924
  135.2 7.6 %copy-start.15 = (f32[2,2304]{1,0:T(2,128)S(1)}, f32[2,2304]{1,0:T(2,128)}, u32[]{:S(2)}) copy-start(f32[2,2304]{1,0:T(2,128)} %and_convert_fusion) | copy-start | bytes 55300
  388.7 5.8 copy-start.11
  389.9 4.9 copy-start.16
  398.9 4.9 copy-start
  398.9 4.9 copy-start.1
  463.3 201.4 %copy-start.10 = (f32[51840]{0:T(1024)S(1)}, f32[51840]{0:T(1024)}, u32[]{:S(2)}) copy-start(f32[51840]{0:T(1024)} %param.10) | copy-start | bytes 622084
  463.3 201.4 %copy-start.13 = (f32[51840]{0:T(1024)S(1)}, f32[51840]{0:T(1024)}, u32[]{:S(2)}) copy-start(f32[51840]{0:T(1024)} %param.12) | copy-start | bytes 622084
  463.3 201.4 %copy-start.14 = (f32[51840]{0:T(1024)S(1)}, f32[51840]{0:T(1024)}, u32[]{:S(2)}) copy-start(f32[51840]{0:T(1024)} %param.11) | copy-start | bytes 622084
  (4 other events, 11.0 us)
Sparse Core Ops, SparseCore 0:
  11.5 73.5 all-gather.2
  463.4 158.5 all-reduce.2

commit v2 on v1

--- a/solution.py
+++ b/solution.py
@@ -547,85 +547,434 @@
         name="attention_backward",
     )(sides, *inputs, middle, grad_post, *weights)
 
+MESH = pl.DeviceIdType.MESH
+
+
+class Place:
+    def __init__(self):
+        self.dp = lax.axis_index("dp")
+        fsdp = lax.axis_index("fsdp")
+        self.y, self.x = self.dp // 2, self.dp % 2
+        self.z, self.core = fsdp // 2, fsdp % 2
+        self.beside_x = (self.dp + 1 - 2 * self.x, fsdp)
+        self.beside_y = (self.dp + 2 - 4 * self.y, fsdp)
+        self.beside_core = (self.dp, fsdp + 1 - 2 * self.core)
+
+    def up(self, k):
+        return (self.z + k) % 4
+
+    def along_z(self, k):
+        return (self.dp, self.up(k) * 2 + self.core)
+
+    def partners(self):
+        return [self.beside_core, self.beside_x, self.beside_y] + [self.along_z(k) for k in (1, 2, 3)]
+
+    def greet(self):
+        barrier = pltpu.get_barrier_semaphore()
+        partners = self.partners()
+        for device in partners:
+            pl.semaphore_signal(barrier, inc=1, device_id=device, device_id_type=MESH)
+        pl.semaphore_wait(barrier, len(partners))
+
+
+class Sender:
+    def __init__(self, send, recv):
+        self.send, self.recv, self.started = send, recv, []
+
+    def __call__(self, source, target, device):
+        k = len(self.started)
+        copy = pltpu.make_async_remote_copy(
+            src_ref=source,
+            dst_ref=target,
+            send_sem=self.send.at[k],
+            recv_sem=self.recv.at[k],
+            device_id=device,
+            device_id_type=MESH,
+        )
+        copy.start()
+        self.started.append(copy)
+        return copy
+
+    def finish(self):
+        for copy in self.started:
+            copy.wait_send()
+
+
+def gather_kernel(own, out, own_sem, send_sem, recv_sem):
+    me = Place()
+    half = own.shape[0] // 2
+    first, second = pl.ds(0, half), pl.ds(half, half)
+    send = Sender(send_sem, recv_sem)
+    copy = pltpu.make_async_copy(own, out.at[me.core, me.dp, me.z], own_sem)
+    copy.start()
+    me.greet()
+    slot = out.at[me.core, me.dp, me.z]
+    z_copies = [send(own, slot, me.along_z(k)) for k in (1, 2, 3)]
+    x_copies = [send(own, slot, me.beside_x)]
+    y_copies = [send(own, slot, me.beside_y)]
+    core_copies = [send(own, slot, me.beside_core)]
+    half_copies = []
+
+    def forward(k):
+        z = (me.z + 4 - k) % 4
+        x_copies[k].wait_recv()
+        dp = me.beside_x[0]
+        slot = out.at[me.core, dp, z]
+        half_copies.append(send(slot.at[first], slot.at[first], me.beside_y))
+        core_copies.append(send(slot, slot, me.beside_core))
+        y_copies[k].wait_recv()
+        dp = me.beside_y[0]
+        slot = out.at[me.core, dp, z]
+        half_copies.append(send(slot.at[second], slot.at[second], me.beside_x))
+        core_copies.append(send(slot, slot, me.beside_core))
+
+    forward(0)
+    for k in (1, 2, 3):
+        z_copies[k - 1].wait_recv()
+        slot = out.at[me.core, me.dp, (me.z + 4 - k) % 4]
+        x_copies.append(send(slot, slot, me.beside_x))
+        y_copies.append(send(slot, slot, me.beside_y))
+        core_copies.append(send(slot, slot, me.beside_core))
+        forward(k)
+    for k in range(4):
+        half_copies[2 * k].wait_recv()
+        half_copies[2 * k + 1].wait_recv()
+        slot = out.at[me.core, 3 - me.dp, (me.z + 4 - k) % 4]
+        core_copies.append(send(slot, slot, me.beside_core))
+    for copied in core_copies:
+        copied.wait_recv()
+    copy.wait()
+    send.finish()
+
+
+def gather_slots(own):
+    count = 35
+    return pl.pallas_call(
+        gather_kernel,
+        out_shape=jax.ShapeDtypeStruct((2, 4, 4) + own.shape, own.dtype),
+        in_specs=[pl.BlockSpec(memory_space=pltpu.VMEM)],
+        out_specs=pl.BlockSpec(memory_space=pltpu.VMEM),
+        scratch_shapes=[
+            pltpu.SemaphoreType.DMA(()),
+            pltpu.SemaphoreType.DMA((count,)),
+            pltpu.SemaphoreType.DMA((count,)),
+        ],
+        compiler_params=pltpu.CompilerParams(
+            collective_id=0, has_side_effects=True, vmem_limit_bytes=VMEM_BYTES
+        ),
+        name="gather_weights",
+    )(own)
+
+
+def reduce_kernel(grads, shard, squares, core_in, y_in, x_in, x_last, y_last, z_in, small, send_sem, recv_sem):
+    me = Place()
+    rows = grads.shape[3]
+    half = rows // 2
+    first, second = pl.ds(0, half), pl.ds(half, half)
+    send = Sender(send_sem, recv_sem)
+    other_x, other_y = 1 - me.x, 1 - me.y
+    me.greet()
+    order = [2 * other_y + other_x, 2 * other_y + me.x, 2 * me.y + other_x, me.dp]
+    core_copies = [send(grads.at[1 - me.core, dp], core_in.at[dp], me.beside_core) for dp in order]
+
+    def add(dp):
+        for z in range(4):
+            core_in[dp, z] = (core_in[dp, z].astype(F32) + grads[me.core, dp, z].astype(F32)).astype(BF)
+
+    core_copies[0].wait_recv()
+    add(order[0])
+    y_copies = [send(core_in.at[order[0], :, first], y_in.at[0], me.beside_y)]
+    x_copies = [send(core_in.at[order[0], :, second], x_in.at[0], me.beside_x)]
+    core_copies[1].wait_recv()
+    add(order[1])
+    y_copies.append(send(core_in.at[order[1], :, first], y_in.at[1], me.beside_y))
+    core_copies[2].wait_recv()
+    add(order[2])
+    x_copies.append(send(core_in.at[order[2], :, second], x_in.at[1], me.beside_x))
+    core_copies[3].wait_recv()
+    add(order[3])
+    y_copies[0].wait_recv()
+    x_copies[0].wait_recv()
+    last = []
+    for k in (0, 1, 2, 3):
+        z = (me.z + k) % 4
+        y_in[0, z] = (y_in[0, z].astype(F32) + core_in[order[2], z, first].astype(F32)).astype(BF)
+        last.append(send(y_in.at[0, z], x_last.at[z], me.beside_x))
+        x_in[0, z] = (x_in[0, z].astype(F32) + core_in[order[1], z, second].astype(F32)).astype(BF)
+        last.append(send(x_in.at[0, z], y_last.at[z], me.beside_y))
+    y_copies[1].wait_recv()
+    x_copies[1].wait_recv()
+    z_copies = []
+    for k in (1, 2, 3, 0):
+        z = (me.z + k) % 4
+        last[2 * k].wait_recv()
+        last[2 * k + 1].wait_recv()
+        low = y_in[1, z].astype(F32) + core_in[me.dp, z, first].astype(F32) + x_last[z].astype(F32)
+        high = x_in[1, z].astype(F32) + core_in[me.dp, z, second].astype(F32) + y_last[z].astype(F32)
+        if k == 0:
+            shard[first, :] = low
+            shard[second, :] = high
+        else:
+            z_in[k - 1, first] = low.astype(BF)
+            z_in[k - 1, second] = high.astype(BF)
+            z_copies.append(send(z_in.at[k - 1], z_in.at[k + 2], me.along_z(k)))
+    for k in (0, 1, 2):
+        z_copies[k].wait_recv()
+        shard[...] += z_in[k + 3].astype(F32)
+    total = shard[0:8, :] * shard[0:8, :]
+    for k in range(1, rows // 8):
+        part = shard[8 * k : 8 * k + 8, :]
+        total = total + part * part
+    small[0] = total
+    for k, device in enumerate((me.beside_core, me.beside_x, me.beside_y)):
+        copied = send(small.at[k], small.at[4 + k], device)
+        copied.wait_recv()
+        small[k + 1] = small[k] + small[4 + k]
+    copies = [send(small.at[3], small.at[8 + me.z], me.along_z(k)) for k in (1, 2, 3)]
+    small[8 + me.z] = small[3]
+    for copied in copies:
+        copied.wait_recv()
+    squares[...] = ((small[8] + small[9]) + small[10]) + small[11]
+    send.finish()
+
+
+def reduce_slots(grads):
+    rows = grads.shape[3]
+    half = rows // 2
+    count = 4 + 4 + 8 + 3 + 6
+    return pl.pallas_call(
+        reduce_kernel,
+        out_shape=[jax.ShapeDtypeStruct((rows, 128), F32), jax.ShapeDtypeStruct((8, 128), F32)],
+        in_specs=[pl.BlockSpec(memory_space=pltpu.VMEM)],
+        out_specs=[pl.BlockSpec(memory_space=pltpu.VMEM)] * 2,
+        scratch_shapes=[
+            pltpu.VMEM((4, 4, rows, 128), BF),
+            pltpu.VMEM((2, 4, half, 128), BF),
+            pltpu.VMEM((2, 4, half, 128), BF),
+            pltpu.VMEM((4, half, 128), BF),
+            pltpu.VMEM((4, half, 128), BF),
+            pltpu.VMEM((6, rows, 128), BF),
+            pltpu.VMEM((12, 8, 128), F32),
+            pltpu.SemaphoreType.DMA((count,)),
+            pltpu.SemaphoreType.DMA((count,)),
+        ],
+        compiler_params=pltpu.CompilerParams(
+            collective_id=1, has_side_effects=True, vmem_limit_bytes=VMEM_BYTES
+        ),
+        name="reduce_gradients",
+    )(grads)
+
 
 def layout_shapes(model_width, hidden_width):
     return [
-        (model_width,),
-        (model_width,),
-        (model_width, model_width),
-        (model_width,),
-        (4 * model_width, model_width),
-        (model_width,),
-        (model_width,),
-        (model_width,),
-        (model_width, 2 * model_width),
-        (model_width,),
-        (model_width, model_width),
-        (model_width,),
-        (model_width,),
-        (model_width,),
-        (model_width, hidden_width),
-        (hidden_width,),
-        (9, hidden_width),
-        (hidden_width,),
-        (hidden_width, model_width),
-        (model_width,),
+        ("pre_gain", (model_width,)),
+        ("pre_shift", (model_width,)),
+        ("query_weight", (model_width, model_width)),
+        ("query_bias", (model_width,)),
+        ("reduce_weight", (4 * model_width, model_width)),
+        ("reduce_bias", (model_width,)),
+        ("reduce_gain", (model_width,)),
+        ("reduce_shift", (model_width,)),
+        ("pair_weight", (model_width, 2 * model_width)),
+        ("value_bias", (model_width,)),
+        ("output_weight", (model_width, model_width)),
+        ("output_bias", (model_width,)),
+        ("mlp_gain", (model_width,)),
+        ("mlp_shift", (model_width,)),
+        ("expand_weight", (model_width, hidden_width)),
+        ("expand_bias", (hidden_width,)),
+        ("spatial_weight", (9, hidden_width)),
+        ("spatial_bias", (hidden_width,)),
+        ("shrink_weight", (hidden_width, model_width)),
+        ("shrink_bias", (model_width,)),
     ]
 
 
-def unpack_params(flat, model_width, hidden_width):
-    pieces = []
-    offset = 0
-    for shape in layout_shapes(model_width, hidden_width):
-        count = math.prod(shape)
-        pieces.append(flat[offset : offset + count].reshape(shape))
-        offset += count
-    return pieces
-
-
-def arrange_weights(flat, width, hidden):
-    (
-        pre_gain,
-        pre_shift,
-        query_weight,
-        query_bias,
-        reduce_weight,
-        reduce_bias,
-        reduce_gain,
-        reduce_shift,
-        pair_weight,
-        value_bias,
-        output_weight,
-        output_bias,
-        mlp_gain,
-        mlp_shift,
-        expand_weight,
-        expand_bias,
-        spatial_weight,
-        spatial_bias,
-        shrink_weight,
-        shrink_bias,
-    ) = unpack_params(flat, width, hidden)
-
-    def with_bias(weight, bias, extra):
-        return jnp.concatenate([weight.T, bias[:, None], jnp.zeros((width, extra - 1), BF)], axis=1)
-
-    columns = jnp.stack([pre_gain, pre_shift, mlp_gain, mlp_shift, shrink_bias]).astype(F32)
-    return dict(
-        vec=jnp.broadcast_to(columns[:, :, None], (5, width, 128)),
-        rows=jnp.stack([reduce_bias, reduce_gain, reduce_shift]).astype(F32),
-        wq=query_weight,
-        wqt=with_bias(query_weight, query_bias, EXT),
-        wr=reduce_weight.reshape(4, width, width),
-        wk=pair_weight[:, :width],
-        wv=pair_weight[:, width:],
-        wvt=with_bias(pair_weight[:, width:], value_bias, 64),
-        wo=output_weight,
-        wot=with_bias(output_weight, output_bias, EXT),
-        we=jnp.concatenate([expand_weight, expand_bias[None], jnp.zeros((63, hidden), BF)]),
-        wst=shrink_weight.T,
-        taps=jnp.concatenate([spatial_weight, spatial_bias[None]]).astype(F32),
+def row_bases(width, hidden):
+    bases = {}
+    row = 0
+    for name, shape in layout_shapes(width, hidden):
+        bases[name] = row
+        row += math.prod(shape) // width
+    return bases, row
+
+
+SPAN = 96
+
+
+def unpack_kernel(
+    order, slot_rows, bases,
+    slots, vec, rows, wq, wqt, wr, wk, wv, wvt, wo, wot, we, wst, taps,
+    flat, wide,
+):
+    width = wq.shape[0]
+    hidden = wst.shape[1]
+    for slot, place in enumerate(order):
+        flat[pl.ds(slot * slot_rows, slots.shape[1]), :] = slots[place].astype(F32)
+    low = lax.broadcasted_iota(jnp.int32, (SPAN, 128), 1) < 64
+
+    def regroup(t, _):
+        part = [flat[pl.ds(t * (5 * SPAN) + k, SPAN, stride=5), :] for k in range(5)]
+        turned = [pltpu.roll(part[k], 64, 1) for k in (2, 3, 4)]
+        even = pl.ds(t * (2 * SPAN), SPAN, stride=2)
+        odd = pl.ds(t * (2 * SPAN) + 1, SPAN, stride=2)
+        for k in range(3):
+            wide[k, even, :] = part[k]
+        wide[0, odd, :] = jnp.where(low, turned[0], turned[1])
+        wide[1, odd, :] = jnp.where(low, turned[1], turned[2])
+        wide[2, odd, :] = turned[2]
+        return 0
+
+    lax.fori_loop(0, wide.shape[1] // (2 * SPAN), regroup, 0)
+
+    def take(base, count, stride=1):
+        at = pl.ds(base, count, stride=stride) if stride > 1 else pl.ds(base, count)
+        return jnp.concatenate([wide[0, at, :], wide[1, at, :], wide[2, at, :][:, 0 : width - 256]], axis=1)
+
+    def take_hidden(base, count):
+        return jnp.concatenate([take(base + q, count, hidden // width) for q in range(hidden // width)], axis=1)
+
+    def bordered(weight, bias, extra):
+        index = lax.broadcasted_iota(jnp.int32, (extra, weight.shape[1]), 0)
+        return jnp.concatenate([weight, jnp.where(index == 0, bias, 0.0)], axis=0)
+
+    names = ("pre_gain", "pre_shift", "mlp_gain", "mlp_shift", "shrink_bias")
+    for k, name in enumerate(names):
+        vec[k] = jnp.broadcast_to(take(bases[name], 1), (128, width)).T
+    for k, name in enumerate(("reduce_bias", "reduce_gain", "reduce_shift")):
+        rows[k : k + 1, :] = take(bases[name], 1)
+    query = take(bases["query_weight"], width)
+    wq[...] = query.astype(BF)
+    wqt[...] = bordered(query, take(bases["query_bias"], 1), EXT).T.astype(BF)
+    for p in range(4):
+        wr[p] = take(bases["reduce_weight"] + p * width, width).astype(BF)
+    wk[...] = take(bases["pair_weight"], width, 2).astype(BF)
+    value = take(bases["pair_weight"] + 1, width, 2)
+    wv[...] = value.astype(BF)
+    wvt[...] = bordered(value, take(bases["value_bias"], 1), 64).T.astype(BF)
+    out = take(bases["output_weight"], width)
+    wo[...] = out.astype(BF)
+    wot[...] = bordered(out, take(bases["output_bias"], 1), EXT).T.astype(BF)
+    we[0:width, :] = take_hidden(bases["expand_weight"], width).astype(BF)
+    we[width : width + 64, :] = first_row(take_hidden(bases["expand_bias"], 1), 64).astype(BF)
+    taps[0:9, :] = take_hidden(bases["spatial_weight"], 9)
+    taps[9:10, :] = take_hidden(bases["spatial_bias"], 1)
+    for k in range(hidden // 128):
+        wst[:, 128 * k : 128 * k + 128] = take(bases["shrink_weight"] + 128 * k, 128).T.astype(BF)
+
+
+def wide_rows(count):
+    return -(-count // (2 * SPAN)) * 2 * SPAN
+
+
+def unpack_weights(slots, order, slot_rows, width):
+    hidden = 4 * width
+    bases, count = row_bases(width, hidden)
+    shape = jax.ShapeDtypeStruct
+    outs = dict(
+        vec=shape((5, width, 128), F32),
+        rows=shape((3, width), F32),
+        wq=shape((width, width), BF),
+        wqt=shape((width, width + EXT), BF),
+        wr=shape((4, width, width), BF),
+        wk=shape((width, width), BF),
+        wv=shape((width, width), BF),
+        wvt=shape((width, width + 64), BF),
+        wo=shape((width, width), BF),
+        wot=shape((width, width + EXT), BF),
+        we=shape((width + 64, hidden), BF),
+        wst=shape((width, hidden), BF),
+        taps=shape((10, hidden), F32),
     )
+    flat_rows = max(len(order) * slot_rows, wide_rows(count) * width // 128) + slots.shape[1]
+    values = pl.pallas_call(
+        partial(unpack_kernel, order, slot_rows, bases),
+        out_shape=list(outs.values()),
+        in_specs=[pl.BlockSpec(memory_space=pltpu.VMEM)],
+        out_specs=[pl.BlockSpec(memory_space=pltpu.VMEM)] * len(outs),
+        scratch_shapes=[pltpu.VMEM((flat_rows, 128), F32), pltpu.VMEM((3, wide_rows(count), 128), F32)],
+        compiler_params=pltpu.CompilerParams(vmem_limit_bytes=VMEM_BYTES),
+        name="unpack_weights",
+    )(slots)
+    return dict(zip(outs, values, strict=True))
+
+
+def pack_kernel(
+    order, slot_rows, bases,
+    gwe, gwst, gtaps, gbias, gwo, gwq, gpair, gwr, gcols, grows, slots,
+    flat, wide,
+):
+    width = gwst.shape[0]
+    hidden = gwst.shape[1]
+    used = bases["shrink_bias"] + 1
+    for k in range(3):
+        wide[k, pl.ds(used, wide.shape[1] - used), :] = jnp.zeros((wide.shape[1] - used, 128), F32)
+    done = wide.shape[1] * width // 128
+    flat[done:, :] = jnp.zeros((flat.shape[0] - done, 128), F32)
+
+    def put(base, value, stride=1):
+        count = value.shape[0]
+        at = pl.ds(base, count, stride=stride) if stride > 1 else pl.ds(base, count)
+        wide[0, at, :] = value[:, 0:128]
+        wide[1, at, :] = value[:, 128:256]
+        wide[2, at, 0 : width - 256] = value[:, 256:width]
+
+    for k, name in enumerate(("pre_gain", "pre_shift", "mlp_gain", "mlp_shift")):
+        put(bases[name], jnp.sum(gcols[k].T, axis=0, keepdims=True))
+    put(bases["shrink_bias"], jnp.sum(gbias[...].T, axis=0, keepdims=True))
+    for k, name in enumerate(("reduce_bias", "reduce_gain", "reduce_shift")):
+        put(bases[name], jnp.sum(grows[8 * k : 8 * k + 8, :], axis=0, keepdims=True))
+    put(bases["query_weight"], gwq[0 : width + 1, :])
+    for p in range(4):
+        put(bases["reduce_weight"] + p * width, gwr[p].T)
+    put(bases["pair_weight"], gpair[0:width, :].T[0:width], 2)
+    value = gpair[width : 2 * width, :].T
+    put(bases["pair_weight"] + 1, value[0:width], 2)
+    put(bases["value_bias"], value[width : width + 1])
+    put(bases["output_weight"], gwo[0 : width + 1, :])
+    sums = jnp.concatenate(
+        [jnp.sum(gtaps[8 * k : 8 * k + 8, :], axis=0, keepdims=True) for k in range(10)], axis=0
+    )
+    for q in range(hidden // width):
+        put(bases["expand_weight"] + q, gwe[0 : width + 1, q * width : (q + 1) * width], hidden // width)
+        put(bases["spatial_weight"] + q, sums[:, q * width : (q + 1) * width], hidden // width)
+    for k in range(hidden // 128):
+        put(bases["shrink_weight"] + 128 * k, gwst[:, 128 * k : 128 * k + 128].T)
+    low = lax.broadcasted_iota(jnp.int32, (SPAN, 128), 1) < 64
+
+    def regroup(t, _):
+        even = pl.ds(t * (2 * SPAN), SPAN, stride=2)
+        odd = pl.ds(t * (2 * SPAN) + 1, SPAN, stride=2)
+        turned = [pltpu.roll(wide[k, odd, :], 64, 1) for k in range(3)]
+        part = [
+            wide[0, even, :],
+            wide[1, even, :],
+            jnp.where(low, wide[2, even, :], turned[0]),
+            jnp.where(low, turned[0], turned[1]),
+            jnp.where(low, turned[1], turned[2]),
+        ]
+        for k in range(5):
+            flat[pl.ds(t * (5 * SPAN) + k, SPAN, stride=5), :] = part[k]
+        return 0
+
+    lax.fori_loop(0, wide.shape[1] // (2 * SPAN), regroup, 0)
+    inside = lax.broadcasted_iota(jnp.int32, slots.shape[1:], 0) < slot_rows
+    for slot, place in enumerate(order):
+        slots[place] = jnp.where(inside, flat[pl.ds(slot * slot_rows, slots.shape[1]), :], 0.0).astype(BF)
+
+
+def pack_gradients(grads, order, slot_rows, padded_rows, width):
+    bases, count = row_bases(width, 4 * width)
+    flat_rows = max(len(order) * slot_rows, wide_rows(count) * width // 128) + padded_rows
+    return pl.pallas_call(
+        partial(pack_kernel, order, slot_rows, bases),
+        out_shape=jax.ShapeDtypeStruct((len(order), padded_rows, 128), BF),
+        in_specs=[pl.BlockSpec(memory_space=pltpu.VMEM)] * len(grads),
+        out_specs=pl.BlockSpec(memory_space=pltpu.VMEM),
+        scratch_shapes=[pltpu.VMEM((flat_rows, 128), F32), pltpu.VMEM((3, wide_rows(count), 128), F32)],
+        compiler_params=pltpu.CompilerParams(vmem_limit_bytes=VMEM_BYTES),
+        name="pack_gradients",
+    )(*grads)
 
 
 def device_step(images, cotangent, kv_sides, w):
@@ -647,48 +996,32 @@
     return output, grad_images, (gwe, gwst, gtaps, gbias, gwo, gwq, gpair, gwr, gcols, grows)
 
 
-def gradient_pieces(grads, width, hidden):
-    gwe, gwst, gtaps, gbias, gwo, gwq, gpair, gwr, gcols, grows = grads
-    columns = gcols.sum(axis=2)
-    sums = grows.reshape(3, 8, width).sum(axis=1)
-    taps = gtaps.reshape(10, 8, hidden).sum(axis=1)
-    pair = gpair.T
-    return [
-        columns[0],
-        columns[1],
-        gwq[:width],
-        gwq[width],
-        gwr.transpose(0, 2, 1),
-        sums[0],
-        sums[1],
-        sums[2],
-        pair[:width],
-        pair[width, width:],
-        gwo[:width],
-        gwo[width],
-        columns[2],
-        columns[3],
-        gwe[:width],
-        gwe[width],
-        taps[:9],
-        taps[9],
-        gwst.T,
-        gbias.sum(axis=1),
-    ]
-
-
-def local(images, cotangent, kv_sides, params, first_moment, second_moment):
+def step(on_grid, images, cotangent, kv_sides, params, first_moment, second_moment):
     width = images.shape[2]
-    hidden = 4 * width
-    total_entries = params.shape[0] * lax.axis_size("dp") * lax.axis_size("fsdp")
-    flat = lax.all_gather(params.astype(BF), ("dp", "fsdp"), axis=0, tiled=True)
+    axes = ("dp", "fsdp")
+    outer, inner = lax.axis_size("dp"), lax.axis_size("fsdp")
+    slot_rows = params.shape[0] // 128
+    padded_rows = -(-slot_rows // 32) * 32
+    own = jnp.pad(params.reshape(slot_rows, 128).astype(BF), ((0, padded_rows - slot_rows), (0, 0)))
+    if on_grid:
+        order = [(s % 2) * 16 + s // 8 * 4 + s % 8 // 2 for s in range(32)]
+        slots = gather_slots(own).reshape(32, padded_rows, 128)
+    else:
+        order = list(range(outer * inner))
+        slots = lax.all_gather(own, axes)
+    weights = unpack_weights(slots, order, slot_rows, width)
     output, grad_images, grads = device_step(
-        images.transpose(0, 2, 1), cotangent.transpose(0, 2, 1), kv_sides, arrange_weights(flat, width, hidden)
+        images.transpose(0, 2, 1), cotangent.transpose(0, 2, 1), kv_sides, weights
     )
-    flat_grads = jnp.concatenate([piece.reshape(-1) for piece in gradient_pieces(grads, width, hidden)])
-    flat_grads = jnp.concatenate([flat_grads, jnp.zeros((total_entries - flat_grads.shape[0],), F32)])
-    shard = lax.psum_scatter(flat_grads, ("dp", "fsdp"), scatter_dimension=0, tiled=True)
-    grad_norm = jnp.sqrt(lax.psum(jnp.sum(shard * shard), ("dp", "fsdp")))
+    slots = pack_gradients(grads, order, slot_rows, padded_rows, width)
+    if on_grid:
+        shard, squares = reduce_slots(slots.reshape(2, 4, 4, padded_rows, 128))
+        squares = jnp.sum(squares)
+    else:
+        shard = lax.psum_scatter(slots.astype(F32), axes)
+        squares = lax.psum(jnp.sum(shard * shard), axes)
+    shard = shard[:slot_rows].reshape(-1)
+    grad_norm = jnp.sqrt(squares)
     clipped = shard * jnp.minimum(1.0, CLIP_NORM / (grad_norm + 1e-06))
     new_first = BETA_FIRST * first_moment + (1.0 - BETA_FIRST) * clipped
     new_second = BETA_SECOND * second_moment + (1.0 - BETA_SECOND) * clipped * clipped
@@ -708,8 +1041,9 @@
 def solution(mesh):
     data = P(("dp", "fsdp"), None, None)
     flat = P(("dp", "fsdp"))
+    on_grid = dict(mesh.shape) == {"dp": 4, "fsdp": 8}
     return jax.shard_map(
-        local,
+        partial(step, on_grid),
         mesh=mesh,
         in_specs=(data, data, flat, flat, flat, flat),
         out_specs=(data, data, P(), flat, flat, flat),

time: 685 us -> 341 us (0.50); the launches traced: 675 us -> 339 us
  waiting for transfers between devices: 232 us -> 0 us
  local copies, waits for them, and re-layouts: 114 us -> 1.34 us
  Pallas kernels: 236 us -> 330 us
  blocking collectives: 40.3 us -> 0 us
  other arithmetic: 35.7 us -> 4.84 us
  between operations: 16.7 us -> 2.8 us
    unnamed x3 -> x0, waiting for transfers between devices: 159 us -> none
    pallas_call x0 -> x4, Pallas kernels: none -> 93.9 us  [the longest x1 43.3 us: reduce_slots(): pl.pallas_call(reduce_kernel, out_shape=[jax.ShapeDtypeStruct((rows, 128)...]
    all_gather x1 -> x0, waiting for transfers between devices: 73.5 us -> none  [local(): flat = lax.all_gather(params.astype(BF), ('dp', 'fsdp'), axis=0, tiled=True)]
    concatenate x4 -> x0, local copies, waits for them, and re-layouts: 61.6 us -> none  [the longest x1 59.5 us: local(): jnp.concatenate([flat_grads, jnp.zeros((total_entries - flat_grads.shape[...]
    psum x1 -> x0, blocking collectives: 40.3 us -> none  [local(): grad_norm = jnp.sqrt(lax.psum(jnp.sum(shard * shard), ('dp', 'fsdp')))]
    all_gather x1 -> x0, other arithmetic: 21.5 us -> none  [local(): flat = lax.all_gather(params.astype(BF), ('dp', 'fsdp'), axis=0, tiled=True)]
    reshape x14 -> x0, local copies, waits for them, and re-layouts: 15.6 us -> none  [the longest x7 10 us: local(): piece.reshape(-1)]
    slice x19 -> x0, local copies, waits for them, and re-layouts: 14.2 us -> none  [the longest x7 5.59 us: unpack_params(): pieces.append(flat[offset:offset + count].reshape(shape))]
  transfers between devices with their start and end apart: 2 -> 0, of which waited for: 2 -> 0; matrix products, arithmetic and copies ran while one was open for 0% -> 0% of each run, Pallas kernels for 0% -> 0%
where the time goes in v2:
time: 341 us; the launch traced here: 339 us
  Pallas kernels  330 us (97%)
  other arithmetic  4.84 us (1%)
    pallas_call x1, Pallas kernels, feed_forward(): pl.pallas_call(feed_forward_kernel, grid=(n, hidden // block), in_specs=[...  115 us
    pallas_call x1, Pallas kernels, attention_backward(): pl.pallas_call(attention_backward_kernel, grid_spec=pltpu.PrefetchScalarG...  79.9 us
    pallas_call x1, Pallas kernels, reduce_slots(): pl.pallas_call(reduce_kernel, out_shape=[jax.ShapeDtypeStruct((rows, 128)...  43.3 us
    pallas_call x1, Pallas kernels, attention_forward(): pl.pallas_call(attention_forward_kernel, grid_spec=pltpu.PrefetchScalarGr...  40.6 us
    pallas_call x1, Pallas kernels, gather_slots(): pl.pallas_call(gather_kernel, out_shape=jax.ShapeDtypeStruct((2, 4, 4) +...  31.5 us
    pallas_call x1, Pallas kernels, pack_gradients(): pl.pallas_call(partial(pack_kernel, order, slot_rows, bases), out_shape=j...  10.6 us
    pallas_call x1, Pallas kernels, unpack_weights(): pl.pallas_call(partial(unpack_kernel, order, slot_rows, bases), out_shape...  8.46 us

profile of v2, /device:TPU:0, one launch (start us, length us, event | category | flops | bytes accessed | tf_op | source)
XLA Modules:
  0.0 338.6 jit_solution(17465335995714242670)
XLA Ops:
  0.6 0.7 broadcast_multiply_fusion
  1.3 0.1 and_convert_fusion
  1.4 0.9 convert_bitcast_fusion
  2.3 0.7 pad.4.own
  3.0 0.7 broadcast_in_dim.2.mask
  3.7 31.5 %gather_weights.1 = bf16[2,4,4,416,128]{4,3,2,1,0:T(8,128)(2,1)} custom-call(bf16[416,128]{1,0:T(8,128)(2,1)} %pad.4.own), custom_call_target="tpu_custom_call" | custom-call | tf_op jit(solution)/shard_map/gather_weights/pallas_call | solution.py:652
  35.2 8.5 %unpack_weights.1 = (f32[5,320,128]{2,1,0:T(8,128)}, f32[3,320]{1,0:T(4,128)}, bf16[320,320]{1,0:T(8,128)(2,1)}, bf16[320,336]{1,0:T(8,128)(2,1)}, bf16[4,320,32...) custom-call(bf16[32,416,128]{2,1,0:T(8,128)(2,1)} %bitcast.15), custom_call_target="tpu_custom_call" | custom-call | tf_op jit(solution)/shard_map/unpack_weights/pallas_call | solution.py:890
  43.6 40.6 %attention_forward.1 = (bf16[2,336,2304]{2,1,0:T(8,128)(2,1)}, bf16[2,4,576,320]{3,2,1,0:T(8,128)(2,1)}, f32[2,576,320]{2,1,0:T(8,128)}, bf16[2,576,384]{2,1,0:T...) custom-call(s32[2]{0:T(128)} %sides.3, ...), custom_call_target="tpu_custom_call" | custom-call | tf_op jit(solution)/shard_map/attention_forward/pallas_call | solution.py:201
  84.3 115.1 %feed_forward.1 = (bf16[2,320,2304]{2,1,0:T(8,128)(2,1)}, f32[2,320,2304]{2,1,0:T(8,128)}, f32[336,1280]{1,0:T(8,128)}, f32[320,1280]{1,0:T(8,128)}, f32[80,1280]{1,0:T(8,128)}, /*index=5*/f32[320,128]{1,0:T(8,128)}) custom-call(bf16[2,336,2304]{2,1,0:T(8,128)(2,1)} %get-tuple-element.49.post, bf16[2,320,2304]{2,1,0:T(8,128)(2,1)} %bitcast.19, ...), custom_call_target="tpu_custom_call" | custom-call | tf_op jit(solution)/shard_map/feed_forward/pallas_call | solution.py:370
  199.4 79.9 %attention_backward.1 = (f32[2,320,2304]{2,1,0:T(8,128)}, f32[336,320]{1,0:T(8,128)}, f32[336,320]{1,0:T(8,128)}, f32[640,384]{1,0:T(8,128)}, f32[4,320,320]{2,1...) custom-call(s32[2]{0:T(128)} %sides.3, bf16[2,320,2304]{2,1,0:T(8,128)(2,1)} %bitcast.18, ...), custom_call_target="tpu_custom_call" | custom-call | tf_op jit(solution)/shard_map/attention_backward/pallas_call | solution.py:523
  279.3 10.6 %pack_gradients.1 = bf16[32,416,128]{2,1,0:T(8,128)(2,1)} custom-call(f32[336,1280]{1,0:T(8,128)} %get-tuple-element.66.gwe, f32[320,1280]{1,0:T(8,128)} %get-tuple-element.67.gwst, f32[80,1280]{1,0:T(8,128)} %get-tuple-element.68.gtaps, f32[320,128]{1,0:T(8,128)} %get-tuple-element.69.gbias, f32[336,320]{1,0:T(8,128)} %get-tuple-element.70.gwo, ...), custom_call_target="tpu_custom_call" | custom-call | tf_op jit(solution)/shard_map/pack_gradients/pallas_call | solution.py:969
  290.0 0.0 copy-start
  290.0 0.0 copy-start.1
  290.0 0.0 copy-start.2
  290.0 43.3 %reduce_gradients.1 = (f32[416,128]{1,0:T(8,128)}, f32[8,128]{1,0:T(8,128)}) custom-call(bf16[2,4,4,416,128]{4,3,2,1,0:T(8,128)(2,1)} %bitcast.16), custom_call_target="tpu_custom_call" | custom-call | tf_op jit(solution)/shard_map/reduce_gradients/pallas_call | solution.py:745
  333.3 1.3 reduce_sum.9
  335.3 0.0 copy-done
  335.3 0.0 copy-done.1
  335.3 0.0 copy-done.2
  335.3 1.9 multiply_subtract_fusion
  (1 shorter events, 0.0 us)
Async XLA Ops:
  290.0 45.4 %copy-start = (f32[51840]{0:T(1024)S(1)}, f32[51840]{0:T(1024)}, u32[]{:S(2)}) copy-start(f32[51840]{0:T(1024)} %param.10) | copy-start | bytes 622084
  290.0 45.4 %copy-start.1 = (f32[51840]{0:T(1024)S(1)}, f32[51840]{0:T(1024)}, u32[]{:S(2)}) copy-start(f32[51840]{0:T(1024)} %param.12) | copy-start | bytes 622084
  290.0 45.4 %copy-start.2 = (f32[51840]{0:T(1024)S(1)}, f32[51840]{0:T(1024)}, u32[]{:S(2)}) copy-start(f32[51840]{0:T(1024)} %param.11) | copy-start | bytes 622084

commit v3 on v2

--- a/solution.py
+++ b/solution.py
@@ -217,145 +217,197 @@
 
 
 def feed_forward_kernel(
-    post, cot, mask, middle, we, wst, taps, vec,
+    post_next, cot_next, mask_next, we_next, wst_next, taps,
+    post, cot, mask, middle, we, wst, vec,
     output, grad_post, gwe, gwst, gtaps, gbias,
-    padded, grad_padded, grad_act, act, grad_exp, post_rows, out_grad, out_grad_rows, total,
+    padded_0, padded_1, grad_padded, grad_act, act_0, act_1, grad_exp_0, grad_exp_1,
+    post_rows, out_grad_rows, out_grad, total,
 ):
-    i = pl.program_id(0)
-    j = pl.program_id(1)
+    s = pl.program_id(0)
+    last = pl.num_programs(0) - 1
     width, block = wst.shape
+    blocks = gwst.shape[1] // block
     halves = block // 128
-    rows = 8
+    rows = 16
     chunks = GRID // rows
     span = rows * GRID
-    cols = 16
-
-    @pl.when((i == 0) & (j == 0))
-    def _():
-        for ref in (padded, grad_padded, gwe, gwst, gtaps, gbias, post_rows):
-            ref[...] = jnp.zeros_like(ref)
-
-    @pl.when(j == 0)
-    def _():
-        for t in range(TOKENS // 384):
-            at = slice(t * 384, (t + 1) * 384)
-            grad = cot[0, :, at].astype(F32) * mask[0, 0:1, at]
-            gbias[...] += grad[:, 0:128] + grad[:, 128:256] + grad[:, 256:384]
-            grad = grad.astype(BF)
-            out_grad[:, at] = grad
-            out_grad_rows[at, :] = grad.T
-            post_rows[at, 0 : width + EXT] = post[0, :, at].T
-
-    def expand(t, _):
-        at = pl.ds(pl.multiple_of(t * span, span), span)
+    js = pl.ds(pl.multiple_of(lax.rem(s, blocks) * block, block), block)
+    js_done = pl.ds(pl.multiple_of(lax.rem(jnp.maximum(s - 1, 0), blocks) * block, block), block)
+
+    def tokens(t):
+        return pl.ds(pl.multiple_of(t * span, span), span)
+
+    def expand(t, padded, we, wst):
+        at = tokens(t)
         filled = mm(post_rows[at, :], we[...]).astype(BF).astype(F32)
         for h in range(halves):
             for r in range(rows):
                 start = pl.multiple_of((t * rows + r + 1) * PITCH + 8, 8)
-                padded[h, pl.ds(start, GRID), :] = filled[
-                    r * GRID : (r + 1) * GRID, h * 128 : (h + 1) * 128
-                ]
-        grad_act[at, :] = mm(out_grad_rows[at, :], wst[...])
-        return 0
-
-    lax.fori_loop(0, chunks, expand, 0)
-
-    def convolve(t, _):
+                padded[h, pl.ds(start, GRID), :] = filled[r * GRID : (r + 1) * GRID, h * 128 : (h + 1) * 128]
+        grad_act[at, :] = mm(out_grad_rows[at, :], wst[...]).astype(BF)
+
+    def finish(t, act, grad_exp):
+        at = tokens(t)
+        total[:, at] += mm(wst[...], act[at, :], NT)
+        grad_post[0, :, at] += mm(we[0:width, :], grad_exp[at, :], NT)
+        gwst[:, js_done] += mm(out_grad[:, at], act[at, :])
+        gwe[:, js_done] += mm(post[0, :, at], grad_exp[at, :])
+
+    def convolve(t, padded, act):
         for h in range(halves):
             hs = slice(h * 128, (h + 1) * 128)
-            w = [jnp.broadcast_to(taps[k : k + 1, hs], (cols, 128)) for k in range(10)]
+            w = [jnp.broadcast_to(taps[k : k + 1, hs], (GRID, 128)).astype(BF) for k in range(10)]
             sums = jnp.zeros((8, 128), F32)
-            for ct in range(GRID // cols):
-                open_rows = {}
-                for q in range(-1, rows + 1):
-                    base = (t * rows + q + 1) * PITCH + 8 + ct * cols
-                    x = [padded[h, pl.ds(base + s, cols), :] for s in (-1, 0, 1)]
-                    for a in (2, 1, 0):
-                        r = q + 1 - a
-                        if 0 <= r < rows:
-                            part = w[3 * a] * x[0] + w[3 * a + 1] * x[1] + w[3 * a + 2] * x[2]
-                            open_rows[r] = part + open_rows.get(r, w[9])
-                    r = q - 1
-                    if r < 0:
-                        continue
-                    conv = open_rows.pop(r)
-                    square = conv * conv
-                    half = 0.5 * jnp.tanh(conv * (GELU_B * square + GELU_A)) + 0.5
-                    gelu = conv * half
-                    slope = half + gelu * (1.0 - half) * ((6.0 * GELU_B) * square + 2.0 * GELU_A)
-                    at = pl.ds(pl.multiple_of((t * rows + r) * GRID + ct * cols, cols), cols)
-                    act[at, hs] = gelu.astype(BF)
-                    grad = grad_act[at, hs] * slope
-                    start = pl.multiple_of((t * rows + r + 1) * PITCH + 8 + ct * cols, 8)
-                    grad_padded[h, pl.ds(start, cols), :] = grad
-                    sums = sums + grad[0:8] + grad[8:16]
-            js = pl.ds(pl.multiple_of(j * block + h * 128, 128), 128)
-            gtaps[72:80, js] += sums
-        return 0
-
-    lax.fori_loop(0, chunks, convolve, 0)
-
-    def convolve_back(t, _):
+            open_rows = {}
+            for q in range(-1, rows + 1):
+                base = (t * rows + q + 1) * PITCH + 8
+                x = [padded[h, pl.ds(base + d, GRID), :].astype(BF) for d in (-1, 0, 1)]
+                for a in (2, 1, 0):
+                    r = q + 1 - a
+                    if 0 <= r < rows:
+                        part = w[3 * a] * x[0] + w[3 * a + 1] * x[1] + w[3 * a + 2] * x[2]
+                        open_rows[r] = part + open_rows.get(r, w[9])
+                r = q - 1
+                if r < 0:
+                    continue
+                at = pl.ds(pl.multiple_of((t * rows + r) * GRID, GRID), GRID)
+                gelu, slope = gelu_pair(open_rows.pop(r))
+                act[at, hs] = gelu
+                grad = (grad_act[at, hs] * slope).astype(F32)
+                start = pl.multiple_of((t * rows + r + 1) * PITCH + 8, 8)
+                grad_padded[h, pl.ds(start, GRID), :] = grad
+                sums = sums + fold_rows(grad)
+            cols = pl.ds(pl.multiple_of(lax.rem(s, blocks) * block + h * 128, 128), 128)
+            gtaps[72:80, cols] += sums
+
+    def convolve_back(t, padded, grad_exp):
         for h in range(halves):
             hs = slice(h * 128, (h + 1) * 128)
-            w = [jnp.broadcast_to(taps[k : k + 1, hs], (cols, 128)) for k in range(9)]
+            w = [jnp.broadcast_to(taps[k : k + 1, hs], (GRID, 128)).astype(BF) for k in range(9)]
             sums = [jnp.zeros((8, 128), F32) for _ in range(9)]
-            for ct in range(GRID // cols):
-                open_rows = {}
-                x = {}
-                for q in range(-1, rows + 1):
-                    base = (t * rows + q + 1) * PITCH + 8 + ct * cols
-                    grads = [grad_padded[h, pl.ds(base + 1 - b, cols), :] for b in range(3)]
-                    if q + 1 < rows:
-                        start = pl.multiple_of((t * rows + q + 2) * PITCH + 8 + ct * cols, 8)
-                        x[q + 1] = padded[h, pl.ds(start, cols), :]
-                    for a in range(3):
-                        r = q + a - 1
-                        if not 0 <= r < rows:
-                            continue
-                        part = w[3 * a] * grads[0] + w[3 * a + 1] * grads[1] + w[3 * a + 2] * grads[2]
-                        open_rows[r] = part + open_rows[r] if r in open_rows else part
-                        for b in range(3):
-                            product = x[r] * grads[b]
-                            sums[3 * a + b] = sums[3 * a + b] + product[0:8] + product[8:16]
-                    r = q - 1
-                    if r >= 0:
-                        at = pl.ds(pl.multiple_of((t * rows + r) * GRID + ct * cols, cols), cols)
-                        grad_exp[at, hs] = open_rows.pop(r).astype(BF)
-                        x.pop(r)
-            js = pl.ds(pl.multiple_of(j * block + h * 128, 128), 128)
+            waiting = {}
+            open_rows = {}
+            x = {}
+            for q in range(-1, rows + 1):
+                base = (t * rows + q + 1) * PITCH + 8
+                grads = [grad_padded[h, pl.ds(base + 1 - b, GRID), :].astype(BF) for b in range(3)]
+                if q + 1 < rows:
+                    start = pl.multiple_of((t * rows + q + 2) * PITCH + 8, 8)
+                    x[q + 1] = padded[h, pl.ds(start, GRID), :].astype(BF)
+                for a in range(3):
+                    r = q + a - 1
+                    if not 0 <= r < rows:
+                        continue
+                    part = w[3 * a] * grads[0] + w[3 * a + 1] * grads[1] + w[3 * a + 2] * grads[2]
+                    open_rows[r] = part + open_rows[r] if r in open_rows else part
+                    for b in range(3):
+                        k = 3 * a + b
+                        product = x[r] * grads[b]
+                        product = product[0:16] + product[16:32] + product[32:48]
+                        if k in waiting:
+                            product = (product + waiting.pop(k)).astype(F32)
+                            sums[k] = sums[k] + product[0:8] + product[8:16]
+                        else:
+                            waiting[k] = product
+                r = q - 1
+                if r >= 0:
+                    at = pl.ds(pl.multiple_of((t * rows + r) * GRID, GRID), GRID)
+                    grad_exp[at, hs] = open_rows.pop(r)
+                    x.pop(r)
+            cols = pl.ds(pl.multiple_of(lax.rem(s, blocks) * block + h * 128, 128), 128)
             for k in range(9):
-                gtaps[8 * k : 8 * k + 8, js] += sums[k]
-        return 0
-
-    lax.fori_loop(0, chunks, convolve_back, 0)
-
-    js = pl.ds(pl.multiple_of(j * block, block), block)
-    gwst[:, js] += mm(out_grad[...], act[...])
-    gwe[:, js] += mm(post[0], grad_exp[...])
-    shrunk = mm(wst[...], act[...], NT)
-    back = mm(we[0:width, :], grad_exp[...], NT)
-
-    @pl.when(j == 0)
+                gtaps[8 * k : 8 * k + 8, cols] += sums[k]
+
+    @pl.when(s == 0)
     def _():
-        total[...] = shrunk
-        grad_post[0] = back
-
-    @pl.when(j != 0)
+        for ref in (padded_0, padded_1, grad_padded, act_1, grad_exp_1, out_grad, gwe, gwst, gtaps, gbias, post_rows):
+            ref[...] = jnp.zeros_like(ref)
+
+    @pl.when((s == 0) | ((lax.rem(s + 1, blocks) == 0) & (s + 1 < last)))
     def _():
-        total[...] += shrunk
-        grad_post[0] += back
-
-    @pl.when(j == pl.num_programs(1) - 1)
+        for t in range(TOKENS // 384):
+            at = slice(t * 384, (t + 1) * 384)
+            grad = cot_next[0, :, at].astype(F32) * mask_next[0, 0:1, at]
+            gbias[...] += grad[:, 0:128] + grad[:, 128:256] + grad[:, 256:384]
+            out_grad_rows[at, :] = grad.astype(BF).T
+            post_rows[at, 0 : width + EXT] = post_next[0, :, at].T
+
+    @pl.when(lax.rem(s, blocks) == min(1, blocks - 1))
+    def _():
+        for t in range(TOKENS // 384):
+            at = slice(t * 384, (t + 1) * 384)
+            out_grad[:, at] = (cot[0, :, at].astype(F32) * mask[0, 0:1, at]).astype(BF)
+
+    @pl.when((s == 0) | (lax.rem(s, blocks) == min(1, blocks - 1)))
+    def _():
+        total[...] = jnp.zeros_like(total)
+        grad_post[...] = jnp.zeros_like(grad_post)
+
+    @pl.when(s == 0)
+    def _():
+        def first(t, _):
+            expand(t, padded_0, we, wst)
+            return 0
+
+        lax.fori_loop(0, chunks, first, 0)
+
+    def work(padded, padded_next, act, act_done, grad_exp, grad_exp_done):
+        def forward(t, _):
+            finish(t, act_done, grad_exp_done)
+            convolve(t, padded, act)
+            return 0
+
+        def backward(t, _):
+            expand(t, padded_next, we_next, wst_next)
+            convolve_back(t, padded, grad_exp)
+            return 0
+
+        lax.fori_loop(0, chunks, forward, 0)
+        lax.fori_loop(0, chunks, backward, 0)
+
+    @pl.when((s < last) & (lax.rem(s, 2) == 0))
+    def _():
+        work(padded_0, padded_1, act_0, act_1, grad_exp_0, grad_exp_1)
+
+    @pl.when((s < last) & (lax.rem(s, 2) == 1))
+    def _():
+        work(padded_1, padded_0, act_1, act_0, grad_exp_1, grad_exp_0)
+
+    @pl.when(s == last)
+    def _():
+        def rest(t, _):
+            @pl.when(lax.rem(s, 2) == 0)
+            def _():
+                finish(t, act_1, grad_exp_1)
+
+            @pl.when(lax.rem(s, 2) == 1)
+            def _():
+                finish(t, act_0, grad_exp_0)
+
+            return 0
+
+        lax.fori_loop(0, chunks, rest, 0)
+
+    @pl.when((s > 0) & (lax.rem(s, blocks) == 0))
     def _():
         for t in range(TOKENS // 128):
             at = slice(t * 128, (t + 1) * 128)
             output[0, :, at] = ((middle[0, :, at] + total[:, at] + vec[4]) * mask[0, 0:1, at]).astype(BF)
 
 
+def gelu_pair(x):
+    kind = x.dtype.type
+    square = x * x
+    half = kind(0.5) * jnp.tanh(x * (kind(GELU_B) * square + kind(GELU_A))) + kind(0.5)
+    gelu = x * half
+    return gelu, half + gelu * (kind(1.0) - half) * (kind(6.0 * GELU_B) * square + kind(2.0 * GELU_A))
+
+
 def feed_forward(post, cot, mask, middle, we, wst, taps, vec, block=256):
     n, width, tokens = cot.shape
     hidden = wst.shape[1]
+    blocks = hidden // block
+    count = n * blocks
     shape = jax.ShapeDtypeStruct
     outs = [
         shape((n, width, tokens), BF),
@@ -365,29 +417,40 @@
         shape((80, hidden), F32),
         shape((width, 128), F32),
     ]
-    one = {"pipeline_mode": pl.Buffered(1)}
-    columns = lambda x: pl.BlockSpec((x.shape[0], block), lambda i, j: (0, j))
+
+    def ahead(s):
+        return jnp.minimum(s + 1, count - 1)
+
+    def behind(s):
+        return jnp.maximum(s - 1, 0)
+
+    def image(x, step):
+        zeros = (0,) * (len(x.shape) - 1)
+        return pl.BlockSpec((1,) + tuple(x.shape[1:]), lambda s: (step(s) // blocks,) + zeros)
+
+    def columns(x, step):
+        return pl.BlockSpec((x.shape[0], block), lambda s: (0, lax.rem(step(s), blocks)))
+
     return pl.pallas_call(
         feed_forward_kernel,
-        grid=(n, hidden // block),
-        in_specs=[per_image(post), per_image(cot), per_image(mask), per_image(middle, **one)]
-        + [columns(we), columns(wst), columns(taps), whole(vec)],
-        out_specs=[per_image(x) for x in outs[:2]] + [whole(x) for x in outs[2:]],
+        grid=(count + 1,),
+        in_specs=[image(x, ahead) for x in (post, cot, mask)]
+        + [columns(we, ahead), columns(wst, ahead), columns(taps, lambda s: jnp.minimum(s, count - 1))]
+        + [image(x, behind) for x in (post, cot, mask, middle)]
+        + [columns(we, behind), columns(wst, behind), whole(vec)],
+        out_specs=[image(x, behind) for x in outs[:2]] + [whole(x) for x in outs[2:]],
         out_shape=outs,
-        scratch_shapes=[
-            pltpu.VMEM((block // 128, (GRID + 2) * PITCH + 8, 128), F32),
-            pltpu.VMEM((block // 128, (GRID + 2) * PITCH + 8, 128), F32),
-            pltpu.VMEM((tokens, block), F32),
-            pltpu.VMEM((tokens, block), BF),
-            pltpu.VMEM((tokens, block), BF),
+        scratch_shapes=[pltpu.VMEM((block // 128, (GRID + 2) * PITCH + 8, 128), F32)] * 3
+        + [pltpu.VMEM((tokens, block), BF)] * 5
+        + [
             pltpu.VMEM((tokens, width + 64), BF),
+            pltpu.VMEM((tokens, width), BF),
             pltpu.VMEM((width, tokens), BF),
-            pltpu.VMEM((tokens, width), BF),
             pltpu.VMEM((width, tokens), F32),
         ],
         compiler_params=pltpu.CompilerParams(vmem_limit_bytes=VMEM_BYTES),
         name="feed_forward",
-    )(post, cot, mask, middle, we, wst, taps, vec)
+    )(post, cot, mask, we, wst, taps, post, cot, mask, middle, we, wst, vec)
 
 
 def attention_backward_kernel(

time: 341 us -> 317 us (0.930)
  Pallas kernels: 330 us -> 305 us
    pallas_call x1, Pallas kernels: 115 us -> 90.9 us  [feed_forward(): pl.pallas_call(feed_forward_kernel, grid=(count + 1,), in_specs=[image(x,...]
where the time goes in v3:
time: 317 us; the launch traced here: 314 us
  Pallas kernels  305 us (96%)
  other arithmetic  4.84 us (2%)
    pallas_call x1, Pallas kernels, feed_forward(): pl.pallas_call(feed_forward_kernel, grid=(count + 1,), in_specs=[image(x,...  90.9 us
    pallas_call x1, Pallas kernels, attention_backward(): pl.pallas_call(attention_backward_kernel, grid_spec=pltpu.PrefetchScalarG...  79.9 us
    pallas_call x1, Pallas kernels, reduce_slots(): pl.pallas_call(reduce_kernel, out_shape=[jax.ShapeDtypeStruct((rows, 128)...  43.3 us
    pallas_call x1, Pallas kernels, attention_forward(): pl.pallas_call(attention_forward_kernel, grid_spec=pltpu.PrefetchScalarGr...  40.6 us
    pallas_call x1, Pallas kernels, gather_slots(): pl.pallas_call(gather_kernel, out_shape=jax.ShapeDtypeStruct((2, 4, 4) +...  31.5 us
    pallas_call x1, Pallas kernels, pack_gradients(): pl.pallas_call(partial(pack_kernel, order, slot_rows, bases), out_shape=j...  10.6 us
    pallas_call x1, Pallas kernels, unpack_weights(): pl.pallas_call(partial(unpack_kernel, order, slot_rows, bases), out_shape...  8.46 us

profile of v3, /device:TPU:0, one launch (start us, length us, event | category | flops | bytes accessed | tf_op | source)
XLA Modules:
  0.0 314.3 jit_solution(6148493497343544031)
XLA Ops:
  0.6 0.7 broadcast_multiply_fusion
  1.3 0.1 and_convert_fusion
  1.4 0.9 convert_bitcast_fusion
  2.3 0.7 pad.4.own
  3.0 0.7 broadcast_in_dim.2.mask.mask_next
  3.7 31.5 %gather_weights.1 = bf16[2,4,4,416,128]{4,3,2,1,0:T(8,128)(2,1)} custom-call(bf16[416,128]{1,0:T(8,128)(2,1)} %pad.4.own), custom_call_target="tpu_custom_call" | custom-call | tf_op jit(solution)/shard_map/gather_weights/pallas_call | solution.py:715
  35.2 8.5 %unpack_weights.1 = (f32[5,320,128]{2,1,0:T(8,128)}, f32[3,320]{1,0:T(4,128)}, bf16[320,320]{1,0:T(8,128)(2,1)}, bf16[320,336]{1,0:T(8,128)(2,1)}, bf16[4,320,32...) custom-call(bf16[32,416,128]{2,1,0:T(8,128)(2,1)} %bitcast.18), custom_call_target="tpu_custom_call" | custom-call | tf_op jit(solution)/shard_map/unpack_weights/pallas_call | solution.py:953
  43.6 40.6 %attention_forward.1 = (bf16[2,336,2304]{2,1,0:T(8,128)(2,1)}, bf16[2,4,576,320]{3,2,1,0:T(8,128)(2,1)}, f32[2,576,320]{2,1,0:T(8,128)}, bf16[2,576,384]{2,1,0:T...) custom-call(s32[2]{0:T(128)} %sides.3, ...), custom_call_target="tpu_custom_call" | custom-call | tf_op jit(solution)/shard_map/attention_forward/pallas_call | solution.py:201
  84.3 90.9 %feed_forward.1 = (bf16[2,320,2304]{2,1,0:T(8,128)(2,1)}, f32[2,320,2304]{2,1,0:T(8,128)}, f32[336,1280]{1,0:T(8,128)}, f32[320,1280]{1,0:T(8,128)}, f32[80,1280]{1,0:T(8,128)}, /*index=5*/f32[320,128]{1,0:T(8,128)}) custom-call(bf16[2,336,2304]{2,1,0:T(8,128)(2,1)} %get-tuple-element.49.post_next.post, bf16[2,320,2304]{2,1,0:T(8,128)(2,1)} %bitcast.15, ...), custom_call_target="tpu_custom_call" | custom-call | tf_op jit(solution)/shard_map/feed_forward/pallas_call | solution.py:434
  175.2 79.9 %attention_backward.1 = (f32[2,320,2304]{2,1,0:T(8,128)}, f32[336,320]{1,0:T(8,128)}, f32[336,320]{1,0:T(8,128)}, f32[640,384]{1,0:T(8,128)}, f32[4,320,320]{2,1...) custom-call(s32[2]{0:T(128)} %sides.3, bf16[2,320,2304]{2,1,0:T(8,128)(2,1)} %bitcast.21, ...), custom_call_target="tpu_custom_call" | custom-call | tf_op jit(solution)/shard_map/attention_backward/pallas_call | solution.py:586
  255.1 10.6 %pack_gradients.1 = bf16[32,416,128]{2,1,0:T(8,128)(2,1)} custom-call(f32[336,1280]{1,0:T(8,128)} %get-tuple-element.66.gwe, f32[320,1280]{1,0:T(8,128)} %get-tuple-element.67.gwst, f32[80,1280]{1,0:T(8,128)} %get-tuple-element.68.gtaps, f32[320,128]{1,0:T(8,128)} %get-tuple-element.69.gbias, f32[336,320]{1,0:T(8,128)} %get-tuple-element.70.gwo, ...), custom_call_target="tpu_custom_call" | custom-call | tf_op jit(solution)/shard_map/pack_gradients/pallas_call | solution.py:1032
  265.7 0.0 copy-start
  265.7 0.0 copy-start.1
  265.8 0.0 copy-start.2
  265.8 43.3 %reduce_gradients.1 = (f32[416,128]{1,0:T(8,128)}, f32[8,128]{1,0:T(8,128)}) custom-call(bf16[2,4,4,416,128]{4,3,2,1,0:T(8,128)(2,1)} %bitcast.19), custom_call_target="tpu_custom_call" | custom-call | tf_op jit(solution)/shard_map/reduce_gradients/pallas_call | solution.py:808
  309.1 1.3 reduce_sum.9
  311.1 0.0 copy-done
  311.1 0.0 copy-done.1
  311.1 0.0 copy-done.2
  311.1 1.9 multiply_subtract_fusion
  (1 shorter events, 0.0 us)
Async XLA Ops:
  265.7 45.4 %copy-start = (f32[51840]{0:T(1024)S(1)}, f32[51840]{0:T(1024)}, u32[]{:S(2)}) copy-start(f32[51840]{0:T(1024)} %param.10) | copy-start | bytes 622084
  265.7 45.4 %copy-start.1 = (f32[51840]{0:T(1024)S(1)}, f32[51840]{0:T(1024)}, u32[]{:S(2)}) copy-start(f32[51840]{0:T(1024)} %param.12) | copy-start | bytes 622084
  265.8 45.4 %copy-start.2 = (f32[51840]{0:T(1024)S(1)}, f32[51840]{0:T(1024)}, u32[]{:S(2)}) copy-start(f32[51840]{0:T(1024)} %param.11) | copy-start | bytes 622084

commit v4 on v3

--- a/solution.py
+++ b/solution.py
@@ -616,25 +616,24 @@
 class Place:
     def __init__(self):
         self.dp = lax.axis_index("dp")
-        fsdp = lax.axis_index("fsdp")
+        self.fsdp = lax.axis_index("fsdp")
         self.y, self.x = self.dp // 2, self.dp % 2
-        self.z, self.core = fsdp // 2, fsdp % 2
-        self.beside_x = (self.dp + 1 - 2 * self.x, fsdp)
-        self.beside_y = (self.dp + 2 - 4 * self.y, fsdp)
-        self.beside_core = (self.dp, fsdp + 1 - 2 * self.core)
-
-    def up(self, k):
-        return (self.z + k) % 4
+        self.z, self.core = self.fsdp // 2, self.fsdp % 2
+        self.other_core = 1 - self.core
+        self.beside_x = (self.dp + 1 - 2 * self.x, self.fsdp)
+        self.beside_y = (self.dp + 2 - 4 * self.y, self.fsdp)
+        self.across = (3 - self.dp, self.fsdp)
+        self.beside_core = (self.dp, self.fsdp + 1 - 2 * self.core)
+        self.others = (self.z + 1 - 2 * (self.z % 2), 2 - self.z // 2, 3 * (1 - self.z // 2))
+
+    def at_z(self, z):
+        return (self.dp, z * 2 + self.core)
 
     def along_z(self, k):
-        return (self.dp, self.up(k) * 2 + self.core)
-
-    def partners(self):
-        return [self.beside_core, self.beside_x, self.beside_y] + [self.along_z(k) for k in (1, 2, 3)]
-
-    def greet(self):
+        return self.at_z((self.z + k) % 4)
+
+    def greet(self, partners):
         barrier = pltpu.get_barrier_semaphore()
-        partners = self.partners()
         for device in partners:
             pl.semaphore_signal(barrier, inc=1, device_id=device, device_id_type=MESH)
         pl.semaphore_wait(barrier, len(partners))
@@ -644,13 +643,13 @@
     def __init__(self, send, recv):
         self.send, self.recv, self.started = send, recv, []
 
-    def __call__(self, source, target, device):
+    def __call__(self, source, target, device, recv=None):
         k = len(self.started)
         copy = pltpu.make_async_remote_copy(
             src_ref=source,
             dst_ref=target,
             send_sem=self.send.at[k],
-            recv_sem=self.recv.at[k],
+            recv_sem=self.recv.at[k] if recv is None else recv,
             device_id=device,
             device_id_type=MESH,
         )
@@ -663,124 +662,176 @@
             copy.wait_send()
 
 
-def gather_kernel(own, out, own_sem, send_sem, recv_sem):
+def gather_kernel(slot_rows, bases, own, *refs):
+    outs, (slots, wide, line, own_sem, send_sem, recv_sem, z_sem) = refs[:13], refs[13:]
     me = Place()
     half = own.shape[0] // 2
     first, second = pl.ds(0, half), pl.ds(half, half)
     send = Sender(send_sem, recv_sem)
-    copy = pltpu.make_async_copy(own, out.at[me.core, me.dp, me.z], own_sem)
+    copy = pltpu.make_async_copy(own, slots.at[me.core, me.dp, me.z], own_sem)
     copy.start()
-    me.greet()
-    slot = out.at[me.core, me.dp, me.z]
-    z_copies = [send(own, slot, me.along_z(k)) for k in (1, 2, 3)]
-    x_copies = [send(own, slot, me.beside_x)]
-    y_copies = [send(own, slot, me.beside_y)]
-    core_copies = [send(own, slot, me.beside_core)]
+    me.greet([me.beside_core, me.beside_x, me.beside_y] + [me.at_z(z) for z in me.others])
+    own_slot = slots.at[me.core, me.dp, me.z]
+
+    def send_z(j):
+        return send(own, own_slot, me.at_z(me.others[j]), z_sem.at[me.z])
+
+    send_z(0)
+    x_copies = [send(own, own_slot, me.beside_x)]
+    y_copies = [send(own, own_slot, me.beside_y)]
+    core_copies = [(send(own, own_slot, me.beside_core), me.dp, me.z)]
+    send_z(1)
     half_copies = []
+    order = (me.z,) + me.others
+
+    def open_slot(core, dp, z):
+        spread_slot(slots[core, dp, z], (dp * 8 + z * 2 + core), slot_rows, line, wide)
 
     def forward(k):
-        z = (me.z + 4 - k) % 4
+        z = order[k]
         x_copies[k].wait_recv()
-        dp = me.beside_x[0]
-        slot = out.at[me.core, dp, z]
+        slot = slots.at[me.core, me.beside_x[0], z]
         half_copies.append(send(slot.at[first], slot.at[first], me.beside_y))
-        core_copies.append(send(slot, slot, me.beside_core))
+        core_copies.append((send(slot, slot, me.beside_core), me.beside_x[0], z))
         y_copies[k].wait_recv()
-        dp = me.beside_y[0]
-        slot = out.at[me.core, dp, z]
+        slot = slots.at[me.core, me.beside_y[0], z]
         half_copies.append(send(slot.at[second], slot.at[second], me.beside_x))
-        core_copies.append(send(slot, slot, me.beside_core))
-
+        core_copies.append((send(slot, slot, me.beside_core), me.beside_y[0], z))
+        open_slot(me.core, me.beside_x[0], z)
+        open_slot(me.core, me.beside_y[0], z)
+
+    copy.wait()
+    open_slot(me.core, me.dp, me.z)
     forward(0)
     for k in (1, 2, 3):
-        z_copies[k - 1].wait_recv()
-        slot = out.at[me.core, me.dp, (me.z + 4 - k) % 4]
+        z = order[k]
+        slot = slots.at[me.core, me.dp, z]
+        pltpu.make_async_remote_copy(
+            src_ref=own,
+            dst_ref=slot,
+            send_sem=send_sem.at[0],
+            recv_sem=z_sem.at[z],
+            device_id=me.at_z(z),
+            device_id_type=MESH,
+        ).wait_recv()
         x_copies.append(send(slot, slot, me.beside_x))
         y_copies.append(send(slot, slot, me.beside_y))
-        core_copies.append(send(slot, slot, me.beside_core))
+        core_copies.append((send(slot, slot, me.beside_core), me.dp, z))
+        if k == 1:
+            send_z(2)
+        open_slot(me.core, me.dp, z)
         forward(k)
     for k in range(4):
         half_copies[2 * k].wait_recv()
         half_copies[2 * k + 1].wait_recv()
-        slot = out.at[me.core, 3 - me.dp, (me.z + 4 - k) % 4]
-        core_copies.append(send(slot, slot, me.beside_core))
-    for copied in core_copies:
+        slot = slots.at[me.core, me.across[0], order[k]]
+        core_copies.append((send(slot, slot, me.beside_core), me.across[0], order[k]))
+        open_slot(me.core, me.across[0], order[k])
+    for copied, dp, z in core_copies:
         copied.wait_recv()
-    copy.wait()
+        open_slot(me.other_core, dp, z)
     send.finish()
-
-
-def gather_slots(own):
-    count = 35
-    return pl.pallas_call(
-        gather_kernel,
-        out_shape=jax.ShapeDtypeStruct((2, 4, 4) + own.shape, own.dtype),
+    write_weights(bases, wide, *outs)
+
+
+def gather_weights(own, slot_rows, width):
+    bases, count = row_bases(width, 4 * width)
+    outs = weight_shapes(width)
+    copies = 35
+    values = pl.pallas_call(
+        partial(gather_kernel, slot_rows, bases),
+        out_shape=list(outs.values()),
         in_specs=[pl.BlockSpec(memory_space=pltpu.VMEM)],
-        out_specs=pl.BlockSpec(memory_space=pltpu.VMEM),
+        out_specs=[pl.BlockSpec(memory_space=pltpu.VMEM)] * len(outs),
         scratch_shapes=[
+            pltpu.VMEM((2, 4, 4) + own.shape, BF),
+            pltpu.VMEM((3, -(-32 * slot_rows * 128 // width // 8) * 8 + 8, 128), F32),
+            pltpu.VMEM(own.shape, F32),
             pltpu.SemaphoreType.DMA(()),
-            pltpu.SemaphoreType.DMA((count,)),
-            pltpu.SemaphoreType.DMA((count,)),
+            pltpu.SemaphoreType.DMA((copies,)),
+            pltpu.SemaphoreType.DMA((copies,)),
+            pltpu.SemaphoreType.DMA((4,)),
         ],
         compiler_params=pltpu.CompilerParams(
             collective_id=0, has_side_effects=True, vmem_limit_bytes=VMEM_BYTES
         ),
         name="gather_weights",
     )(own)
-
-
-def reduce_kernel(grads, shard, squares, core_in, y_in, x_in, x_last, y_last, z_in, small, send_sem, recv_sem):
+    return dict(zip(outs, values, strict=True))
+
+
+def reduce_kernel(
+    grads, shard, squares,
+    core_in, y_in, x_in, x_last, y_last, z_in, small, send_sem, recv_sem,
+):
     me = Place()
     rows = grads.shape[3]
     half = rows // 2
     first, second = pl.ds(0, half), pl.ds(half, half)
     send = Sender(send_sem, recv_sem)
+    peers = [(me.dp, (me.z + k) % 4 * 2 + core) for k in range(4) for core in (me.core, me.other_core)][1:]
+    planes = [me.beside_x, me.beside_y, me.across]
+    me.greet(peers + planes)
+    units = [(me.z + k) % 4 for k in (2, 1, 3, 0)]
+    core_copies = [send(grads.at[me.other_core, z], core_in.at[z], me.beside_core) for z in units]
+    y_copies, x_copies, last = [], [], []
     other_x, other_y = 1 - me.x, 1 - me.y
-    me.greet()
-    order = [2 * other_y + other_x, 2 * other_y + me.x, 2 * me.y + other_x, me.dp]
-    core_copies = [send(grads.at[1 - me.core, dp], core_in.at[dp], me.beside_core) for dp in order]
-
-    def add(dp):
-        for z in range(4):
-            core_in[dp, z] = (core_in[dp, z].astype(F32) + grads[me.core, dp, z].astype(F32)).astype(BF)
-
-    core_copies[0].wait_recv()
-    add(order[0])
-    y_copies = [send(core_in.at[order[0], :, first], y_in.at[0], me.beside_y)]
-    x_copies = [send(core_in.at[order[0], :, second], x_in.at[0], me.beside_x)]
-    core_copies[1].wait_recv()
-    add(order[1])
-    y_copies.append(send(core_in.at[order[1], :, first], y_in.at[1], me.beside_y))
-    core_copies[2].wait_recv()
-    add(order[2])
-    x_copies.append(send(core_in.at[order[2], :, second], x_in.at[1], me.beside_x))
-    core_copies[3].wait_recv()
-    add(order[3])
-    y_copies[0].wait_recv()
-    x_copies[0].wait_recv()
-    last = []
-    for k in (0, 1, 2, 3):
-        z = (me.z + k) % 4
-        y_in[0, z] = (y_in[0, z].astype(F32) + core_in[order[2], z, first].astype(F32)).astype(BF)
-        last.append(send(y_in.at[0, z], x_last.at[z], me.beside_x))
-        x_in[0, z] = (x_in[0, z].astype(F32) + core_in[order[1], z, second].astype(F32)).astype(BF)
-        last.append(send(x_in.at[0, z], y_last.at[z], me.beside_y))
-    y_copies[1].wait_recv()
-    x_copies[1].wait_recv()
+
+    def cores(k):
+        z = units[k]
+        core_copies[k].wait_recv()
+        for dp in range(4):
+            core_in[z, dp] = (core_in[z, dp].astype(F32) + grads[me.core, z, dp].astype(F32)).astype(BF)
+        y_copies.append(
+            [send(core_in.at[z, 2 * other_y + x, first], y_in.at[z, x], me.beside_y) for x in range(2)]
+        )
+        x_copies.append(
+            [send(core_in.at[z, 2 * y + other_x, second], x_in.at[z, y], me.beside_x) for y in range(2)]
+        )
+
+    def plane(k):
+        z = units[k]
+        for copied in y_copies[k]:
+            copied.wait_recv()
+        y_in[z, other_x] = (
+            y_in[z, other_x].astype(F32) + core_in[z, 2 * me.y + other_x, first].astype(F32)
+        ).astype(BF)
+        to_x = send(y_in.at[z, other_x], x_last.at[z], me.beside_x)
+        for copied in x_copies[k]:
+            copied.wait_recv()
+        x_in[z, other_y] = (
+            x_in[z, other_y].astype(F32) + core_in[z, 2 * other_y + me.x, second].astype(F32)
+        ).astype(BF)
+        last.append((to_x, send(x_in.at[z, other_y], y_last.at[z], me.beside_y)))
+
     z_copies = []
-    for k in (1, 2, 3, 0):
-        z = (me.z + k) % 4
-        last[2 * k].wait_recv()
-        last[2 * k + 1].wait_recv()
-        low = y_in[1, z].astype(F32) + core_in[me.dp, z, first].astype(F32) + x_last[z].astype(F32)
-        high = x_in[1, z].astype(F32) + core_in[me.dp, z, second].astype(F32) + y_last[z].astype(F32)
-        if k == 0:
+
+    def column(k):
+        z = units[k]
+        for copied in last[k]:
+            copied.wait_recv()
+        low = y_in[z, me.x].astype(F32) + core_in[z, me.dp, first].astype(F32) + x_last[z].astype(F32)
+        high = x_in[z, me.y].astype(F32) + core_in[z, me.dp, second].astype(F32) + y_last[z].astype(F32)
+        if k == 3:
             shard[first, :] = low
             shard[second, :] = high
         else:
-            z_in[k - 1, first] = low.astype(BF)
-            z_in[k - 1, second] = high.astype(BF)
-            z_copies.append(send(z_in.at[k - 1], z_in.at[k + 2], me.along_z(k)))
+            z_in[k, first] = low.astype(BF)
+            z_in[k, second] = high.astype(BF)
+            z_copies.append(send(z_in.at[k], z_in.at[k + 3], me.at_z(z)))
+
+    cores(0)
+    cores(1)
+    plane(0)
+    cores(2)
+    plane(1)
+    column(0)
+    cores(3)
+    plane(2)
+    column(1)
+    plane(3)
+    column(2)
+    column(3)
     for k in (0, 1, 2):
         z_copies[k].wait_recv()
         shard[...] += z_in[k + 3].astype(F32)
@@ -789,22 +840,26 @@
         part = shard[8 * k : 8 * k + 8, :]
         total = total + part * part
     small[0] = total
-    for k, device in enumerate((me.beside_core, me.beside_x, me.beside_y)):
-        copied = send(small.at[k], small.at[4 + k], device)
-        copied.wait_recv()
-        small[k + 1] = small[k] + small[4 + k]
-    copies = [send(small.at[3], small.at[8 + me.z], me.along_z(k)) for k in (1, 2, 3)]
-    small[8 + me.z] = small[3]
+    small[2 + me.fsdp] = total
+    copies = [send(small.at[0], small.at[2 + me.fsdp], device) for device in peers]
     for copied in copies:
         copied.wait_recv()
-    squares[...] = ((small[8] + small[9]) + small[10]) + small[11]
+    total = small[2]
+    for k in range(1, 8):
+        total = total + small[2 + k]
+    small[1] = total
+    small[10 + me.dp] = total
+    copies = [send(small.at[1], small.at[10 + me.dp], device) for device in planes]
+    for copied in copies:
+        copied.wait_recv()
+    squares[...] = ((small[10] + small[11]) + small[12]) + small[13]
     send.finish()
 
 
 def reduce_slots(grads):
     rows = grads.shape[3]
     half = rows // 2
-    count = 4 + 4 + 8 + 3 + 6
+    count = 4 + 16 + 8 + 3 + 7 + 3
     return pl.pallas_call(
         reduce_kernel,
         out_shape=[jax.ShapeDtypeStruct((rows, 128), F32), jax.ShapeDtypeStruct((8, 128), F32)],
@@ -812,12 +867,12 @@
         out_specs=[pl.BlockSpec(memory_space=pltpu.VMEM)] * 2,
         scratch_shapes=[
             pltpu.VMEM((4, 4, rows, 128), BF),
-            pltpu.VMEM((2, 4, half, 128), BF),
-            pltpu.VMEM((2, 4, half, 128), BF),
+            pltpu.VMEM((4, 2, half, 128), BF),
+            pltpu.VMEM((4, 2, half, 128), BF),
             pltpu.VMEM((4, half, 128), BF),
             pltpu.VMEM((4, half, 128), BF),
             pltpu.VMEM((6, rows, 128), BF),
-            pltpu.VMEM((12, 8, 128), F32),
+            pltpu.VMEM((14, 8, 128), F32),
             pltpu.SemaphoreType.DMA((count,)),
             pltpu.SemaphoreType.DMA((count,)),
         ],
@@ -865,30 +920,53 @@
 SPAN = 96
 
 
-def unpack_kernel(
-    order, slot_rows, bases,
-    slots, vec, rows, wq, wqt, wr, wk, wv, wvt, wo, wot, we, wst, taps,
-    flat, wide,
-):
-    width = wq.shape[0]
-    hidden = wst.shape[1]
+def regroup_lines(read, write, low):
+    part = [read(k) for k in range(5)]
+    turned = [pltpu.roll(part[k], 64, 1) for k in (2, 3, 4)]
+    for k in range(3):
+        write(0, k, part[k])
+    write(1, 0, jnp.where(low, turned[0], turned[1]))
+    write(1, 1, jnp.where(low, turned[1], turned[2]))
+    write(1, 2, turned[2])
+
+
+def spread_slot(values, slot, slot_rows, line, wide):
+    pairs = slot_rows // 5
+    line[...] = values.astype(F32)
+
+    def part(start, count):
+        low = lax.broadcasted_iota(jnp.int32, (count, 128), 1) < 64
+
+        def write(parity, k, value):
+            wide[k, pl.ds(slot * (2 * pairs) + 2 * start + parity, count, stride=2), :] = value
+
+        regroup_lines(lambda k: line[pl.ds(5 * start + k, count, stride=5), :], write, low)
+
+    part(0, pairs // 8 * 8)
+    if pairs % 8:
+        part(pairs // 8 * 8, pairs % 8)
+
+
+def unpack_kernel(order, slot_rows, bases, slots, *refs):
+    outs, (flat, wide) = refs[:13], refs[13:]
     for slot, place in enumerate(order):
         flat[pl.ds(slot * slot_rows, slots.shape[1]), :] = slots[place].astype(F32)
     low = lax.broadcasted_iota(jnp.int32, (SPAN, 128), 1) < 64
 
     def regroup(t, _):
-        part = [flat[pl.ds(t * (5 * SPAN) + k, SPAN, stride=5), :] for k in range(5)]
-        turned = [pltpu.roll(part[k], 64, 1) for k in (2, 3, 4)]
-        even = pl.ds(t * (2 * SPAN), SPAN, stride=2)
-        odd = pl.ds(t * (2 * SPAN) + 1, SPAN, stride=2)
-        for k in range(3):
-            wide[k, even, :] = part[k]
-        wide[0, odd, :] = jnp.where(low, turned[0], turned[1])
-        wide[1, odd, :] = jnp.where(low, turned[1], turned[2])
-        wide[2, odd, :] = turned[2]
+        def write(parity, k, value):
+            wide[k, pl.ds(t * (2 * SPAN) + parity, SPAN, stride=2), :] = value
+
+        regroup_lines(lambda k: flat[pl.ds(t * (5 * SPAN) + k, SPAN, stride=5), :], write, low)
         return 0
 
     lax.fori_loop(0, wide.shape[1] // (2 * SPAN), regroup, 0)
+    write_weights(bases, wide, *outs)
+
+
+def write_weights(bases, wide, vec, rows, wq, wqt, wr, wk, wv, wvt, wo, wot, we, wst, taps):
+    width = wq.shape[0]
+    hidden = wst.shape[1]
 
     def take(base, count, stride=1):
         at = pl.ds(base, count, stride=stride) if stride > 1 else pl.ds(base, count)
@@ -930,11 +1008,10 @@
     return -(-count // (2 * SPAN)) * 2 * SPAN
 
 
-def unpack_weights(slots, order, slot_rows, width):
+def weight_shapes(width):
     hidden = 4 * width
-    bases, count = row_bases(width, hidden)
     shape = jax.ShapeDtypeStruct
-    outs = dict(
+    return dict(
         vec=shape((5, width, 128), F32),
         rows=shape((3, width), F32),
         wq=shape((width, width), BF),
@@ -949,6 +1026,11 @@
         wst=shape((width, hidden), BF),
         taps=shape((10, hidden), F32),
     )
+
+
+def unpack_weights(slots, order, slot_rows, width):
+    bases, count = row_bases(width, 4 * width)
+    outs = weight_shapes(width)
     flat_rows = max(len(order) * slot_rows, wide_rows(count) * width // 128) + slots.shape[1]
     values = pl.pallas_call(
         partial(unpack_kernel, order, slot_rows, bases),
@@ -1066,16 +1148,16 @@
     slot_rows = params.shape[0] // 128
     padded_rows = -(-slot_rows // 32) * 32
     own = jnp.pad(params.reshape(slot_rows, 128).astype(BF), ((0, padded_rows - slot_rows), (0, 0)))
+    order = list(range(outer * inner))
     if on_grid:
-        order = [(s % 2) * 16 + s // 8 * 4 + s % 8 // 2 for s in range(32)]
-        slots = gather_slots(own).reshape(32, padded_rows, 128)
+        weights = gather_weights(own, slot_rows, width)
     else:
-        order = list(range(outer * inner))
-        slots = lax.all_gather(own, axes)
-    weights = unpack_weights(slots, order, slot_rows, width)
+        weights = unpack_weights(lax.all_gather(own, axes), order, slot_rows, width)
     output, grad_images, grads = device_step(
         images.transpose(0, 2, 1), cotangent.transpose(0, 2, 1), kv_sides, weights
     )
+    if on_grid:
+        order = [s % 2 * 16 + s % 8 // 2 * 4 + s // 8 for s in range(32)]
     slots = pack_gradients(grads, order, slot_rows, padded_rows, width)
     if on_grid:
         shard, squares = reduce_slots(slots.reshape(2, 4, 4, padded_rows, 128))

time: 317 us -> 303 us (0.956)
  Pallas kernels: 305 us -> 290 us
    pallas_call x1, Pallas kernels: 43.3 us -> 33.5 us  [reduce_slots(): pl.pallas_call(reduce_kernel, out_shape=[jax.ShapeDtypeStruct((rows, 128)...]
    pallas_call x2 -> x1, Pallas kernels: 40 us -> 34.7 us  [gather_weights(): pl.pallas_call(partial(gather_kernel, slot_rows, bases), out_shape=list(o...]
where the time goes in v4:
time: 303 us; the launch traced here: 299 us
  Pallas kernels  290 us (96%)
  other arithmetic  4.84 us (2%)
    pallas_call x1, Pallas kernels, feed_forward(): pl.pallas_call(feed_forward_kernel, grid=(count + 1,), in_specs=[image(x,...  90.8 us
    pallas_call x1, Pallas kernels, attention_backward(): pl.pallas_call(attention_backward_kernel, grid_spec=pltpu.PrefetchScalarG...  80 us
    pallas_call x1, Pallas kernels, attention_forward(): pl.pallas_call(attention_forward_kernel, grid_spec=pltpu.PrefetchScalarGr...  40.7 us
    pallas_call x1, Pallas kernels, gather_weights(): pl.pallas_call(partial(gather_kernel, slot_rows, bases), out_shape=list(o...  34.7 us
    pallas_call x1, Pallas kernels, reduce_slots(): pl.pallas_call(reduce_kernel, out_shape=[jax.ShapeDtypeStruct((rows, 128)...  33.5 us
    pallas_call x1, Pallas kernels, pack_gradients(): pl.pallas_call(partial(pack_kernel, order, slot_rows, bases), out_shape=j...  10.6 us

profile of v4, /device:TPU:0, one launch (start us, length us, event | category | flops | bytes accessed | tf_op | source)
XLA Modules:
  0.0 299.2 jit_solution(12705695020307256623)
XLA Ops:
  0.6 0.7 broadcast_multiply_fusion
  1.3 0.1 and_convert_fusion
  1.4 0.9 convert_bitcast_fusion
  2.3 0.7 pad.4.own
  3.0 0.7 broadcast_in_dim.2.mask.mask_next
  3.7 34.7 %gather_weights.1 = (f32[5,320,128]{2,1,0:T(8,128)}, f32[3,320]{1,0:T(4,128)}, bf16[320,320]{1,0:T(8,128)(2,1)}, bf16[320,336]{1,0:T(8,128)(2,1)}, bf16[4,320,32...) custom-call(bf16[416,128]{1,0:T(8,128)(2,1)} %pad.4.own), custom_call_target="tpu_custom_call" | custom-call | tf_op jit(solution)/shard_map/gather_weights/pallas_call | solution.py:741
  38.4 40.7 %attention_forward.1 = (bf16[2,336,2304]{2,1,0:T(8,128)(2,1)}, bf16[2,4,576,320]{3,2,1,0:T(8,128)(2,1)}, f32[2,576,320]{2,1,0:T(8,128)}, bf16[2,576,384]{2,1,0:T...) custom-call(s32[2]{0:T(128)} %sides.3, ...), custom_call_target="tpu_custom_call" | custom-call | tf_op jit(solution)/shard_map/attention_forward/pallas_call | solution.py:201
  79.1 90.8 %feed_forward.1 = (bf16[2,320,2304]{2,1,0:T(8,128)(2,1)}, f32[2,320,2304]{2,1,0:T(8,128)}, f32[336,1280]{1,0:T(8,128)}, f32[320,1280]{1,0:T(8,128)}, f32[80,1280]{1,0:T(8,128)}, /*index=5*/f32[320,128]{1,0:T(8,128)}) custom-call(bf16[2,336,2304]{2,1,0:T(8,128)(2,1)} %get-tuple-element.49.post_next.post, bf16[2,320,2304]{2,1,0:T(8,128)(2,1)} %bitcast.14, ...), custom_call_target="tpu_custom_call" | custom-call | tf_op jit(solution)/shard_map/feed_forward/pallas_call | solution.py:434
  169.9 80.0 %attention_backward.1 = (f32[2,320,2304]{2,1,0:T(8,128)}, f32[336,320]{1,0:T(8,128)}, f32[336,320]{1,0:T(8,128)}, f32[640,384]{1,0:T(8,128)}, f32[4,320,320]{2,1...) custom-call(s32[2]{0:T(128)} %sides.3, bf16[2,320,2304]{2,1,0:T(8,128)(2,1)} %bitcast.19, ...), custom_call_target="tpu_custom_call" | custom-call | tf_op jit(solution)/shard_map/attention_backward/pallas_call | solution.py:586
  249.8 10.6 %pack_gradients.1 = bf16[32,416,128]{2,1,0:T(8,128)(2,1)} custom-call(f32[336,1280]{1,0:T(8,128)} %get-tuple-element.66.gwe, f32[320,1280]{1,0:T(8,128)} %get-tuple-element.67.gwst, f32[80,1280]{1,0:T(8,128)} %get-tuple-element.68.gtaps, f32[320,128]{1,0:T(8,128)} %get-tuple-element.69.gbias, f32[336,320]{1,0:T(8,128)} %get-tuple-element.70.gwo, ...), custom_call_target="tpu_custom_call" | custom-call | tf_op jit(solution)/shard_map/pack_gradients/pallas_call | solution.py:1114
  260.4 0.0 copy-start
  260.5 0.0 copy-start.1
  260.5 0.0 copy-start.2
  260.5 33.5 %reduce_gradients.1 = (f32[416,128]{1,0:T(8,128)}, f32[8,128]{1,0:T(8,128)}) custom-call(bf16[2,4,4,416,128]{4,3,2,1,0:T(8,128)(2,1)} %bitcast.17), custom_call_target="tpu_custom_call" | custom-call | tf_op jit(solution)/shard_map/reduce_gradients/pallas_call | solution.py:863
  294.0 1.3 reduce_sum.9
  296.0 0.0 copy-done
  296.0 0.0 copy-done.1
  296.0 0.0 copy-done.2
  296.0 1.9 multiply_subtract_fusion
  (1 shorter events, 0.0 us)
Async XLA Ops:
  260.4 35.5 %copy-start = (f32[51840]{0:T(1024)S(1)}, f32[51840]{0:T(1024)}, u32[]{:S(2)}) copy-start(f32[51840]{0:T(1024)} %param.10) | copy-start | bytes 622084
  260.5 35.5 %copy-start.1 = (f32[51840]{0:T(1024)S(1)}, f32[51840]{0:T(1024)}, u32[]{:S(2)}) copy-start(f32[51840]{0:T(1024)} %param.12) | copy-start | bytes 622084
  260.5 35.6 %copy-start.2 = (f32[51840]{0:T(1024)S(1)}, f32[51840]{0:T(1024)}, u32[]{:S(2)}) copy-start(f32[51840]{0:T(1024)} %param.11) | copy-start | bytes 622084

commit v5 on v4

--- a/solution.py
+++ b/solution.py
@@ -30,6 +30,7 @@
 KEYS = KV * KV
 PITCH = GRID + 8
 EXT = 16
+DEPTH = 512
 LOG2E = math.log2(math.e)
 QUERY_SCALE = HEAD_DIM**-0.5 * LOG2E
 GELU_A = math.sqrt(2.0 / math.pi)
@@ -225,7 +226,7 @@
 ):
     s = pl.program_id(0)
     last = pl.num_programs(0) - 1
-    width, block = wst.shape
+    width, block = cot.shape[1], wst.shape[1]
     blocks = gwst.shape[1] // block
     halves = block // 128
     rows = 16
@@ -239,16 +240,16 @@
 
     def expand(t, padded, we, wst):
         at = tokens(t)
-        filled = mm(post_rows[at, :], we[...]).astype(BF).astype(F32)
+        filled = mm(post_rows[at, :], we[...])
         for h in range(halves):
             for r in range(rows):
                 start = pl.multiple_of((t * rows + r + 1) * PITCH + 8, 8)
                 padded[h, pl.ds(start, GRID), :] = filled[r * GRID : (r + 1) * GRID, h * 128 : (h + 1) * 128]
-        grad_act[at, :] = mm(out_grad_rows[at, :], wst[...]).astype(BF)
+        grad_act[at, :] = mm(out_grad_rows[at, :], wst[...])
 
     def finish(t, act, grad_exp):
         at = tokens(t)
-        total[:, at] += mm(wst[...], act[at, :], NT)
+        total[:, at] += mm(wst[0:width, :], act[at, :], NT)
         grad_post[0, :, at] += mm(we[0:width, :], grad_exp[at, :], NT)
         gwst[:, js_done] += mm(out_grad[:, at], act[at, :])
         gwe[:, js_done] += mm(post[0, :, at], grad_exp[at, :])
@@ -273,7 +274,7 @@
                 at = pl.ds(pl.multiple_of((t * rows + r) * GRID, GRID), GRID)
                 gelu, slope = gelu_pair(open_rows.pop(r))
                 act[at, hs] = gelu
-                grad = (grad_act[at, hs] * slope).astype(F32)
+                grad = (grad_act[at, hs].astype(BF) * slope).astype(F32)
                 start = pl.multiple_of((t * rows + r + 1) * PITCH + 8, 8)
                 grad_padded[h, pl.ds(start, GRID), :] = grad
                 sums = sums + fold_rows(grad)
@@ -320,7 +321,7 @@
 
     @pl.when(s == 0)
     def _():
-        for ref in (padded_0, padded_1, grad_padded, act_1, grad_exp_1, out_grad, gwe, gwst, gtaps, gbias, post_rows):
+        for ref in (padded_0, padded_1, grad_padded, act_1, grad_exp_1, out_grad, gwe, gwst, gtaps, gbias, post_rows, out_grad_rows):
             ref[...] = jnp.zeros_like(ref)
 
     @pl.when((s == 0) | ((lax.rem(s + 1, blocks) == 0) & (s + 1 < last)))
@@ -329,7 +330,7 @@
             at = slice(t * 384, (t + 1) * 384)
             grad = cot_next[0, :, at].astype(F32) * mask_next[0, 0:1, at]
             gbias[...] += grad[:, 0:128] + grad[:, 128:256] + grad[:, 256:384]
-            out_grad_rows[at, :] = grad.astype(BF).T
+            out_grad_rows[at, 0:width] = grad.astype(BF).T
             post_rows[at, 0 : width + EXT] = post_next[0, :, at].T
 
     @pl.when(lax.rem(s, blocks) == min(1, blocks - 1))
@@ -441,10 +442,11 @@
         out_specs=[image(x, behind) for x in outs[:2]] + [whole(x) for x in outs[2:]],
         out_shape=outs,
         scratch_shapes=[pltpu.VMEM((block // 128, (GRID + 2) * PITCH + 8, 128), F32)] * 3
-        + [pltpu.VMEM((tokens, block), BF)] * 5
+        + [pltpu.VMEM((tokens, block), F32)]
+        + [pltpu.VMEM((tokens, block), BF)] * 4
         + [
-            pltpu.VMEM((tokens, width + 64), BF),
-            pltpu.VMEM((tokens, width), BF),
+            pltpu.VMEM((tokens, DEPTH), BF),
+            pltpu.VMEM((tokens, DEPTH), BF),
             pltpu.VMEM((width, tokens), BF),
             pltpu.VMEM((width, tokens), F32),
         ],
@@ -632,11 +634,13 @@
     def along_z(self, k):
         return self.at_z((self.z + k) % 4)
 
-    def greet(self, partners):
+    def call(self, partners):
         barrier = pltpu.get_barrier_semaphore()
         for device in partners:
             pl.semaphore_signal(barrier, inc=1, device_id=device, device_id_type=MESH)
-        pl.semaphore_wait(barrier, len(partners))
+
+    def answer(self, count):
+        pl.semaphore_wait(pltpu.get_barrier_semaphore(), count)
 
 
 class Sender:
@@ -670,7 +674,8 @@
     send = Sender(send_sem, recv_sem)
     copy = pltpu.make_async_copy(own, slots.at[me.core, me.dp, me.z], own_sem)
     copy.start()
-    me.greet([me.beside_core, me.beside_x, me.beside_y] + [me.at_z(z) for z in me.others])
+    me.call([me.beside_core, me.beside_x, me.beside_y] + [me.at_z(z) for z in me.others])
+    me.answer(6)
     own_slot = slots.at[me.core, me.dp, me.z]
 
     def send_z(j):
@@ -760,28 +765,39 @@
     return dict(zip(outs, values, strict=True))
 
 
-def reduce_kernel(
-    grads, shard, squares,
-    core_in, y_in, x_in, x_last, y_last, z_in, small, send_sem, recv_sem,
-):
+def reduce_kernel(slot_rows, bases, *refs):
+    grads, (shard, squares) = refs[:10], refs[10:12]
+    wide, line, own, core_out, core_in, y_in, x_in, x_last, y_last, z_in, small, send_sem, recv_sem = refs[12:]
     me = Place()
-    rows = grads.shape[3]
+    rows = shard.shape[0]
     half = rows // 2
     first, second = pl.ds(0, half), pl.ds(half, half)
     send = Sender(send_sem, recv_sem)
     peers = [(me.dp, (me.z + k) % 4 * 2 + core) for k in range(4) for core in (me.core, me.other_core)][1:]
     planes = [me.beside_x, me.beside_y, me.across]
-    me.greet(peers + planes)
+    me.call(peers + planes)
+    collect_gradients(bases, wide, *grads)
+    line[...] = jnp.zeros_like(line)
+    me.answer(len(peers + planes))
     units = [(me.z + k) % 4 for k in (2, 1, 3, 0)]
-    core_copies = [send(grads.at[me.other_core, z], core_in.at[z], me.beside_core) for z in units]
-    y_copies, x_copies, last = [], [], []
+    core_copies, y_copies, x_copies, last = [], [], [], []
     other_x, other_y = 1 - me.x, 1 - me.y
+
+    def give(k):
+        z = units[k]
+        for dp in range(4):
+            join_slot(wide, dp * 8 + z * 2 + me.other_core, slot_rows, line)
+            core_out[z, dp] = line[...].astype(BF)
+        core_copies.append(send(core_out.at[z], core_in.at[z], me.beside_core))
+        for dp in range(4):
+            join_slot(wide, dp * 8 + z * 2 + me.core, slot_rows, line)
+            own[z, dp] = line[...]
 
     def cores(k):
         z = units[k]
         core_copies[k].wait_recv()
         for dp in range(4):
-            core_in[z, dp] = (core_in[z, dp].astype(F32) + grads[me.core, z, dp].astype(F32)).astype(BF)
+            core_in[z, dp] = (core_in[z, dp].astype(F32) + own[z, dp]).astype(BF)
         y_copies.append(
             [send(core_in.at[z, 2 * other_y + x, first], y_in.at[z, x], me.beside_y) for x in range(2)]
         )
@@ -820,9 +836,13 @@
             z_in[k, second] = high.astype(BF)
             z_copies.append(send(z_in.at[k], z_in.at[k + 3], me.at_z(z)))
 
+    give(0)
+    give(1)
     cores(0)
+    give(2)
     cores(1)
     plane(0)
+    give(3)
     cores(2)
     plane(1)
     column(0)
@@ -856,16 +876,20 @@
     send.finish()
 
 
-def reduce_slots(grads):
-    rows = grads.shape[3]
+def reduce_gradients(grads, slot_rows, rows, width):
+    bases, _ = row_bases(width, 4 * width)
     half = rows // 2
     count = 4 + 16 + 8 + 3 + 7 + 3
     return pl.pallas_call(
-        reduce_kernel,
+        partial(reduce_kernel, slot_rows, bases),
         out_shape=[jax.ShapeDtypeStruct((rows, 128), F32), jax.ShapeDtypeStruct((8, 128), F32)],
-        in_specs=[pl.BlockSpec(memory_space=pltpu.VMEM)],
+        in_specs=[pl.BlockSpec(memory_space=pltpu.VMEM)] * len(grads),
         out_specs=[pl.BlockSpec(memory_space=pltpu.VMEM)] * 2,
         scratch_shapes=[
+            pltpu.VMEM((3, -(-32 * slot_rows * 128 // width // 8) * 8 + 8, 128), F32),
+            pltpu.VMEM((rows, 128), F32),
+            pltpu.VMEM((4, 4, rows, 128), F32),
+            pltpu.VMEM((4, 4, rows, 128), BF),
             pltpu.VMEM((4, 4, rows, 128), BF),
             pltpu.VMEM((4, 2, half, 128), BF),
             pltpu.VMEM((4, 2, half, 128), BF),
@@ -880,7 +904,7 @@
             collective_id=1, has_side_effects=True, vmem_limit_bytes=VMEM_BYTES
         ),
         name="reduce_gradients",
-    )(grads)
+    )(*grads)
 
 
 def layout_shapes(model_width, hidden_width):
@@ -997,11 +1021,12 @@
     wo[...] = out.astype(BF)
     wot[...] = bordered(out, take(bases["output_bias"], 1), EXT).T.astype(BF)
     we[0:width, :] = take_hidden(bases["expand_weight"], width).astype(BF)
-    we[width : width + 64, :] = first_row(take_hidden(bases["expand_bias"], 1), 64).astype(BF)
+    we[width:DEPTH, :] = first_row(take_hidden(bases["expand_bias"], 1), DEPTH - width).astype(BF)
     taps[0:9, :] = take_hidden(bases["spatial_weight"], 9)
     taps[9:10, :] = take_hidden(bases["spatial_bias"], 1)
+    wst[width:DEPTH, :] = jnp.zeros((DEPTH - width, hidden), BF)
     for k in range(hidden // 128):
-        wst[:, 128 * k : 128 * k + 128] = take(bases["shrink_weight"] + 128 * k, 128).T.astype(BF)
+        wst[0:width, 128 * k : 128 * k + 128] = take(bases["shrink_weight"] + 128 * k, 128).T.astype(BF)
 
 
 def wide_rows(count):
@@ -1022,8 +1047,8 @@
         wvt=shape((width, width + 64), BF),
         wo=shape((width, width), BF),
         wot=shape((width, width + EXT), BF),
-        we=shape((width + 64, hidden), BF),
-        wst=shape((width, hidden), BF),
+        we=shape((DEPTH, hidden), BF),
+        wst=shape((DEPTH, hidden), BF),
         taps=shape((10, hidden), F32),
     )
 
@@ -1044,18 +1069,12 @@
     return dict(zip(outs, values, strict=True))
 
 
-def pack_kernel(
-    order, slot_rows, bases,
-    gwe, gwst, gtaps, gbias, gwo, gwq, gpair, gwr, gcols, grows, slots,
-    flat, wide,
-):
+def collect_gradients(bases, wide, gwe, gwst, gtaps, gbias, gwo, gwq, gpair, gwr, gcols, grows):
     width = gwst.shape[0]
     hidden = gwst.shape[1]
     used = bases["shrink_bias"] + 1
     for k in range(3):
         wide[k, pl.ds(used, wide.shape[1] - used), :] = jnp.zeros((wide.shape[1] - used, 128), F32)
-    done = wide.shape[1] * width // 128
-    flat[done:, :] = jnp.zeros((flat.shape[0] - done, 128), F32)
 
     def put(base, value, stride=1):
         count = value.shape[0]
@@ -1085,21 +1104,50 @@
         put(bases["spatial_weight"] + q, sums[:, q * width : (q + 1) * width], hidden // width)
     for k in range(hidden // 128):
         put(bases["shrink_weight"] + 128 * k, gwst[:, 128 * k : 128 * k + 128].T)
+
+def join_lines(read, write, low):
+    turned = [pltpu.roll(read(1, k), 64, 1) for k in range(3)]
+    write(0, read(0, 0))
+    write(1, read(0, 1))
+    write(2, jnp.where(low, read(0, 2), turned[0]))
+    write(3, jnp.where(low, turned[0], turned[1]))
+    write(4, jnp.where(low, turned[1], turned[2]))
+
+
+def join_slot(wide, slot, slot_rows, line):
+    pairs = slot_rows // 5
+
+    def part(start, count):
+        low = lax.broadcasted_iota(jnp.int32, (count, 128), 1) < 64
+
+        def read(parity, k):
+            return wide[k, pl.ds(slot * (2 * pairs) + 2 * start + parity, count, stride=2), :]
+
+        def write(k, value):
+            line[pl.ds(5 * start + k, count, stride=5), :] = value
+
+        join_lines(read, write, low)
+
+    part(0, pairs // 8 * 8)
+    if pairs % 8:
+        part(pairs // 8 * 8, pairs % 8)
+
+
+def pack_kernel(order, slot_rows, bases, *refs):
+    grads, (slots, flat, wide) = refs[:10], refs[10:]
+    collect_gradients(bases, wide, *grads)
+    done = wide.shape[1] * 5 // 2
+    flat[done:, :] = jnp.zeros((flat.shape[0] - done, 128), F32)
     low = lax.broadcasted_iota(jnp.int32, (SPAN, 128), 1) < 64
 
     def regroup(t, _):
-        even = pl.ds(t * (2 * SPAN), SPAN, stride=2)
-        odd = pl.ds(t * (2 * SPAN) + 1, SPAN, stride=2)
-        turned = [pltpu.roll(wide[k, odd, :], 64, 1) for k in range(3)]
-        part = [
-            wide[0, even, :],
-            wide[1, even, :],
-            jnp.where(low, wide[2, even, :], turned[0]),
-            jnp.where(low, turned[0], turned[1]),
-            jnp.where(low, turned[1], turned[2]),
-        ]
-        for k in range(5):
-            flat[pl.ds(t * (5 * SPAN) + k, SPAN, stride=5), :] = part[k]
+        def read(parity, k):
+            return wide[k, pl.ds(t * (2 * SPAN) + parity, SPAN, stride=2), :]
+
+        def write(k, value):
+            flat[pl.ds(t * (5 * SPAN) + k, SPAN, stride=5), :] = value
+
+        join_lines(read, write, low)
         return 0
 
     lax.fori_loop(0, wide.shape[1] // (2 * SPAN), regroup, 0)
@@ -1157,12 +1205,10 @@
         images.transpose(0, 2, 1), cotangent.transpose(0, 2, 1), kv_sides, weights
     )
     if on_grid:
-        order = [s % 2 * 16 + s % 8 // 2 * 4 + s // 8 for s in range(32)]
-    slots = pack_gradients(grads, order, slot_rows, padded_rows, width)
-    if on_grid:
-        shard, squares = reduce_slots(slots.reshape(2, 4, 4, padded_rows, 128))
+        shard, squares = reduce_gradients(grads, slot_rows, padded_rows, width)
         squares = jnp.sum(squares)
     else:
+        slots = pack_gradients(grads, order, slot_rows, padded_rows, width)
         shard = lax.psum_scatter(slots.astype(F32), axes)
         squares = lax.psum(jnp.sum(shard * shard), axes)
     shard = shard[:slot_rows].reshape(-1)

time: 303 us -> 282 us (0.931)
  Pallas kernels: 290 us -> 269 us
    pallas_call x1, Pallas kernels: 90.8 us -> 78.1 us  [feed_forward(): pl.pallas_call(feed_forward_kernel, grid=(count + 1,), in_specs=[image(x,...]
    pallas_call x2 -> x1, Pallas kernels: 44.1 us -> 35.8 us  [reduce_gradients(): pl.pallas_call(partial(reduce_kernel, slot_rows, bases), out_shape=[jax.S...]
where the time goes in v5:
time: 282 us; the launch traced here: 278 us
  Pallas kernels  269 us (95%)
  other arithmetic  4.84 us (2%)
    pallas_call x1, Pallas kernels, attention_backward(): pl.pallas_call(attention_backward_kernel, grid_spec=pltpu.PrefetchScalarG...  79.9 us
    pallas_call x1, Pallas kernels, feed_forward(): pl.pallas_call(feed_forward_kernel, grid=(count + 1,), in_specs=[image(x,...  78.1 us
    pallas_call x1, Pallas kernels, attention_forward(): pl.pallas_call(attention_forward_kernel, grid_spec=pltpu.PrefetchScalarGr...  40.7 us
    pallas_call x1, Pallas kernels, reduce_gradients(): pl.pallas_call(partial(reduce_kernel, slot_rows, bases), out_shape=[jax.S...  35.8 us
    pallas_call x1, Pallas kernels, gather_weights(): pl.pallas_call(partial(gather_kernel, slot_rows, bases), out_shape=list(o...  35 us

profile of v5, /device:TPU:0, one launch (start us, length us, event | category | flops | bytes accessed | tf_op | source)
XLA Modules:
  0.0 278.4 jit_solution(1525510287497566440)
XLA Ops:
  0.6 0.7 broadcast_multiply_fusion
  1.3 0.1 and_convert_fusion
  1.4 0.9 convert_bitcast_fusion
  2.3 0.7 pad.4.own
  3.0 0.7 broadcast_in_dim.2.mask.mask_next
  3.7 35.0 %gather_weights.1 = (f32[5,320,128]{2,1,0:T(8,128)}, f32[3,320]{1,0:T(4,128)}, bf16[320,320]{1,0:T(8,128)(2,1)}, bf16[320,336]{1,0:T(8,128)(2,1)}, bf16[4,320,32...) custom-call(bf16[416,128]{1,0:T(8,128)(2,1)} %pad.4.own), custom_call_target="tpu_custom_call" | custom-call | tf_op jit(solution)/shard_map/gather_weights/pallas_call | solution.py:746
  38.6 40.7 %attention_forward.1 = (bf16[2,336,2304]{2,1,0:T(8,128)(2,1)}, bf16[2,4,576,320]{3,2,1,0:T(8,128)(2,1)}, f32[2,576,320]{2,1,0:T(8,128)}, bf16[2,576,384]{2,1,0:T...) custom-call(s32[2]{0:T(128)} %sides.3, ...), custom_call_target="tpu_custom_call" | custom-call | tf_op jit(solution)/shard_map/attention_forward/pallas_call | solution.py:202
  79.3 78.1 %feed_forward.1 = (bf16[2,320,2304]{2,1,0:T(8,128)(2,1)}, f32[2,320,2304]{2,1,0:T(8,128)}, f32[336,1280]{1,0:T(8,128)}, f32[320,1280]{1,0:T(8,128)}, f32[80,1280]{1,0:T(8,128)}, /*index=5*/f32[320,128]{1,0:T(8,128)}) custom-call(bf16[2,336,2304]{2,1,0:T(8,128)(2,1)} %get-tuple-element.49.post_next.post, bf16[2,320,2304]{2,1,0:T(8,128)(2,1)} %bitcast.13, ...), custom_call_target="tpu_custom_call" | custom-call | tf_op jit(solution)/shard_map/feed_forward/pallas_call | solution.py:435
  157.4 79.9 %attention_backward.1 = (f32[2,320,2304]{2,1,0:T(8,128)}, f32[336,320]{1,0:T(8,128)}, f32[336,320]{1,0:T(8,128)}, f32[640,384]{1,0:T(8,128)}, f32[4,320,320]{2,1...) custom-call(s32[2]{0:T(128)} %sides.3, bf16[2,320,2304]{2,1,0:T(8,128)(2,1)} %bitcast.17, ...), custom_call_target="tpu_custom_call" | custom-call | tf_op jit(solution)/shard_map/attention_backward/pallas_call | solution.py:588
  237.3 0.0 copy-start
  237.3 0.0 copy-start.1
  237.4 0.0 copy-start.2
  237.4 35.8 %reduce_gradients.1 = (f32[416,128]{1,0:T(8,128)}, f32[8,128]{1,0:T(8,128)}) custom-call(f32[336,1280]{1,0:T(8,128)} %get-tuple-element.66.refs_0_, f32[320,1280]{1,0:T(8,128)} %get-tuple-element.67.refs_1_, f32[80,1280]{1,0:T(8,128)} %get-tuple-element.68.refs_2_, f32[320,128]{1,0:T(8,128)} %get-tuple-element.69.refs_3_, ...), custom_call_target="tpu_custom_call" | custom-call | tf_op jit(solution)/shard_map/reduce_gradients/pallas_call | solution.py:883
  273.2 1.3 reduce_sum.9
  275.2 0.0 copy-done
  275.2 0.0 copy-done.1
  275.2 0.0 copy-done.2
  275.2 1.9 multiply_subtract_fusion
  (1 shorter events, 0.0 us)
Async XLA Ops:
  237.3 37.9 %copy-start = (f32[51840]{0:T(1024)S(1)}, f32[51840]{0:T(1024)}, u32[]{:S(2)}) copy-start(f32[51840]{0:T(1024)} %param.10) | copy-start | bytes 622084
  237.3 37.9 %copy-start.1 = (f32[51840]{0:T(1024)S(1)}, f32[51840]{0:T(1024)}, u32[]{:S(2)}) copy-start(f32[51840]{0:T(1024)} %param.12) | copy-start | bytes 622084
  237.4 37.9 %copy-start.2 = (f32[51840]{0:T(1024)S(1)}, f32[51840]{0:T(1024)}, u32[]{:S(2)}) copy-start(f32[51840]{0:T(1024)} %param.11) | copy-start | bytes 622084

commit v6 on v5

--- a/solution.py
+++ b/solution.py
@@ -131,13 +131,13 @@
             normed, _unused = norm_columns(x)
             pre[0, 0:width, at] = (normed * vec[0] + vec[1]).astype(BF)
             pre[0, width : width + EXT, at] = first_row(jnp.ones((1, 128), F32)).astype(BF)
-        at = pl.ds(pl.multiple_of(t * 384, 128), 384)
-        picked = mm(perm[...], pre[0, 0:width, at], NT).astype(BF)
+        return 0
+
+    lax.fori_loop(0, TOKENS // 384, first_norm, 0)
+    for t in range(TOKENS // 384):
+        picked = mm(perm[...], pre[0, 0:width, t * 384 : (t + 1) * 384], NT).astype(BF)
         for p in range(4):
-            patches[0, p, pl.ds(pl.multiple_of(t * 96, 32), 96), :] = picked[p * 96 : (p + 1) * 96]
-        return 0
-
-    lax.fori_loop(0, TOKENS // 384, first_norm, 0)
+            patches[0, p, t * 96 : (t + 1) * 96, :] = picked[p * 96 : (p + 1) * 96]
 
     total = rows[0:1, :]
     for p in range(4):
@@ -169,13 +169,13 @@
         mixed[0, at, :] = (out[0:HEAD_DIM] * (1.0 / total)).astype(BF)
         lse[0, h : h + 1, :] = top + jnp.log2(total)
 
+    middle[0] = mm(wot[...], mixed[0])
+
     def second_norm(t, _):
-        at = pl.ds(pl.multiple_of(t * 384, 128), 384)
-        branch = mm(wot[...], mixed[0, :, at])
         for u in range(3):
             at = pl.ds(pl.multiple_of(t * 384 + u * 128, 128), 128)
             here = mask[0, 0:1, at]
-            x = images[0, :, at].astype(F32) * here + branch[:, u * 128 : (u + 1) * 128]
+            x = images[0, :, at].astype(F32) * here + middle[0, :, at]
             middle[0, :, at] = x
             normed, _unused = norm_columns(x)
             post[0, 0:width, at] = ((normed * vec[2] + vec[3]) * here).astype(BF)
@@ -257,7 +257,7 @@
     def convolve(t, padded, act):
         for h in range(halves):
             hs = slice(h * 128, (h + 1) * 128)
-            w = [jnp.broadcast_to(taps[k : k + 1, hs], (GRID, 128)).astype(BF) for k in range(10)]
+            w = [jnp.broadcast_to(0.5 * taps[k : k + 1, hs], (GRID, 128)).astype(BF) for k in range(10)]
             sums = jnp.zeros((8, 128), F32)
             open_rows = {}
             for q in range(-1, rows + 1):
@@ -305,11 +305,10 @@
                         k = 3 * a + b
                         product = x[r] * grads[b]
                         product = product[0:16] + product[16:32] + product[32:48]
-                        if k in waiting:
-                            product = (product + waiting.pop(k)).astype(F32)
+                        waiting[k] = waiting[k] + product if k in waiting else product
+                        if r % 4 == 3:
+                            product = waiting.pop(k).astype(F32)
                             sums[k] = sums[k] + product[0:8] + product[8:16]
-                        else:
-                            waiting[k] = product
                 r = q - 1
                 if r >= 0:
                     at = pl.ds(pl.multiple_of((t * rows + r) * GRID, GRID), GRID)
@@ -321,8 +320,16 @@
 
     @pl.when(s == 0)
     def _():
-        for ref in (padded_0, padded_1, grad_padded, act_1, grad_exp_1, out_grad, gwe, gwst, gtaps, gbias, post_rows, out_grad_rows):
+        for ref in (act_1, grad_exp_1, out_grad, gwe, gwst, gtaps, gbias):
             ref[...] = jnp.zeros_like(ref)
+        for ref in (post_rows, out_grad_rows):
+            ref[:, 256:DEPTH] = jnp.zeros((TOKENS, DEPTH - 256), BF)
+        for ref in (padded_0, padded_1, grad_padded):
+            for h in range(halves):
+                ref[h, 0 : PITCH + 8, :] = jnp.zeros((PITCH + 8, 128), F32)
+                ref[h, (GRID + 1) * PITCH :, :] = jnp.zeros((PITCH + 8, 128), F32)
+                for r in range(1, GRID):
+                    ref[h, (r + 1) * PITCH : (r + 1) * PITCH + 8, :] = jnp.zeros((8, 128), F32)
 
     @pl.when((s == 0) | ((lax.rem(s + 1, blocks) == 0) & (s + 1 < last)))
     def _():
@@ -330,7 +337,7 @@
             at = slice(t * 384, (t + 1) * 384)
             grad = cot_next[0, :, at].astype(F32) * mask_next[0, 0:1, at]
             gbias[...] += grad[:, 0:128] + grad[:, 128:256] + grad[:, 256:384]
-            out_grad_rows[at, 0:width] = grad.astype(BF).T
+            out_grad_rows[at, 0:width] = (0.5 * grad).astype(BF).T
             post_rows[at, 0 : width + EXT] = post_next[0, :, at].T
 
     @pl.when(lax.rem(s, blocks) == min(1, blocks - 1))
@@ -396,12 +403,12 @@
             output[0, :, at] = ((middle[0, :, at] + total[:, at] + vec[4]) * mask[0, 0:1, at]).astype(BF)
 
 
-def gelu_pair(x):
-    kind = x.dtype.type
-    square = x * x
-    half = kind(0.5) * jnp.tanh(x * (kind(GELU_B) * square + kind(GELU_A))) + kind(0.5)
-    gelu = x * half
-    return gelu, half + gelu * (kind(1.0) - half) * (kind(6.0 * GELU_B) * square + kind(2.0 * GELU_A))
+def gelu_pair(half):
+    kind = half.dtype.type
+    square = half * half
+    upper = jnp.tanh(half * (kind(8.0 * GELU_B) * square + kind(2.0 * GELU_A))) + kind(1.0)
+    gelu = half * upper
+    return gelu, upper + gelu * (kind(2.0) - upper) * (kind(24.0 * GELU_B) * square + kind(2.0 * GELU_A))
 
 
 def feed_forward(post, cot, mask, middle, we, wst, taps, vec, block=256):
@@ -499,10 +506,13 @@
         key_ref[h, :, 0:HEAD_DIM] = keys[:, at]
         value_ref[h, :, 0:HEAD_DIM] = values[:, at]
 
-    span = TOKENS // 2
+    span = TOKENS // 3
     index = lax.broadcasted_iota(jnp.int32, (64, span), 0)
-    for t in range(TOKENS // span):
-        at = slice(t * span, (t + 1) * span)
+    grad_values[...] = jnp.zeros_like(grad_values)
+    grad_keys[...] = jnp.zeros_like(grad_keys)
+
+    def part(t, _):
+        at = pl.ds(pl.multiple_of(t * span, 128), span)
         for h in range(HEADS):
             hs = slice(h * HEAD_DIM, (h + 1) * HEAD_DIM)
             one, two, three = three_parts(-lse[0, h : h + 1, at])
@@ -518,15 +528,12 @@
             tail = jnp.where(index == 1, one, tail).astype(BF)
             grad_attend = mm(value_ref[h], jnp.concatenate([grad, tail], axis=0))
             grad_scores = (attend * grad_attend).astype(BF)
-            grad_value = mm(grad, low, NT)
-            grad_key = mm(query, grad_scores, NT) * (1.0 / LOG2E)
-            if t == 0:
-                grad_values[hs, :] = grad_value
-                grad_keys[hs, :] = grad_key
-            else:
-                grad_values[hs, :] += grad_value
-                grad_keys[hs, :] += grad_key
+            grad_values[hs, :] += mm(grad, low, NT)
+            grad_keys[hs, :] += mm(query, grad_scores, NT) * (1.0 / LOG2E)
             grad_queries[hs, at] = (mm(keys_t[hs, :], grad_scores) * HEAD_DIM**-0.5).astype(BF)
+        return 0
+
+    lax.fori_loop(0, TOKENS // span, part, 0)
 
     low_keys = grad_keys[...].astype(BF)
     low_values = grad_values[...].astype(BF)

time: 282 us -> 280 us (level)
    pallas_call x1, Pallas kernels: 40.7 us -> 37.4 us  [attention_forward(): pl.pallas_call(attention_forward_kernel, grid_spec=pltpu.PrefetchScalarGr...]
where the time goes in v6:
time: 280 us; the launch traced here: 276 us
  Pallas kernels  267 us (95%)
  other arithmetic  4.84 us (2%)
    pallas_call x1, Pallas kernels, attention_backward(): pl.pallas_call(attention_backward_kernel, grid_spec=pltpu.PrefetchScalarG...  81.7 us
    pallas_call x1, Pallas kernels, feed_forward(): pl.pallas_call(feed_forward_kernel, grid=(count + 1,), in_specs=[image(x,...  77.1 us
    pallas_call x1, Pallas kernels, attention_forward(): pl.pallas_call(attention_forward_kernel, grid_spec=pltpu.PrefetchScalarGr...  37.4 us
    pallas_call x1, Pallas kernels, reduce_gradients(): pl.pallas_call(partial(reduce_kernel, slot_rows, bases), out_shape=[jax.S...  35.8 us
    pallas_call x1, Pallas kernels, gather_weights(): pl.pallas_call(partial(gather_kernel, slot_rows, bases), out_shape=list(o...  35 us

profile of v6, /device:TPU:0, one launch (start us, length us, event | category | flops | bytes accessed | tf_op | source)
XLA Modules:
  0.0 275.9 jit_solution(15247542272275827220)
XLA Ops:
  0.6 0.7 broadcast_multiply_fusion
  1.3 0.1 and_convert_fusion
  1.4 0.9 convert_bitcast_fusion
  2.3 0.7 pad.4.own
  3.0 0.7 broadcast_in_dim.2.mask.mask_next
  3.7 35.0 %gather_weights.1 = (f32[5,320,128]{2,1,0:T(8,128)}, f32[3,320]{1,0:T(4,128)}, bf16[320,320]{1,0:T(8,128)(2,1)}, bf16[320,336]{1,0:T(8,128)(2,1)}, bf16[4,320,32...) custom-call(bf16[416,128]{1,0:T(8,128)(2,1)} %pad.4.own), custom_call_target="tpu_custom_call" | custom-call | tf_op jit(solution)/shard_map/gather_weights/pallas_call | solution.py:753
  38.6 37.4 %attention_forward.1 = (bf16[2,336,2304]{2,1,0:T(8,128)(2,1)}, bf16[2,4,576,320]{3,2,1,0:T(8,128)(2,1)}, f32[2,576,320]{2,1,0:T(8,128)}, bf16[2,576,384]{2,1,0:T...) custom-call(s32[2]{0:T(128)} %sides.3, ...), custom_call_target="tpu_custom_call" | custom-call | tf_op jit(solution)/shard_map/attention_forward/pallas_call | solution.py:202
  76.1 77.1 %feed_forward.1 = (bf16[2,320,2304]{2,1,0:T(8,128)(2,1)}, f32[2,320,2304]{2,1,0:T(8,128)}, f32[336,1280]{1,0:T(8,128)}, f32[320,1280]{1,0:T(8,128)}, f32[80,1280]{1,0:T(8,128)}, /*index=5*/f32[320,128]{1,0:T(8,128)}) custom-call(bf16[2,336,2304]{2,1,0:T(8,128)(2,1)} %get-tuple-element.49.post_next.post, bf16[2,320,2304]{2,1,0:T(8,128)(2,1)} %bitcast.13, ...), custom_call_target="tpu_custom_call" | custom-call | tf_op jit(solution)/shard_map/feed_forward/pallas_call | solution.py:442
  153.2 81.7 %attention_backward.1 = (f32[2,320,2304]{2,1,0:T(8,128)}, f32[336,320]{1,0:T(8,128)}, f32[336,320]{1,0:T(8,128)}, f32[640,384]{1,0:T(8,128)}, f32[4,320,320]{2,1...) custom-call(s32[2]{0:T(128)} %sides.3, bf16[2,320,2304]{2,1,0:T(8,128)(2,1)} %bitcast.17, ...), custom_call_target="tpu_custom_call" | custom-call | tf_op jit(solution)/shard_map/attention_backward/pallas_call | solution.py:595
  234.9 0.0 copy-start
  234.9 0.0 copy-start.1
  234.9 0.0 copy-start.2
  234.9 35.8 %reduce_gradients.1 = (f32[416,128]{1,0:T(8,128)}, f32[8,128]{1,0:T(8,128)}) custom-call(f32[336,1280]{1,0:T(8,128)} %get-tuple-element.66.refs_0_, f32[320,1280]{1,0:T(8,128)} %get-tuple-element.67.refs_1_, f32[80,1280]{1,0:T(8,128)} %get-tuple-element.68.refs_2_, f32[320,128]{1,0:T(8,128)} %get-tuple-element.69.refs_3_, ...), custom_call_target="tpu_custom_call" | custom-call | tf_op jit(solution)/shard_map/reduce_gradients/pallas_call | solution.py:890
  270.7 1.3 reduce_sum.9
  272.7 0.0 copy-done
  272.8 0.0 copy-done.1
  272.8 0.0 copy-done.2
  272.8 1.9 multiply_subtract_fusion
  (1 shorter events, 0.0 us)
Async XLA Ops:
  234.9 37.9 %copy-start = (f32[51840]{0:T(1024)S(1)}, f32[51840]{0:T(1024)}, u32[]{:S(2)}) copy-start(f32[51840]{0:T(1024)} %param.10) | copy-start | bytes 622084
  234.9 37.9 %copy-start.1 = (f32[51840]{0:T(1024)S(1)}, f32[51840]{0:T(1024)}, u32[]{:S(2)}) copy-start(f32[51840]{0:T(1024)} %param.12) | copy-start | bytes 622084
  234.9 37.9 %copy-start.2 = (f32[51840]{0:T(1024)S(1)}, f32[51840]{0:T(1024)}, u32[]{:S(2)}) copy-start(f32[51840]{0:T(1024)} %param.11) | copy-start | bytes 622084

commit v7 on v6

--- a/solution.py
+++ b/solution.py
@@ -97,6 +97,13 @@
     return pl.BlockSpec(x.shape, lambda *_: zeros)
 
 
+FAR = pl.BlockSpec(memory_space=pl.ANY)
+
+
+def near(x):
+    return pltpu.VMEM((1,) + tuple(x.shape[1:]), x.dtype)
+
+
 def per_image(x, **kwargs):
     zeros = (0,) * (len(x.shape) - 1)
     return pl.BlockSpec((1,) + tuple(x.shape[1:]), lambda i, *_: (i,) + zeros, **kwargs)
@@ -118,11 +125,14 @@
 
 def attention_forward_kernel(
     sides, images, mask, perm, vec, rows, wqt, wr, wk, wvt, wot,
-    pre, patches, reduced, memory, mixed, lse, middle, post,
-    key_ref, value_ref,
+    pre_far, patches_far, reduced_far, memory_far, mixed_far, lse, middle, post,
+    pre, patches, reduced, memory, mixed, key_ref, value_ref, sems,
 ):
     i = pl.program_id(0)
     width = images.shape[1]
+    far = (pre_far, patches_far, reduced_far, memory_far, mixed_far)
+    kept = (pre, patches, reduced, memory, mixed)
+    away = [pltpu.make_async_copy(y, x.at[pl.ds(i, 1)], sems.at[k]) for k, (x, y) in enumerate(zip(far, kept))]
 
     def first_norm(t, _):
         for u in range(3):
@@ -138,6 +148,8 @@
         picked = mm(perm[...], pre[0, 0:width, t * 384 : (t + 1) * 384], NT).astype(BF)
         for p in range(4):
             patches[0, p, t * 96 : (t + 1) * 96, :] = picked[p * 96 : (p + 1) * 96]
+    away[0].start()
+    away[1].start()
 
     total = rows[0:1, :]
     for p in range(4):
@@ -147,6 +159,8 @@
     memory[0, :, 0:width] = (normed * rows[1:2, :] + rows[2:3, :]).astype(BF)
     lane = lax.broadcasted_iota(jnp.int32, (KEYS, 64), 1)
     memory[0, :, width : width + 64] = jnp.where(lane == 0, 1.0, 0.0).astype(BF)
+    away[2].start()
+    away[3].start()
     keys = mm(memory[0, :, 0:width], wk[...]).astype(BF)
     key_columns(key_ref, sides[i], range(HEADS), 1, 0, True)
     values = mm(wvt[...], memory[0], NT).astype(BF)
@@ -169,6 +183,7 @@
         mixed[0, at, :] = (out[0:HEAD_DIM] * (1.0 / total)).astype(BF)
         lse[0, h : h + 1, :] = top + jnp.log2(total)
 
+    away[4].start()
     middle[0] = mm(wot[...], mixed[0])
 
     def second_norm(t, _):
@@ -183,6 +198,8 @@
         return 0
 
     lax.fori_loop(0, TOKENS // 384, second_norm, 0)
+    for copy in away:
+        copy.wait()
 
 
 def attention_forward(sides, images, mask, perm, vec, rows, wqt, wr, wk, wvt, wot):
@@ -205,10 +222,12 @@
             num_scalar_prefetch=1,
             grid=(n,),
             in_specs=[per_image(images), per_image(mask)] + [whole(x) for x in weights],
-            out_specs=[per_image(x) for x in outs],
-            scratch_shapes=[
+            out_specs=[FAR] * 5 + [per_image(x) for x in outs[5:]],
+            scratch_shapes=[near(x) for x in outs[:5]]
+            + [
                 pltpu.VMEM((HEADS, KEYS, 128), BF),
                 pltpu.VMEM((HEADS, HEAD_DIM + EXT, KEYS), BF),
+                pltpu.SemaphoreType.DMA((5,)),
             ],
         ),
         out_shape=outs,
@@ -219,10 +238,10 @@
 
 def feed_forward_kernel(
     post_next, cot_next, mask_next, we_next, wst_next, taps,
-    post, cot, mask, middle, we, wst, vec,
+    post, cot, mask, middle_far, we, wst, vec,
     output, grad_post, gwe, gwst, gtaps, gbias,
     padded_0, padded_1, grad_padded, grad_act, act_0, act_1, grad_exp_0, grad_exp_1,
-    post_rows, out_grad_rows, out_grad, total,
+    post_rows, out_grad_rows, out_grad, total, middle, middle_sem,
 ):
     s = pl.program_id(0)
     last = pl.num_programs(0) - 1
@@ -340,13 +359,16 @@
             out_grad_rows[at, 0:width] = (0.5 * grad).astype(BF).T
             post_rows[at, 0 : width + EXT] = post_next[0, :, at].T
 
-    @pl.when(lax.rem(s, blocks) == min(1, blocks - 1))
+    fetch = pltpu.make_async_copy(middle_far.at[pl.ds(jnp.maximum(s - 1, 0) // blocks, 1)], middle, middle_sem)
+
+    @pl.when(lax.rem(s, blocks) == 1)
     def _():
+        fetch.start()
         for t in range(TOKENS // 384):
             at = slice(t * 384, (t + 1) * 384)
             out_grad[:, at] = (cot[0, :, at].astype(F32) * mask[0, 0:1, at]).astype(BF)
 
-    @pl.when((s == 0) | (lax.rem(s, blocks) == min(1, blocks - 1)))
+    @pl.when((s == 0) | (lax.rem(s, blocks) == 1))
     def _():
         total[...] = jnp.zeros_like(total)
         grad_post[...] = jnp.zeros_like(grad_post)
@@ -398,6 +420,7 @@
 
     @pl.when((s > 0) & (lax.rem(s, blocks) == 0))
     def _():
+        fetch.wait()
         for t in range(TOKENS // 128):
             at = slice(t * 128, (t + 1) * 128)
             output[0, :, at] = ((middle[0, :, at] + total[:, at] + vec[4]) * mask[0, 0:1, at]).astype(BF)
@@ -444,8 +467,8 @@
         grid=(count + 1,),
         in_specs=[image(x, ahead) for x in (post, cot, mask)]
         + [columns(we, ahead), columns(wst, ahead), columns(taps, lambda s: jnp.minimum(s, count - 1))]
-        + [image(x, behind) for x in (post, cot, mask, middle)]
-        + [columns(we, behind), columns(wst, behind), whole(vec)],
+        + [image(x, behind) for x in (post, cot, mask)]
+        + [FAR, columns(we, behind), columns(wst, behind), whole(vec)],
         out_specs=[image(x, behind) for x in outs[:2]] + [whole(x) for x in outs[2:]],
         out_shape=outs,
         scratch_shapes=[pltpu.VMEM((block // 128, (GRID + 2) * PITCH + 8, 128), F32)] * 3
@@ -456,6 +479,8 @@
             pltpu.VMEM((tokens, DEPTH), BF),
             pltpu.VMEM((width, tokens), BF),
             pltpu.VMEM((width, tokens), F32),
+            near(middle),
+            pltpu.SemaphoreType.DMA(()),
         ],
         compiler_params=pltpu.CompilerParams(vmem_limit_bytes=VMEM_BYTES),
         name="feed_forward",
@@ -463,13 +488,19 @@
 
 
 def attention_backward_kernel(
-    sides, images, cot, mask, pre, patches, reduced, memory, mixed, lse, middle, grad_post,
+    sides, mixed_far, pre_far, memory_far, reduced_far, patches_far, images_far, cot, mask, lse, middle, grad_post,
     perm, vec, rows, wq, wqt, wr, wk, wv, wvt, wo,
     grad_images, gwo, gwq, gpair, gwr, gcols, grows,
     branch, grad_mixed, queries, grad_queries, key_ref, value_ref, keys_t, grad_keys, grad_values, grad_patches,
+    mixed, pre, memory, reduced, patches, images, sems,
 ):
     i = pl.program_id(0)
-    width = images.shape[1]
+    width = cot.shape[1]
+    far = (mixed_far, pre_far, memory_far, reduced_far, patches_far, images_far)
+    kept = (mixed, pre, memory, reduced, patches, images)
+    fetch = [pltpu.make_async_copy(x.at[pl.ds(i, 1)], y, sems.at[k]) for k, (x, y) in enumerate(zip(far, kept))]
+    for copy in fetch:
+        copy.start()
 
     @pl.when(i == 0)
     def _():
@@ -493,9 +524,12 @@
         return 0
 
     lax.fori_loop(0, TOKENS // 384, mlp_norm_back, 0)
+    fetch[0].wait()
     gwo[...] += mm(mixed[0], branch[...], NT)
     grad_mixed[...] = mm(wo[...], branch[...]).astype(BF)
+    fetch[1].wait()
     queries[...] = (mm(wqt[...], pre[0]) * QUERY_SCALE).astype(BF)
+    fetch[2].wait()
     keys = mm(memory[0, :, 0:width], wk[...]).astype(BF)
     keys_t[...] = keys.T
     values = mm(wvt[...], memory[0], NT).astype(BF).T
@@ -540,12 +574,14 @@
     gpair[0:width, :] += mm(low_keys, memory[0])
     gpair[width : 2 * width, :] += mm(low_values, memory[0])
     grad_memory = mm(low_keys.T, wk[...], NT) + mm(low_values.T, wv[...], NT)
+    fetch[3].wait()
     normed, rstd = norm_rows(reduced[0])
     grows[8:16, :] += fold_rows(grad_memory * normed)
     grows[16:24, :] += fold_rows(grad_memory)
     grad_reduced = norm_rows_back(normed, rstd, grad_memory * rows[1:2, :]).astype(BF)
     grows[0:8, :] += fold_rows(grad_reduced.astype(F32))
     grad_reduced_t = grad_reduced.T
+    fetch[4].wait()
     for p in range(4):
         gwr[p] += mm(grad_reduced_t, patches[0, p])
         grad_patches[p] = mm(grad_reduced, wr[p], NT).astype(BF)
@@ -571,6 +607,7 @@
         gcols[1] += shift
         return 0
 
+    fetch[5].wait()
     lax.fori_loop(0, TOKENS // 384, pre_norm_back, 0)
 
 
@@ -590,16 +627,15 @@
         shape((24, width), F32),
     ]
     one = {"pipeline_mode": pl.Buffered(1)}
-    inputs = (images, cot, mask, pre, patches, reduced, memory, mixed, lse)
+    far = (mixed, pre, memory, reduced, patches, images)
+    inputs = (cot, mask, lse, middle, grad_post)
     weights = (perm, vec, rows, wq, wqt, wr, wk, wv, wvt, wo)
     return pl.pallas_call(
         attention_backward_kernel,
         grid_spec=pltpu.PrefetchScalarGridSpec(
             num_scalar_prefetch=1,
             grid=(n,),
-            in_specs=[per_image(x) for x in inputs]
-            + [per_image(middle, **one), per_image(grad_post, **one)]
-            + [whole(x) for x in weights],
+            in_specs=[FAR] * 6 + [per_image(x) for x in inputs] + [whole(x) for x in weights],
             out_specs=[per_image(outs[0], **one)] + [whole(x) for x in outs[1:]],
             scratch_shapes=[
                 pltpu.VMEM((width, tokens), BF),
@@ -612,12 +648,14 @@
                 pltpu.VMEM((width, KEYS), F32),
                 pltpu.VMEM((width, KEYS), F32),
                 pltpu.VMEM((4, KEYS, width), BF),
-            ],
+            ]
+            + [near(x) for x in far]
+            + [pltpu.SemaphoreType.DMA((6,))],
         ),
         out_shape=outs,
         compiler_params=pltpu.CompilerParams(vmem_limit_bytes=VMEM_BYTES),
         name="attention_backward",
-    )(sides, *inputs, middle, grad_post, *weights)
+    )(sides, *far, *inputs, *weights)
 
 MESH = pl.DeviceIdType.MESH
 

time: 280 us -> 273 us (0.975)
  Pallas kernels: 267 us -> 261 us
    pallas_call x1, Pallas kernels: 81.7 us -> 78 us  [attention_backward(): pl.pallas_call(attention_backward_kernel, grid_spec=pltpu.PrefetchScalarG...]
where the time goes in v7:
time: 273 us; the launch traced here: 269 us
  Pallas kernels  261 us (96%)
  other arithmetic  4.84 us (2%)
  between operations  2.78 us (1%)
    pallas_call x1, Pallas kernels, attention_backward(): pl.pallas_call(attention_backward_kernel, grid_spec=pltpu.PrefetchScalarG...  78 us
    pallas_call x1, Pallas kernels, feed_forward(): pl.pallas_call(feed_forward_kernel, grid=(count + 1,), in_specs=[image(x,...  76.1 us
    pallas_call x1, Pallas kernels, reduce_gradients(): pl.pallas_call(partial(reduce_kernel, slot_rows, bases), out_shape=[jax.S...  35.8 us
    pallas_call x1, Pallas kernels, attention_forward(): pl.pallas_call(attention_forward_kernel, grid_spec=pltpu.PrefetchScalarGr...  35.6 us
    pallas_call x1, Pallas kernels, gather_weights(): pl.pallas_call(partial(gather_kernel, slot_rows, bases), out_shape=list(o...  35 us

profile of v7, /device:TPU:0, one launch (start us, length us, event | category | flops | bytes accessed | tf_op | source)
XLA Modules:
  0.0 269.5 jit_solution(13314801202565824137)
XLA Ops:
  0.6 0.7 broadcast_multiply_fusion
  1.3 0.1 and_convert_fusion
  1.4 0.9 convert_bitcast_fusion
  2.3 0.7 pad.4.own
  3.0 0.7 broadcast_in_dim.2.mask.mask_next
  3.7 35.0 %gather_weights.1 = (f32[5,320,128]{2,1,0:T(8,128)}, f32[3,320]{1,0:T(4,128)}, bf16[320,320]{1,0:T(8,128)(2,1)}, bf16[320,336]{1,0:T(8,128)(2,1)}, bf16[4,320,32...) custom-call(bf16[416,128]{1,0:T(8,128)(2,1)} %pad.4.own), custom_call_target="tpu_custom_call" | custom-call | tf_op jit(solution)/shard_map/gather_weights/pallas_call | solution.py:791
  38.6 35.6 %attention_forward.1 = (bf16[2,336,2304]{2,1,0:T(8,128)(2,1)}, bf16[2,4,576,320]{3,2,1,0:T(8,128)(2,1)}, f32[2,576,320]{2,1,0:T(8,128)}, bf16[2,576,384]{2,1,0:T...) custom-call(s32[2]{0:T(128)} %sides.3, ...), custom_call_target="tpu_custom_call" | custom-call | tf_op jit(solution)/shard_map/attention_forward/pallas_call | solution.py:219
  74.2 76.1 %feed_forward.1 = (bf16[2,320,2304]{2,1,0:T(8,128)(2,1)}, f32[2,320,2304]{2,1,0:T(8,128)}, f32[336,1280]{1,0:T(8,128)}, f32[320,1280]{1,0:T(8,128)}, f32[80,1280]{1,0:T(8,128)}, /*index=5*/f32[320,128]{1,0:T(8,128)}) custom-call(bf16[2,336,2304]{2,1,0:T(8,128)(2,1)} %get-tuple-element.49.post_next.post, bf16[2,320,2304]{2,1,0:T(8,128)(2,1)} %bitcast.13, ...), custom_call_target="tpu_custom_call" | custom-call | tf_op jit(solution)/shard_map/feed_forward/pallas_call | solution.py:465
  150.4 78.0 %attention_backward.1 = (f32[2,320,2304]{2,1,0:T(8,128)}, f32[336,320]{1,0:T(8,128)}, f32[336,320]{1,0:T(8,128)}, f32[640,384]{1,0:T(8,128)}, f32[4,320,320]{2,1...) custom-call(s32[2]{0:T(128)} %sides.3, bf16[2,336,2304]{2,1,0:T(8,128)(2,1)} %get-tuple-element.55.mixed_far, ...), custom_call_target="tpu_custom_call" | custom-call | tf_op jit(solution)/shard_map/attention_backward/pallas_call | solution.py:633
  228.4 0.0 copy-start
  228.4 0.0 copy-start.1
  228.4 0.0 copy-start.2
  228.4 35.8 %reduce_gradients.1 = (f32[416,128]{1,0:T(8,128)}, f32[8,128]{1,0:T(8,128)}) custom-call(f32[336,1280]{1,0:T(8,128)} %get-tuple-element.66.refs_0_, f32[320,1280]{1,0:T(8,128)} %get-tuple-element.67.refs_1_, f32[80,1280]{1,0:T(8,128)} %get-tuple-element.68.refs_2_, f32[320,128]{1,0:T(8,128)} %get-tuple-element.69.refs_3_, ...), custom_call_target="tpu_custom_call" | custom-call | tf_op jit(solution)/shard_map/reduce_gradients/pallas_call | solution.py:928
  264.2 1.3 reduce_sum.9
  266.3 0.0 copy-done
  266.3 0.0 copy-done.1
  266.3 0.0 copy-done.2
  266.3 1.9 multiply_subtract_fusion
  (1 shorter events, 0.0 us)
Async XLA Ops:
  228.4 37.9 %copy-start = (f32[51840]{0:T(1024)S(1)}, f32[51840]{0:T(1024)}, u32[]{:S(2)}) copy-start(f32[51840]{0:T(1024)} %param.10) | copy-start | bytes 622084
  228.4 37.9 %copy-start.1 = (f32[51840]{0:T(1024)S(1)}, f32[51840]{0:T(1024)}, u32[]{:S(2)}) copy-start(f32[51840]{0:T(1024)} %param.12) | copy-start | bytes 622084
  228.4 37.9 %copy-start.2 = (f32[51840]{0:T(1024)S(1)}, f32[51840]{0:T(1024)}, u32[]{:S(2)}) copy-start(f32[51840]{0:T(1024)} %param.11) | copy-start | bytes 622084

commit v8 on v7

--- a/solution.py
+++ b/solution.py
@@ -626,7 +626,6 @@
         shape((4, width, 128), F32),
         shape((24, width), F32),
     ]
-    one = {"pipeline_mode": pl.Buffered(1)}
     far = (mixed, pre, memory, reduced, patches, images)
     inputs = (cot, mask, lse, middle, grad_post)
     weights = (perm, vec, rows, wq, wqt, wr, wk, wv, wvt, wo)
@@ -636,7 +635,7 @@
             num_scalar_prefetch=1,
             grid=(n,),
             in_specs=[FAR] * 6 + [per_image(x) for x in inputs] + [whole(x) for x in weights],
-            out_specs=[per_image(outs[0], **one)] + [whole(x) for x in outs[1:]],
+            out_specs=[per_image(outs[0])] + [whole(x) for x in outs[1:]],
             scratch_shapes=[
                 pltpu.VMEM((width, tokens), BF),
                 pltpu.VMEM((width, tokens), BF),
@@ -711,15 +710,19 @@
             copy.wait_send()
 
 
-def gather_kernel(slot_rows, bases, own, *refs):
-    outs, (slots, wide, line, own_sem, send_sem, recv_sem, z_sem) = refs[:13], refs[13:]
+def gather_kernel(slot_rows, bases, params, *refs):
+    outs, (own, slots, wide, line, own_sem, send_sem, recv_sem, z_sem) = refs[:13], refs[13:]
     me = Place()
+    me.call([me.beside_core, me.beside_x, me.beside_y] + [me.at_z(z) for z in me.others])
     half = own.shape[0] // 2
+    full = slot_rows // 16 * 16
+    own[...] = jnp.zeros_like(own)
+    own[0:full, :] = params[0:full, :].astype(BF)
+    own[full:slot_rows, :] = params[full:slot_rows, :].astype(BF)
     first, second = pl.ds(0, half), pl.ds(half, half)
     send = Sender(send_sem, recv_sem)
     copy = pltpu.make_async_copy(own, slots.at[me.core, me.dp, me.z], own_sem)
     copy.start()
-    me.call([me.beside_core, me.beside_x, me.beside_y] + [me.at_z(z) for z in me.others])
     me.answer(6)
     own_slot = slots.at[me.core, me.dp, me.z]
 
@@ -784,7 +787,8 @@
     write_weights(bases, wide, *outs)
 
 
-def gather_weights(own, slot_rows, width):
+def gather_weights(params, rows, width):
+    slot_rows = params.shape[0]
     bases, count = row_bases(width, 4 * width)
     outs = weight_shapes(width)
     copies = 35
@@ -794,9 +798,10 @@
         in_specs=[pl.BlockSpec(memory_space=pltpu.VMEM)],
         out_specs=[pl.BlockSpec(memory_space=pltpu.VMEM)] * len(outs),
         scratch_shapes=[
-            pltpu.VMEM((2, 4, 4) + own.shape, BF),
+            pltpu.VMEM((rows, 128), BF),
+            pltpu.VMEM((2, 4, 4, rows, 128), BF),
             pltpu.VMEM((3, -(-32 * slot_rows * 128 // width // 8) * 8 + 8, 128), F32),
-            pltpu.VMEM(own.shape, F32),
+            pltpu.VMEM((rows, 128), F32),
             pltpu.SemaphoreType.DMA(()),
             pltpu.SemaphoreType.DMA((copies,)),
             pltpu.SemaphoreType.DMA((copies,)),
@@ -806,13 +811,13 @@
             collective_id=0, has_side_effects=True, vmem_limit_bytes=VMEM_BYTES
         ),
         name="gather_weights",
-    )(own)
+    )(params)
     return dict(zip(outs, values, strict=True))
 
 
 def reduce_kernel(slot_rows, bases, *refs):
-    grads, (shard, squares) = refs[:10], refs[10:12]
-    wide, line, own, core_out, core_in, y_in, x_in, x_last, y_last, z_in, small, send_sem, recv_sem = refs[12:]
+    grads_far, (shard, squares), grads, fetch_sem = refs[:10], refs[10:12], refs[12:22], refs[22]
+    wide, line, own, core_out, core_in, y_in, x_in, x_last, y_last, z_in, small, send_sem, recv_sem = refs[23:]
     me = Place()
     rows = shard.shape[0]
     half = rows // 2
@@ -821,7 +826,10 @@
     peers = [(me.dp, (me.z + k) % 4 * 2 + core) for k in range(4) for core in (me.core, me.other_core)][1:]
     planes = [me.beside_x, me.beside_y, me.across]
     me.call(peers + planes)
-    collect_gradients(bases, wide, *grads)
+    fetch = [pltpu.make_async_copy(x, y, fetch_sem.at[k]) for k, (x, y) in enumerate(zip(grads_far, grads))]
+    for k in COLLECTED:
+        fetch[k].start()
+    collect_gradients(bases, wide, *grads, ready=lambda k: fetch[k].wait())
     line[...] = jnp.zeros_like(line)
     me.answer(len(peers + planes))
     units = [(me.z + k) % 4 for k in (2, 1, 3, 0)]
@@ -917,7 +925,7 @@
     copies = [send(small.at[1], small.at[10 + me.dp], device) for device in planes]
     for copied in copies:
         copied.wait_recv()
-    squares[...] = ((small[10] + small[11]) + small[12]) + small[13]
+    squares[0, 0] = jnp.sum(((small[10] + small[11]) + small[12]) + small[13])
     send.finish()
 
 
@@ -927,10 +935,12 @@
     count = 4 + 16 + 8 + 3 + 7 + 3
     return pl.pallas_call(
         partial(reduce_kernel, slot_rows, bases),
-        out_shape=[jax.ShapeDtypeStruct((rows, 128), F32), jax.ShapeDtypeStruct((8, 128), F32)],
-        in_specs=[pl.BlockSpec(memory_space=pltpu.VMEM)] * len(grads),
-        out_specs=[pl.BlockSpec(memory_space=pltpu.VMEM)] * 2,
+        out_shape=[jax.ShapeDtypeStruct((rows, 128), F32), jax.ShapeDtypeStruct((1, 1), F32)],
+        in_specs=[FAR] * len(grads),
+        out_specs=[pl.BlockSpec(memory_space=pltpu.VMEM), pl.BlockSpec(memory_space=pltpu.SMEM)],
         scratch_shapes=[
+            *[pltpu.VMEM(x.shape, x.dtype) for x in grads],
+            pltpu.SemaphoreType.DMA((len(grads),)),
             pltpu.VMEM((3, -(-32 * slot_rows * 128 // width // 8) * 8 + 8, 128), F32),
             pltpu.VMEM((rows, 128), F32),
             pltpu.VMEM((4, 4, rows, 128), F32),
@@ -1114,7 +1124,10 @@
     return dict(zip(outs, values, strict=True))
 
 
-def collect_gradients(bases, wide, gwe, gwst, gtaps, gbias, gwo, gwq, gpair, gwr, gcols, grows):
+COLLECTED = (8, 3, 9, 5, 7, 6, 4, 2, 0, 1)
+
+
+def collect_gradients(bases, wide, gwe, gwst, gtaps, gbias, gwo, gwq, gpair, gwr, gcols, grows, ready=lambda k: None):
     width = gwst.shape[0]
     hidden = gwst.shape[1]
     used = bases["shrink_bias"] + 1
@@ -1128,25 +1141,35 @@
         wide[1, at, :] = value[:, 128:256]
         wide[2, at, 0 : width - 256] = value[:, 256:width]
 
+    ready(8)
     for k, name in enumerate(("pre_gain", "pre_shift", "mlp_gain", "mlp_shift")):
         put(bases[name], jnp.sum(gcols[k].T, axis=0, keepdims=True))
+    ready(3)
     put(bases["shrink_bias"], jnp.sum(gbias[...].T, axis=0, keepdims=True))
+    ready(9)
     for k, name in enumerate(("reduce_bias", "reduce_gain", "reduce_shift")):
         put(bases[name], jnp.sum(grows[8 * k : 8 * k + 8, :], axis=0, keepdims=True))
+    ready(5)
     put(bases["query_weight"], gwq[0 : width + 1, :])
+    ready(7)
     for p in range(4):
         put(bases["reduce_weight"] + p * width, gwr[p].T)
+    ready(6)
     put(bases["pair_weight"], gpair[0:width, :].T[0:width], 2)
     value = gpair[width : 2 * width, :].T
     put(bases["pair_weight"] + 1, value[0:width], 2)
     put(bases["value_bias"], value[width : width + 1])
+    ready(4)
     put(bases["output_weight"], gwo[0 : width + 1, :])
+    ready(2)
     sums = jnp.concatenate(
         [jnp.sum(gtaps[8 * k : 8 * k + 8, :], axis=0, keepdims=True) for k in range(10)], axis=0
     )
+    ready(0)
     for q in range(hidden // width):
         put(bases["expand_weight"] + q, gwe[0 : width + 1, q * width : (q + 1) * width], hidden // width)
         put(bases["spatial_weight"] + q, sums[:, q * width : (q + 1) * width], hidden // width)
+    ready(1)
     for k in range(hidden // 128):
         put(bases["shrink_weight"] + 128 * k, gwst[:, 128 * k : 128 * k + 128].T)
 
@@ -1219,7 +1242,7 @@
     positions = jnp.arange(TOKENS, dtype=jnp.int32)
     limit = 2 * kv_sides[:, None]
     mask = ((positions[None] // GRID < limit) & (positions[None] % GRID < limit)).astype(F32)
-    mask = jnp.broadcast_to(mask[:, None, :], (mask.shape[0], 8, TOKENS))
+    mask = mask[:, None, :]
     perm = jnp.asarray(patch_order(), BF)
     pre, patches, reduced, memory, mixed, lse, middle, post = attention_forward(
         kv_sides, images, mask, perm, w["vec"], w["rows"], w["wqt"], w["wr"], w["wk"], w["wvt"], w["wot"]
@@ -1240,18 +1263,18 @@
     outer, inner = lax.axis_size("dp"), lax.axis_size("fsdp")
     slot_rows = params.shape[0] // 128
     padded_rows = -(-slot_rows // 32) * 32
-    own = jnp.pad(params.reshape(slot_rows, 128).astype(BF), ((0, padded_rows - slot_rows), (0, 0)))
     order = list(range(outer * inner))
     if on_grid:
-        weights = gather_weights(own, slot_rows, width)
+        weights = gather_weights(params.reshape(slot_rows, 128), padded_rows, width)
     else:
+        own = jnp.pad(params.reshape(slot_rows, 128).astype(BF), ((0, padded_rows - slot_rows), (0, 0)))
         weights = unpack_weights(lax.all_gather(own, axes), order, slot_rows, width)
     output, grad_images, grads = device_step(
         images.transpose(0, 2, 1), cotangent.transpose(0, 2, 1), kv_sides, weights
     )
     if on_grid:
         shard, squares = reduce_gradients(grads, slot_rows, padded_rows, width)
-        squares = jnp.sum(squares)
+        squares = squares[0, 0]
     else:
         slots = pack_gradients(grads, order, slot_rows, padded_rows, width)
         shard = lax.psum_scatter(slots.astype(F32), axes)

time: 273 us -> 268 us (0.982)
  no operation moved by 1% of the time
where the time goes in v8:
time: 268 us; the launch traced here: 265 us
  Pallas kernels  259 us (97%)
  other arithmetic  3.21 us (1%)
  between operations  2.74 us (1%)
    pallas_call x1, Pallas kernels, feed_forward(): pl.pallas_call(feed_forward_kernel, grid=(count + 1,), in_specs=[image(x,...  77 us
    pallas_call x1, Pallas kernels, attention_backward(): pl.pallas_call(attention_backward_kernel, grid_spec=pltpu.PrefetchScalarG...  76.4 us
    pallas_call x1, Pallas kernels, attention_forward(): pl.pallas_call(attention_forward_kernel, grid_spec=pltpu.PrefetchScalarGr...  35.6 us
    pallas_call x1, Pallas kernels, gather_weights(): pl.pallas_call(partial(gather_kernel, slot_rows, bases), out_shape=list(o...  34.9 us
    pallas_call x1, Pallas kernels, reduce_gradients(): pl.pallas_call(partial(reduce_kernel, slot_rows, bases), out_shape=[jax.S...  34.8 us

profile of v8, /device:TPU:0, one launch (start us, length us, event | category | flops | bytes accessed | tf_op | source)
XLA Modules:
  0.0 264.6 jit_solution(3067333004341871188)
XLA Ops:
  0.6 0.7 broadcast_multiply_fusion
  1.3 0.7 and_convert_fusion.mask.mask_next
  2.0 34.9 %gather_weights.1 = (f32[5,320,128]{2,1,0:T(8,128)}, f32[3,320]{1,0:T(4,128)}, bf16[320,320]{1,0:T(8,128)(2,1)}, bf16[320,336]{1,0:T(8,128)(2,1)}, bf16[4,320,32...) custom-call(f32[405,128]{1,0:T(8,128)} %bitcast.18), custom_call_target="tpu_custom_call" | custom-call | tf_op jit(solution)/shard_map/gather_weights/pallas_call | solution.py:795
  36.8 35.6 %attention_forward.1 = (bf16[2,336,2304]{2,1,0:T(8,128)(2,1)}, bf16[2,4,576,320]{3,2,1,0:T(8,128)(2,1)}, f32[2,576,320]{2,1,0:T(8,128)}, bf16[2,576,384]{2,1,0:T...) custom-call(s32[2]{0:T(128)} %sides.3, ...), custom_call_target="tpu_custom_call" | custom-call | tf_op jit(solution)/shard_map/attention_forward/pallas_call | solution.py:219
  72.4 77.0 %feed_forward.1 = (bf16[2,320,2304]{2,1,0:T(8,128)(2,1)}, f32[2,320,2304]{2,1,0:T(8,128)}, f32[336,1280]{1,0:T(8,128)}, f32[320,1280]{1,0:T(8,128)}, f32[80,1280]{1,0:T(8,128)}, /*index=5*/f32[320,128]{1,0:T(8,128)}) custom-call(bf16[2,336,2304]{2,1,0:T(8,128)(2,1)} %get-tuple-element.49.post_next.post, bf16[2,320,2304]{2,1,0:T(8,128)(2,1)} %bitcast.13, ...), custom_call_target="tpu_custom_call" | custom-call | tf_op jit(solution)/shard_map/feed_forward/pallas_call | solution.py:465
  149.4 76.4 %attention_backward.1 = (f32[2,320,2304]{2,1,0:T(8,128)}, f32[336,320]{1,0:T(8,128)}, f32[336,320]{1,0:T(8,128)}, f32[640,384]{1,0:T(8,128)}, f32[4,320,320]{2,1...) custom-call(s32[2]{0:T(128)} %sides.3, bf16[2,336,2304]{2,1,0:T(8,128)(2,1)} %get-tuple-element.55.mixed_far, ...), custom_call_target="tpu_custom_call" | custom-call | tf_op jit(solution)/shard_map/attention_backward/pallas_call | solution.py:632
  225.8 0.0 copy-start
  225.8 0.0 copy-start.1
  225.8 0.0 copy-start.2
  225.8 34.8 %reduce_gradients.1 = (f32[416,128]{1,0:T(8,128)}, f32[1,1]{1,0:T(1,128)}) custom-call(f32[336,1280]{1,0:T(8,128)} %get-tuple-element.66.refs_0_, f32[320,1280]{1,0:T(8,128)} %get-tuple-element.67.refs_1_, f32[80,1280]{1,0:T(8,128)} %get-tuple-element.68.refs_2_, f32[320,128]{1,0:T(8,128)} %get-tuple-element.69.refs_3_, ...), custom_call_target="tpu_custom_call" | custom-call | tf_op jit(solution)/shard_map/reduce_gradients/pallas_call | solution.py:936
  261.4 0.0 copy-done
  261.4 0.0 copy-done.1
  261.4 0.0 copy-done.2
  261.4 1.9 multiply_subtract_fusion
  (1 shorter events, 0.0 us)
Async XLA Ops:
  225.8 35.6 %copy-start = (f32[51840]{0:T(1024)S(1)}, f32[51840]{0:T(1024)}, u32[]{:S(2)}) copy-start(f32[51840]{0:T(1024)} %param.10) | copy-start | bytes 622084
  225.8 35.6 %copy-start.1 = (f32[51840]{0:T(1024)S(1)}, f32[51840]{0:T(1024)}, u32[]{:S(2)}) copy-start(f32[51840]{0:T(1024)} %param.12) | copy-start | bytes 622084
  225.8 35.6 %copy-start.2 = (f32[51840]{0:T(1024)S(1)}, f32[51840]{0:T(1024)}, u32[]{:S(2)}) copy-start(f32[51840]{0:T(1024)} %param.11) | copy-start | bytes 622084

commit v9 on v8

--- a/solution.py
+++ b/solution.py
@@ -268,10 +268,13 @@
 
     def finish(t, act, grad_exp):
         at = tokens(t)
+        gwst[:, js_done] += mm(out_grad[:, at], act[at, :])
+        gwe[:, js_done] += mm(post[0, :, at], grad_exp[at, :])
+
+    def finish_rest(t, act, grad_exp):
+        at = tokens(t)
         total[:, at] += mm(wst[0:width, :], act[at, :], NT)
         grad_post[0, :, at] += mm(we[0:width, :], grad_exp[at, :], NT)
-        gwst[:, js_done] += mm(out_grad[:, at], act[at, :])
-        gwe[:, js_done] += mm(post[0, :, at], grad_exp[at, :])
 
     def convolve(t, padded, act):
         for h in range(halves):
@@ -389,6 +392,7 @@
 
         def backward(t, _):
             expand(t, padded_next, we_next, wst_next)
+            finish_rest(t, act_done, grad_exp_done)
             convolve_back(t, padded, grad_exp)
             return 0
 
@@ -409,10 +413,12 @@
             @pl.when(lax.rem(s, 2) == 0)
             def _():
                 finish(t, act_1, grad_exp_1)
+                finish_rest(t, act_1, grad_exp_1)
 
             @pl.when(lax.rem(s, 2) == 1)
             def _():
                 finish(t, act_0, grad_exp_0)
+                finish_rest(t, act_0, grad_exp_0)
 
             return 0
 

time: 268 us -> 266 us (level)
  no operation moved by 1% of the time
where the time goes in v9:
time: 266 us; the launch traced here: 262 us
  Pallas kernels  257 us (97%)
  other arithmetic  3.21 us (1%)
  between operations  2.74 us (1%)
    pallas_call x1, Pallas kernels, attention_backward(): pl.pallas_call(attention_backward_kernel, grid_spec=pltpu.PrefetchScalarG...  76.4 us
    pallas_call x1, Pallas kernels, feed_forward(): pl.pallas_call(feed_forward_kernel, grid=(count + 1,), in_specs=[image(x,...  74.9 us
    pallas_call x1, Pallas kernels, attention_forward(): pl.pallas_call(attention_forward_kernel, grid_spec=pltpu.PrefetchScalarGr...  35.6 us
    pallas_call x1, Pallas kernels, gather_weights(): pl.pallas_call(partial(gather_kernel, slot_rows, bases), out_shape=list(o...  34.9 us
    pallas_call x1, Pallas kernels, reduce_gradients(): pl.pallas_call(partial(reduce_kernel, slot_rows, bases), out_shape=[jax.S...  34.8 us

profile of v9, /device:TPU:0, one launch (start us, length us, event | category | flops | bytes accessed | tf_op | source)
XLA Modules:
  0.0 262.5 jit_solution(13816333948013211624)
XLA Ops:
  0.6 0.7 broadcast_multiply_fusion
  1.3 0.7 and_convert_fusion.mask.mask_next
  2.0 34.9 %gather_weights.1 = (f32[5,320,128]{2,1,0:T(8,128)}, f32[3,320]{1,0:T(4,128)}, bf16[320,320]{1,0:T(8,128)(2,1)}, bf16[320,336]{1,0:T(8,128)(2,1)}, bf16[4,320,32...) custom-call(f32[405,128]{1,0:T(8,128)} %bitcast.18), custom_call_target="tpu_custom_call" | custom-call | tf_op jit(solution)/shard_map/gather_weights/pallas_call | solution.py:801
  36.8 35.6 %attention_forward.1 = (bf16[2,336,2304]{2,1,0:T(8,128)(2,1)}, bf16[2,4,576,320]{3,2,1,0:T(8,128)(2,1)}, f32[2,576,320]{2,1,0:T(8,128)}, bf16[2,576,384]{2,1,0:T...) custom-call(s32[2]{0:T(128)} %sides.3, ...), custom_call_target="tpu_custom_call" | custom-call | tf_op jit(solution)/shard_map/attention_forward/pallas_call | solution.py:219
  72.4 74.9 %feed_forward.1 = (bf16[2,320,2304]{2,1,0:T(8,128)(2,1)}, f32[2,320,2304]{2,1,0:T(8,128)}, f32[336,1280]{1,0:T(8,128)}, f32[320,1280]{1,0:T(8,128)}, f32[80,1280]{1,0:T(8,128)}, /*index=5*/f32[320,128]{1,0:T(8,128)}) custom-call(bf16[2,336,2304]{2,1,0:T(8,128)(2,1)} %get-tuple-element.49.post_next.post, bf16[2,320,2304]{2,1,0:T(8,128)(2,1)} %bitcast.13, ...), custom_call_target="tpu_custom_call" | custom-call | tf_op jit(solution)/shard_map/feed_forward/pallas_call | solution.py:471
  147.4 76.4 %attention_backward.1 = (f32[2,320,2304]{2,1,0:T(8,128)}, f32[336,320]{1,0:T(8,128)}, f32[336,320]{1,0:T(8,128)}, f32[640,384]{1,0:T(8,128)}, f32[4,320,320]{2,1...) custom-call(s32[2]{0:T(128)} %sides.3, bf16[2,336,2304]{2,1,0:T(8,128)(2,1)} %get-tuple-element.55.mixed_far, ...), custom_call_target="tpu_custom_call" | custom-call | tf_op jit(solution)/shard_map/attention_backward/pallas_call | solution.py:638
  223.7 0.0 copy-start
  223.7 0.0 copy-start.1
  223.7 0.0 copy-start.2
  223.8 34.8 %reduce_gradients.1 = (f32[416,128]{1,0:T(8,128)}, f32[1,1]{1,0:T(1,128)}) custom-call(f32[336,1280]{1,0:T(8,128)} %get-tuple-element.66.refs_0_, f32[320,1280]{1,0:T(8,128)} %get-tuple-element.67.refs_1_, f32[80,1280]{1,0:T(8,128)} %get-tuple-element.68.refs_2_, f32[320,128]{1,0:T(8,128)} %get-tuple-element.69.refs_3_, ...), custom_call_target="tpu_custom_call" | custom-call | tf_op jit(solution)/shard_map/reduce_gradients/pallas_call | solution.py:942
  259.3 0.0 copy-done
  259.3 0.0 copy-done.1
  259.3 0.0 copy-done.2
  259.3 1.9 multiply_subtract_fusion
  (1 shorter events, 0.0 us)
Async XLA Ops:
  223.7 35.6 %copy-start = (f32[51840]{0:T(1024)S(1)}, f32[51840]{0:T(1024)}, u32[]{:S(2)}) copy-start(f32[51840]{0:T(1024)} %param.10) | copy-start | bytes 622084
  223.7 35.6 %copy-start.1 = (f32[51840]{0:T(1024)S(1)}, f32[51840]{0:T(1024)}, u32[]{:S(2)}) copy-start(f32[51840]{0:T(1024)} %param.12) | copy-start | bytes 622084
  223.7 35.6 %copy-start.2 = (f32[51840]{0:T(1024)S(1)}, f32[51840]{0:T(1024)}, u32[]{:S(2)}) copy-start(f32[51840]{0:T(1024)} %param.11) | copy-start | bytes 622084

commit v10 on v9

--- a/solution.py
+++ b/solution.py
@@ -806,8 +806,8 @@
         scratch_shapes=[
             pltpu.VMEM((rows, 128), BF),
             pltpu.VMEM((2, 4, 4, rows, 128), BF),
-            pltpu.VMEM((3, -(-32 * slot_rows * 128 // width // 8) * 8 + 8, 128), F32),
-            pltpu.VMEM((rows, 128), F32),
+            pltpu.VMEM((3, -(-32 * slot_rows * 128 // width // 8) * 8 + 24, 128), F32),
+            pltpu.VMEM((rows + 48, 128), F32),
             pltpu.SemaphoreType.DMA(()),
             pltpu.SemaphoreType.DMA((copies,)),
             pltpu.SemaphoreType.DMA((copies,)),
@@ -846,11 +846,11 @@
         z = units[k]
         for dp in range(4):
             join_slot(wide, dp * 8 + z * 2 + me.other_core, slot_rows, line)
-            core_out[z, dp] = line[...].astype(BF)
+            core_out[z, dp] = line[0:rows, :].astype(BF)
         core_copies.append(send(core_out.at[z], core_in.at[z], me.beside_core))
         for dp in range(4):
             join_slot(wide, dp * 8 + z * 2 + me.core, slot_rows, line)
-            own[z, dp] = line[...]
+            own[z, dp] = line[0:rows, :]
 
     def cores(k):
         z = units[k]
@@ -947,8 +947,8 @@
         scratch_shapes=[
             *[pltpu.VMEM(x.shape, x.dtype) for x in grads],
             pltpu.SemaphoreType.DMA((len(grads),)),
-            pltpu.VMEM((3, -(-32 * slot_rows * 128 // width // 8) * 8 + 8, 128), F32),
-            pltpu.VMEM((rows, 128), F32),
+            pltpu.VMEM((3, -(-32 * slot_rows * 128 // width // 8) * 8 + 24, 128), F32),
+            pltpu.VMEM((rows + 48, 128), F32),
             pltpu.VMEM((4, 4, rows, 128), F32),
             pltpu.VMEM((4, 4, rows, 128), BF),
             pltpu.VMEM((4, 4, rows, 128), BF),
@@ -1017,7 +1017,7 @@
 
 def spread_slot(values, slot, slot_rows, line, wide):
     pairs = slot_rows // 5
-    line[...] = values.astype(F32)
+    line[0 : values.shape[0], :] = values.astype(F32)
 
     def part(start, count):
         low = lax.broadcasted_iota(jnp.int32, (count, 128), 1) < 64

time: 266 us -> 266 us (level)
  no operation moved by 1% of the time
where the time goes in v10:
time: 266 us; the launch traced here: 263 us
  Pallas kernels  257 us (97%)
  other arithmetic  3.21 us (1%)
  between operations  2.74 us (1%)
    pallas_call x1, Pallas kernels, attention_backward(): pl.pallas_call(attention_backward_kernel, grid_spec=pltpu.PrefetchScalarG...  76.4 us
    pallas_call x1, Pallas kernels, feed_forward(): pl.pallas_call(feed_forward_kernel, grid=(count + 1,), in_specs=[image(x,...  74.9 us
    pallas_call x1, Pallas kernels, attention_forward(): pl.pallas_call(attention_forward_kernel, grid_spec=pltpu.PrefetchScalarGr...  35.6 us
    pallas_call x1, Pallas kernels, gather_weights(): pl.pallas_call(partial(gather_kernel, slot_rows, bases), out_shape=list(o...  34.9 us
    pallas_call x1, Pallas kernels, reduce_gradients(): pl.pallas_call(partial(reduce_kernel, slot_rows, bases), out_shape=[jax.S...  34.8 us

profile of v10, /device:TPU:0, one launch (start us, length us, event | category | flops | bytes accessed | tf_op | source)
XLA Modules:
  0.0 262.5 jit_solution(9604383383228010988)
XLA Ops:
  0.6 0.7 broadcast_multiply_fusion
  1.3 0.7 and_convert_fusion.mask.mask_next
  2.0 34.9 %gather_weights.1 = (f32[5,320,128]{2,1,0:T(8,128)}, f32[3,320]{1,0:T(4,128)}, bf16[320,320]{1,0:T(8,128)(2,1)}, bf16[320,336]{1,0:T(8,128)(2,1)}, bf16[4,320,32...) custom-call(f32[405,128]{1,0:T(8,128)} %bitcast.18), custom_call_target="tpu_custom_call" | custom-call | tf_op jit(solution)/shard_map/gather_weights/pallas_call | solution.py:801
  36.9 35.6 %attention_forward.1 = (bf16[2,336,2304]{2,1,0:T(8,128)(2,1)}, bf16[2,4,576,320]{3,2,1,0:T(8,128)(2,1)}, f32[2,576,320]{2,1,0:T(8,128)}, bf16[2,576,384]{2,1,0:T...) custom-call(s32[2]{0:T(128)} %sides.3, ...), custom_call_target="tpu_custom_call" | custom-call | tf_op jit(solution)/shard_map/attention_forward/pallas_call | solution.py:219
  72.4 74.9 %feed_forward.1 = (bf16[2,320,2304]{2,1,0:T(8,128)(2,1)}, f32[2,320,2304]{2,1,0:T(8,128)}, f32[336,1280]{1,0:T(8,128)}, f32[320,1280]{1,0:T(8,128)}, f32[80,1280]{1,0:T(8,128)}, /*index=5*/f32[320,128]{1,0:T(8,128)}) custom-call(bf16[2,336,2304]{2,1,0:T(8,128)(2,1)} %get-tuple-element.49.post_next.post, bf16[2,320,2304]{2,1,0:T(8,128)(2,1)} %bitcast.13, ...), custom_call_target="tpu_custom_call" | custom-call | tf_op jit(solution)/shard_map/feed_forward/pallas_call | solution.py:471
  147.4 76.4 %attention_backward.1 = (f32[2,320,2304]{2,1,0:T(8,128)}, f32[336,320]{1,0:T(8,128)}, f32[336,320]{1,0:T(8,128)}, f32[640,384]{1,0:T(8,128)}, f32[4,320,320]{2,1...) custom-call(s32[2]{0:T(128)} %sides.3, bf16[2,336,2304]{2,1,0:T(8,128)(2,1)} %get-tuple-element.55.mixed_far, ...), custom_call_target="tpu_custom_call" | custom-call | tf_op jit(solution)/shard_map/attention_backward/pallas_call | solution.py:638
  223.7 0.0 copy-start
  223.7 0.0 copy-start.1
  223.7 0.0 copy-start.2
  223.8 34.8 %reduce_gradients.1 = (f32[416,128]{1,0:T(8,128)}, f32[1,1]{1,0:T(1,128)}) custom-call(f32[336,1280]{1,0:T(8,128)} %get-tuple-element.66.refs_0_, f32[320,1280]{1,0:T(8,128)} %get-tuple-element.67.refs_1_, f32[80,1280]{1,0:T(8,128)} %get-tuple-element.68.refs_2_, f32[320,128]{1,0:T(8,128)} %get-tuple-element.69.refs_3_, ...), custom_call_target="tpu_custom_call" | custom-call | tf_op jit(solution)/shard_map/reduce_gradients/pallas_call | solution.py:942
  259.3 0.0 copy-done
  259.3 0.0 copy-done.1
  259.3 0.0 copy-done.2
  259.3 1.9 multiply_subtract_fusion
  (1 shorter events, 0.0 us)
Async XLA Ops:
  223.7 35.6 %copy-start = (f32[51840]{0:T(1024)S(1)}, f32[51840]{0:T(1024)}, u32[]{:S(2)}) copy-start(f32[51840]{0:T(1024)} %param.10) | copy-start | bytes 622084
  223.7 35.6 %copy-start.1 = (f32[51840]{0:T(1024)S(1)}, f32[51840]{0:T(1024)}, u32[]{:S(2)}) copy-start(f32[51840]{0:T(1024)} %param.12) | copy-start | bytes 622084
  223.7 35.6 %copy-start.2 = (f32[51840]{0:T(1024)S(1)}, f32[51840]{0:T(1024)}, u32[]{:S(2)}) copy-start(f32[51840]{0:T(1024)} %param.11) | copy-start | bytes 622084
